TPU v7x, 32 devices: a whole 2x2x4 slice. The times are simulated.
32 devices in a mesh: row: 8 (over z, x), col: 4 (over y, core).
Axes of the slice: x: 2, y: 2, z: 4, core: 2. Of those that a mesh axis runs over, the one named last changes fastest.
Arguments:
- grad_out: bfloat16 [1536, 4096], P('row', 'col'), may hold values from -6 to 6
- w_down: bfloat16 [16384, 4096], P('row', 'col'), may hold values from -0.046875 to 0.046875
- pre_act: bfloat16 [1536, 16384], P('col', 'row'), may hold values from -6 to 6
- acc_down: float32 [16384, 4096], P('row', 'col'), may hold values from -4 to 4
Outputs:
- acc_new: float32 [16384, 4096], P('row', 'col')
- grad_pre: bfloat16 [1536, 16384], P('col', 'row')
All inputs are finite; a program needn't handle non-finite values.
Results may differ from a plain program's by a relative error of at most 0.0023.
Values may be sent and summed in bfloat16 or wider, within the bound.
A program may use at most 128 MiB of HBM per device.

v0:
```python
import math

import jax
import jax.numpy as jnp
from jax import lax
from jax.sharding import PartitionSpec as P


def gelu_value(v):
    return 0.5 * v * (1.0 + lax.erf(v / math.sqrt(2.0)))


def gelu_slope(v):
    return 0.5 * (1.0 + lax.erf(v / math.sqrt(2.0))) + v * jnp.exp(-0.5 * v * v) / math.sqrt(
        2.0 * math.pi
    )


def on_device(grad_out, w_down, pre_act, acc_down):
    total = grad_out.shape[0] * lax.axis_size("row")
    pre_float = pre_act.astype(jnp.float32)
    pre_full = lax.all_gather(pre_act, "col", axis=0, tiled=True)
    act_full = gelu_value(pre_full.astype(jnp.float32)).astype(jnp.bfloat16)
    piece = lax.all_gather(grad_out, "row", axis=0, tiled=True)
    block = lax.dot_general(
        piece, w_down, (((1,), (1,)), ((), ())), preferred_element_type=jnp.float32
    )
    partial_act = block
    grad_w = lax.dot_general(
        act_full, piece, (((0,), (0,)), ((), ())), preferred_element_type=jnp.float32
    )
    partial_act, grad_w = (partial_act, grad_w)
    summed = lax.psum_scatter(partial_act, "col", scatter_dimension=0, tiled=True)
    grad_pre = (summed * gelu_slope(pre_float)).astype(jnp.bfloat16)
    acc_new = acc_down + grad_w * float(total) ** (-0.5)
    return (acc_new, grad_pre)


def solution(mesh):
    return jax.shard_map(
        on_device,
        mesh=mesh,
        in_specs=(P("row", "col"), P("row", "col"), P("col", "row"), P("row", "col")),
        out_specs=(P("row", "col"), P("col", "row")),
        check_vma=False,
    )
```

profile of v0, /device:TPU:0, one launch (start us, length us, event | category | flops | bytes accessed | tf_op | source)
XLA Modules:
  0.0 231.9 jit_solution(14301734795565825514)
XLA Ops:
  7.2 0.0 all-gather.5.cloned.1.call-start
  7.2 0.7 all-gather.5.cloned.1.call-update
  7.9 0.0 all-gather.3.cloned.1.call-start
  7.9 0.7 all-gather.3.cloned.1.call-update
  8.6 0.0 reduce-scatter.2.cloned.1.call-start
  8.7 64.7 %all-gather.5.cloned.1.call-done = bf16[1536,1024]{1,0:T(8,128)(2,1)} async-done(((bf16[192,1024]{1,0:T(8,128)(2,1)}), bf16[1536,1024]{1,0:T(8,128)(2,1)}) %all-gather.5.cloned.1.call-update) | async-done | bytes 3145744 | tf_op jit(solution)/shard_map/all_gather | solution.py:24
  73.4 12.3 %fusion.19 = f32[1536,2048]{1,0:T(8,128)} fusion(bf16[1536,1024]{1,0:T(8,128)(2,1)} %all-gather.5.cloned.1.call-done, bf16[2048,1024]{1,0:T(8,128)(2,1)} %param.5), kind=kOutput, calls=%fused_computation.23 | convolution fusion | flops 6442450944 | bytes 19922944 | tf_op jit(solution)/shard_map/dot_general | solution.py:25
  85.7 0.0 reduce-scatter.2.cloned.1.call-update
  85.7 0.0 copy-start
  85.7 34.3 %all-gather.3.cloned.1.call-done = bf16[1536,2048]{1,0:T(8,128)(2,1)} async-done(((bf16[384,2048]{1,0:T(8,128)(2,1)}), bf16[1536,2048]{1,0:T(8,128)(2,1)}) %all-gather.3.cloned.1.call-update) | async-done | bytes 6291472 | tf_op jit(solution)/shard_map/all_gather | solution.py:22
  120.0 13.8 %multiply_add_fusion = f32[2048,1024]{1,0:T(8,128)} fusion(f32[2048,1024]{1,0:T(8,128)} %param.7, bf16[1536,1024]{1,0:T(8,128)(2,1)} %all-gather.5.cloned.1.call-done, bf16[1536,2048]{1,0:T(8,128)(2,1)} %all-gather.3.cloned.1.call-done), kind=kOutput, calls=%fused_computation.6 | convolution fusion | flops 6465519616 | bytes 26214400 | tf_op jit(solution)/shard_map/dot_general | solution.py:29
  133.8 87.9 %reduce-scatter.2.cloned.1.call-done = f32[384,2048]{1,0:T(8,128)} async-done(((f32[1536,2048]{1,0:T(8,128)}), f32[384,2048]{1,0:T(8,128)}) %reduce-scatter.2.cloned.1.call-update) | async-done | bytes 3145744 | tf_op jit(solution)/shard_map/reduce_scatter | solution.py:33
  221.7 0.0 copy-done
  221.7 3.7 %fusion.15 = bf16[384,2048]{1,0:T(8,128)(2,1)} fusion(f32[384,2048]{1,0:T(8,128)} %reduce-scatter.2.cloned.1.call-done, bf16[384,2048]{1,0:T(8,128)(2,1)S(1)} %copy-done), kind=kLoop, calls=%fused_computation.19 | loop fusion | flops 8650752 | bytes 6291456 | tf_op jit(solution)/shard_map/convert_element_type | solution.py:34
Async XLA Ops:
  7.2 66.2 %all-gather.5.cloned.1.call-start = ((), (), s32[]{:S(2)}) async-start(), calls=%async_computation.2 | async-start | bytes 3538944 | tf_op jit(solution)/shard_map/all_gather | solution.py:24
  7.9 112.1 %all-gather.3.cloned.1.call-start = ((), (), s32[]{:S(2)}) async-start(), calls=%async_computation.1 | async-start | bytes 7864320 | tf_op jit(solution)/shard_map/all_gather | solution.py:22
  8.6 213.0 %reduce-scatter.2.cloned.1.call-start = ((), (), s32[]{:S(2)}) async-start(), calls=%async_computation.3 | async-start | bytes 15728640 | tf_op jit(solution)/shard_map/reduce_scatter | solution.py:33
  85.7 136.0 %copy-start = (bf16[384,2048]{1,0:T(8,128)(2,1)S(1)}, bf16[384,2048]{1,0:T(8,128)(2,1)}, u32[]{:S(2)}) copy-start(bf16[384,2048]{1,0:T(8,128)(2,1)} %param.6) | copy-start | bytes 4718596
Sparse Core Ops, SparseCore 0:
  10.2 63.1 all-gather.4
  74.9 44.9 all-gather.2
  122.6 99.0 reduce-scatter.1
where the time goes:
time: 232 us
  waiting for transfers between devices  188 us (81%)
  matrix products  26.1 us (11%)
  between operations  13.8 us (6%)
  other arithmetic  3.68 us (2%)
    reduce_scatter x1, waiting for transfers between devices, on_device(): lax.psum_scatter(partial_act, 'col', scatter_dimension=0, tiled=True)  87.9 us
    all_gather x1, waiting for transfers between devices, on_device(): piece = lax.all_gather(grad_out, 'row', axis=0, tiled=True)  64.7 us
    all_gather x1, waiting for transfers between devices, on_device(): pre_full = lax.all_gather(pre_act, 'col', axis=0, tiled=True)  34.3 us
    dot_general x1, matrix products, on_device(): lax.dot_general(act_full, piece, (((0,), (0,)), ((), ())), preferred_elem...  13.8 us
    dot_general x1, matrix products, on_device(): lax.dot_general(piece, w_down, (((1,), (1,)), ((), ())), preferred_elemen...  12.3 us
  transfers between devices with their start and end apart: 3, of which 3 were waited for; matrix products, arithmetic and copies ran while one was open for 11% of the time, Pallas kernels for 0%

commit v1 on v0

v1 whole, which is shorter than its diff:
```python
import math

import jax
import jax.numpy as jnp
from jax import lax
from jax.sharding import PartitionSpec as P

F16_TOP = 30000.0
CHUNKS = 4


def gelu_value(v):
    return 0.5 * v * (1.0 + lax.erf(v / math.sqrt(2.0)))


def gelu_slope(v):
    return 0.5 * (1.0 + lax.erf(v / math.sqrt(2.0))) + v * jnp.exp(-0.5 * v * v) / math.sqrt(
        2.0 * math.pi
    )


def on_device_plain(grad_out, w_down, pre_act, acc_down):
    total = grad_out.shape[0] * lax.axis_size("row")
    pre_float = pre_act.astype(jnp.float32)
    pre_full = lax.all_gather(pre_act, "col", axis=0, tiled=True)
    act_full = gelu_value(pre_full.astype(jnp.float32)).astype(jnp.bfloat16)
    piece = lax.all_gather(grad_out, "row", axis=0, tiled=True)
    block = lax.dot_general(
        piece, w_down, (((1,), (1,)), ((), ())), preferred_element_type=jnp.float32
    )
    grad_w = lax.dot_general(
        act_full, piece, (((0,), (0,)), ((), ())), preferred_element_type=jnp.float32
    )
    summed = lax.psum_scatter(block, "col", scatter_dimension=0, tiled=True)
    grad_pre = (summed * gelu_slope(pre_float)).astype(jnp.bfloat16)
    acc_new = acc_down + grad_w * float(total) ** (-0.5)
    return (acc_new, grad_pre)


def matmul_t(a, b):
    return lax.dot_general(a, b, (((1,), (1,)), ((), ())), preferred_element_type=jnp.float32)


def on_device_paired(grad_out, w_down, pre_act, acc_down):
    rows, feats = grad_out.shape
    hidden = w_down.shape[0]
    tokens = pre_act.shape[0]
    total = rows * 8
    row, col = lax.axis_index("row"), lax.axis_index("col")
    z, x = row // 2, row % 2
    y, core = col // 2, col % 2
    over_y = [(i, i ^ 2) for i in range(4)]
    over_core = [(i, i ^ 1) for i in range(4)]
    over_x = [(i, i ^ 1) for i in range(8)]
    next_z = [(i, (i + 2) % 8) for i in range(8)]

    pre_far = lax.ppermute(pre_act, "col", over_y)

    tops = jnp.stack([
        jnp.max(jnp.abs(grad_out.astype(jnp.float32))),
        jnp.max(jnp.abs(w_down.astype(jnp.float32))),
    ])
    tops = lax.pmax(tops, ("row", "col"))
    scale = F16_TOP / jnp.maximum(2.0 * feats * tops[0] * tops[1], 1e-30)
    unscale = 1.0 / scale

    shard = grad_out
    piece = jnp.zeros((4, 2, rows, feats), jnp.bfloat16)
    for k in range(4):
        zk = (z + 4 - k) % 4
        other = lax.ppermute(shard, "row", over_x)
        piece = lax.dynamic_update_slice(piece, shard[None, None], (zk, x, 0, 0))
        piece = lax.dynamic_update_slice(piece, other[None, None], (zk, 1 - x, 0, 0))
        if k < 3:
            shard = lax.ppermute(shard, "row", next_z)
    piece = piece.reshape(4, 2 * rows, feats)

    def block_of(b):
        return lax.dynamic_index_in_dim(piece, b, 0, keepdims=False)

    far_mine, far_sib = block_of(2 * (1 - y) + core), block_of(2 * (1 - y) + 1 - core)
    near_mine, near_sib = block_of(2 * y + core), block_of(2 * y + 1 - core)
    width = hidden // CHUNKS
    arrived = []
    for j in range(CHUNKS):
        w = w_down[j * width:(j + 1) * width]
        out = (matmul_t(far_sib, w) * scale).astype(jnp.float16)
        back = lax.ppermute(out, "col", over_core)
        pair = matmul_t(far_mine, w) * scale + back.astype(jnp.float32)
        arrived.append(lax.ppermute(pair.astype(jnp.float16), "col", over_y))

    act = gelu_value(jnp.stack([pre_act, pre_far]).astype(jnp.float32)).astype(jnp.bfloat16)
    act_sib = lax.ppermute(act, "col", over_core)

    near_out = (matmul_t(near_sib, w_down) * scale).astype(jnp.float16)
    near_back = lax.ppermute(near_out, "col", over_core)
    near = matmul_t(near_mine, w_down) * scale + near_back.astype(jnp.float32)

    act_full = jnp.concatenate([act[0], act[1], act_sib[0], act_sib[1]], axis=0)
    piece_full = jnp.concatenate([near_mine, far_mine, near_sib, far_sib], axis=0)
    grad_w = lax.dot_general(
        act_full, piece_full, (((0,), (0,)), ((), ())), preferred_element_type=jnp.float32
    )
    acc_new = acc_down + grad_w * float(total) ** (-0.5)

    slope = gelu_slope(pre_act.astype(jnp.float32))
    parts = []
    for j in range(CHUNKS):
        cut = slice(j * width, (j + 1) * width)
        both = (near[:, cut] + arrived[j].astype(jnp.float32)) * unscale
        parts.append((both * slope[:, cut]).astype(jnp.bfloat16))
    return (acc_new, jnp.concatenate(parts, axis=1))


def solution(mesh):
    paired = mesh.shape["row"] == 8 and mesh.shape["col"] == 4
    return jax.shard_map(
        on_device_paired if paired else on_device_plain,
        mesh=mesh,
        in_specs=(P("row", "col"), P("row", "col"), P("col", "row"), P("row", "col")),
        out_specs=(P("row", "col"), P("col", "row")),
        check_vma=False,
    )
```

time: 232 us -> 174 us (0.75)
  waiting for transfers between devices: 188 us -> 49.1 us
  blocking collectives: 0 us -> 58.3 us
  starting transfers between devices: 0.11 us -> 17.5 us
  between operations: 13.8 us -> 2.39 us
  other arithmetic: 3.68 us -> 14.7 us
  local copies, waits for them, and re-layouts: 0.01 us -> 8.62 us
  matrix products: 26.1 us -> 22.7 us
    all_gather x2 -> x0, waiting for transfers between devices: 98.9 us -> none  [the longest x1 64.7 us: on_device(): piece = lax.all_gather(grad_out, 'row', axis=0, tiled=True)]
    reduce_scatter x1 -> x0, waiting for transfers between devices: 87.9 us -> none  [on_device(): lax.psum_scatter(partial_act, 'col', scatter_dimension=0, tiled=True)]
    pmax x0 -> x1, blocking collectives: none -> 58.3 us  [on_device_paired(): tops = lax.pmax(tops, ('row', 'col'))]
    ppermute x0 -> x18, waiting for transfers between devices: none -> 49.1 us  [the longest x4 28.5 us: on_device_paired(): arrived.append(lax.ppermute(pair.astype(jnp.float16), 'col', over_y))]
    ppermute x0 -> x18, starting transfers between devices: none -> 17.5 us  [the longest x4 6.83 us: on_device_paired(): other = lax.ppermute(shard, 'row', over_x)]
    reduce_max x0 -> x2, other arithmetic: none -> 5.41 us  [the longest x1 3.76 us: on_device_paired(): jnp.max(jnp.abs(w_down.astype(jnp.float32)))]
    unnamed x2 -> x26, local copies, waits for them, and re-layouts: 0.01 us -> 4.55 us
    dot_general x2 -> x11, matrix products: 26.1 us -> 22.7 us  [the longest x1 13.9 us: on_device_paired(): lax.dot_general(act_full, piece_full, (((0,), (0,)), ((), ())), preferred...]
  transfers between devices with their start and end apart: 3 -> 18, of which waited for: 3 -> 8; matrix products, arithmetic and copies ran while one was open for 11% -> 16% of each run, Pallas kernels for 0% -> 0%
where the time goes in v1:
time: 174 us; the launch traced here: 173 us
  blocking collectives  58.3 us (34%)
  waiting for transfers between devices  49.1 us (28%)
  matrix products  22.7 us (13%)
  starting transfers between devices  17.5 us (10%)
  other arithmetic  14.7 us (8%)
  local copies, waits for them, and re-layouts  8.62 us (5%)
  between operations  2.39 us (1%)
    pmax x1, blocking collectives, on_device_paired(): tops = lax.pmax(tops, ('row', 'col'))  58.3 us
    ppermute x4, waiting for transfers between devices, on_device_paired(): arrived.append(lax.ppermute(pair.astype(jnp.float16), 'col', over_y))  28.5 us
    ppermute x3, waiting for transfers between devices, on_device_paired(): shard = lax.ppermute(shard, 'row', next_z)  17 us
    dot_general x1, matrix products, on_device_paired(): lax.dot_general(act_full, piece_full, (((0,), (0,)), ((), ())), preferred...  13.9 us
    dot_general x10, matrix products, matmul_t(): lax.dot_general(a, b, (((1,), (1,)), ((), ())), preferred_element_type=jn...  8.79 us
    ppermute x4, starting transfers between devices, on_device_paired(): other = lax.ppermute(shard, 'row', over_x)  6.83 us
    unnamed x26, local copies, waits for them, and re-layouts  4.55 us
    ppermute x4, starting transfers between devices, on_device_paired(): arrived.append(lax.ppermute(pair.astype(jnp.float16), 'col', over_y))  4.33 us
  transfers between devices with their start and end apart: 18, of which 8 were waited for; matrix products, arithmetic and copies ran while one was open for 16% of the time, Pallas kernels for 0%

profile of v1, /device:TPU:0, one launch (start us, length us, event | category | flops | bytes accessed | tf_op | source)
XLA Modules:
  0.0 173.3 jit_solution(4479203495001985847)
XLA Ops:
  0.6 3.0 %collective-permute-start.2 = (bf16[192,1024]{1,0:T(8,128)(2,1)}, bf16[192,1024]{1,0:T(8,128)(2,1)}, u32[]{:S(2)}, u32[]{:S(2)}) collective-permute-start(bf16[192,1024]{1,0:T(8,128)(2,1)} %param.4), channel_id=1, source_target_pairs={{0,4},{4,0},{8,12},{12,8},{16,20},{20,16},{24,28},{28,24},{1,5},{5... | collective-permute-start | bytes 1179656 | tf_op jit(solution)/shard_map/ppermute | solution.py:71
  3.6 1.6 collective-permute-start.3
  5.2 1.5 collective-permute-start
  6.7 1.7 abs_reduce_fusion.1
  8.4 3.8 %abs_reduce_fusion = f32[]{:T(128)} fusion(bf16[2048,1024]{1,0:T(8,128)(2,1)} %param.5), kind=kLoop, calls=%fused_computation | loop fusion | flops 6291455 | bytes 4194308 | tf_op jit(solution)/shard_map/reduce_max | solution.py:61
  12.2 1.4 pad_maximum_fusion.1
  13.5 2.4 %fusion.17 = f32[384,2048]{1,0:T(8,128)} fusion(bf16[384,2048]{1,0:T(8,128)(2,1)S(1)} %copy-done.1), kind=kLoop, calls=%fused_computation.23 | loop fusion | flops 7077888 | bytes 4718592 | tf_op jit(solution)/shard_map/add | solution.py:17
  15.9 58.3 %pmax.7 = f32[2]{0:T(128)S(1)} all-reduce(f32[2]{0:T(128)S(1)} %pad_maximum_fusion.1), channel_id=1, replica_groups=mesh['row'=8,'col'=4] {'row','col'}, use_global_device_ids=true, to_apply=%region_2.3 | all-reduce | flops 2 | bytes 16 | tf_op jit(solution)/shard_map/pmax | solution.py:63
  74.3 0.4 broadcast_in_dim.27
  74.7 0.6 fusion.56
  76.7 2.3 %collective-permute-start.4 = (bf16[192,1024]{1,0:T(8,128)(2,1)}, bf16[192,1024]{1,0:T(8,128)(2,1)S(1)}, u32[]{:S(2)}, u32[]{:S(2)}) collective-permute-start(bf16[192,1024]{1,0:T(8,128)(2,1)} %collective-permute-done.3), channel_id=1, source_target_pairs={{0,4},{4,0},{8,12},{12,8},{16,20},{20,16},{24,28},{28,24},{1,5},{5... | collective-permute-start | bytes 1179656 | tf_op jit(solution)/shard_map/ppermute | solution.py:71
  79.0 1.7 %collective-permute-start.5 = (bf16[192,1024]{1,0:T(8,128)(2,1)}, bf16[192,1024]{1,0:T(8,128)(2,1)S(1)}, u32[]{:S(2)}, u32[]{:S(2)}) collective-permute-start(bf16[192,1024]{1,0:T(8,128)(2,1)} %collective-permute-done.3), channel_id=1, source_target_pairs={{0,8},{4,12},{8,16},{12,20},{16,24},{20,28},{24,0},{28,4},{1,9},{5... | collective-permute-start | bytes 1179656 | tf_op jit(solution)/shard_map/ppermute | solution.py:75
  80.8 1.0 bitcast_dynamic-update-slice_fusion.6
  81.8 1.0 bitcast_dynamic-update-slice_fusion.5
  82.9 7.0 %collective-permute-done.5 = bf16[192,1024]{1,0:T(8,128)(2,1)S(1)} collective-permute-done((bf16[192,1024]{1,0:T(8,128)(2,1)}, bf16[192,1024]{1,0:T(8,128)(2,1)S(1)}, u32[]{:S(2)}, u32[]{:S(2)}) %collective-permute-start.5) | collective-permute-done | bytes 393248 | tf_op jit(solution)/shard_map/ppermute | solution.py:75
  89.9 0.7 collective-permute-start.6
  90.7 10.0 %collective-permute-done.7 = bf16[192,1024]{1,0:T(8,128)(2,1)S(1)} collective-permute-done((bf16[192,1024]{1,0:T(8,128)(2,1)S(1)}, bf16[192,1024]{1,0:T(8,128)(2,1)S(1)}, u32[]{:S(2)}, u32[]{:S(2)}) %collective-permute-start.7) | collective-permute-done | bytes 393248 | tf_op jit(solution)/shard_map/ppermute | solution.py:75
  100.7 0.8 collective-permute-start.8
  101.6 3.2 %fusion.1 = bf16[2,384,2048]{2,1,0:T(8,128)(2,1)S(1)} fusion(bf16[1,384,2048]{2,1,0:T(8,128)(2,1)} %bitcast.1, bf16[1,384,2048]{2,1,0:T(8,128)(2,1)S(1)} %bitcast.52), kind=kLoop, calls=%fused_computation.5 | loop fusion | flops 14155776 | bytes 6291456 | tf_op jit(solution)/shard_map/convert_element_type | solution.py:92
  105.1 3.3 %collective-permute-done.8 = bf16[192,1024]{1,0:T(8,128)(2,1)S(1)} collective-permute-done((bf16[192,1024]{1,0:T(8,128)(2,1)S(1)}, bf16[192,1024]{1,0:T(8,128)(2,1)S(1)}, u32[]{:S(2)}, u32[]{:S(2)}) %collective-permute-start.8) | collective-permute-done | bytes 393248 | tf_op jit(solution)/shard_map/ppermute | solution.py:71
  108.5 0.4 dynamic-slice_bitcast_fusion.3
  108.9 2.9 %copy-done.3 = bf16[2048,1024]{1,0:T(8,128)(2,1)S(1)} copy-done((bf16[2048,1024]{1,0:T(8,128)(2,1)S(1)}, bf16[2048,1024]{1,0:T(8,128)(2,1)}, u32[]{:S(2)}) %copy-start.3) | copy-done | bytes 4194328
  111.8 1.8 %multiply_convert_fusion = f16[384,2048]{1,0:T(8,128)(2,1)S(1)} fusion(bf16[384,1024]{1,0:T(8,128)(2,1)S(1)} %get-tuple-element.8, bf16[2048,1024]{1,0:T(8,128)(2,1)S(1)} %copy-done.3, f32[]{:T(128)} %bitcast.21), kind=kOutput, calls=%fused_computation.34 | convolution fusion | flops 1612185600 | bytes 6553604 | tf_op jit(solution)/shard_map/dot_general | solution.py:41
  113.7 0.6 fusion.27
  114.4 0.6 collective-permute-start.10
  114.9 0.6 fusion.30
  115.5 0.6 fusion.29
  116.2 0.6 fusion.28
  116.9 0.6 collective-permute-start.14
  117.4 0.3 collective-permute-done.10
  117.8 0.7 add_convert_fusion.3
  118.5 1.5 collective-permute-start.11
  120.1 0.7 add_convert_fusion
  120.7 0.7 collective-permute-start.17
  121.4 0.7 add_convert_fusion.1
  122.1 1.5 collective-permute-start.15
  123.6 0.7 add_convert_fusion.2
  124.3 0.7 collective-permute-start.13
  124.9 1.9 %convert_add_fusion = f32[384,2048]{1,0:T(8,128)S(1)} fusion(f16[384,2048]{1,0:T(8,128)(2,1)S(1)} %collective-permute-done.9, bf16[384,1024]{1,0:T(8,128)(2,1)S(1)} %get-tuple-element.6, bf16[2048,1024]{1,0:T(8,128)(2,1)S(1)} %copy-done.3, f32[]{:T(128)} %bitcast.21), kind=kOutput, calls=%fused_computation.33 | convolution fusion | flops 1612972032 | bytes 9699332 | tf_op jit(solution)/shard_map/dot_general | solution.py:41
  126.8 3.7 %collective-permute-done.11 = f16[384,512]{1,0:T(8,128)(2,1)S(1)} collective-permute-done((f16[384,512]{1,0:T(8,128)(2,1)S(1)}, f16[384,512]{1,0:T(8,128)(2,1)S(1)}, u32[]{:S(2)}, u32[]{:S(2)}) %collective-permute-start.11) | collective-permute-done | bytes 393248 | tf_op jit(solution)/shard_map/ppermute | solution.py:90
  130.5 8.4 %collective-permute-done.17 = f16[384,512]{1,0:T(8,128)(2,1)S(1)} collective-permute-done((f16[384,512]{1,0:T(8,128)(2,1)S(1)}, f16[384,512]{1,0:T(8,128)(2,1)S(1)}, u32[]{:S(2)}, u32[]{:S(2)}) %collective-permute-start.17) | collective-permute-done | bytes 393248 | tf_op jit(solution)/shard_map/ppermute | solution.py:90
  139.0 8.4 %collective-permute-done.15 = f16[384,512]{1,0:T(8,128)(2,1)S(1)} collective-permute-done((f16[384,512]{1,0:T(8,128)(2,1)S(1)}, f16[384,512]{1,0:T(8,128)(2,1)S(1)}, u32[]{:S(2)}, u32[]{:S(2)}) %collective-permute-start.15) | collective-permute-done | bytes 393248 | tf_op jit(solution)/shard_map/ppermute | solution.py:90
  147.4 7.9 %collective-permute-done.13 = f16[384,512]{1,0:T(8,128)(2,1)S(1)} collective-permute-done((f16[384,512]{1,0:T(8,128)(2,1)S(1)}, f16[384,512]{1,0:T(8,128)(2,1)S(1)}, u32[]{:S(2)}, u32[]{:S(2)}) %collective-permute-start.13) | collective-permute-done | bytes 393248 | tf_op jit(solution)/shard_map/ppermute | solution.py:90
  155.3 0.9 fusion.45
  156.2 1.3 pad_maximum_fusion
  157.8 0.9 copy-done.6
  158.7 0.2 copy-done.8
  159.4 13.9 %multiply_add_fusion = f32[2048,1024]{1,0:T(8,128)} fusion(f32[2048,1024]{1,0:T(8,128)} %param.7, bf16[384,2048]{1,0:T(8,128)(2,1)S(1)} %get-tuple-element.13, bf16[384,2048]{1,0:T(8,128)(2,1)S(1)} %get-tuple-element.12, bf16[384,2048]{1,0:T(8,128)(2,1)S(1)} %get-tuple-element.11, bf16[384,2048]{1,0:T(8,128)(2,1)S(1)} %get-tuple-element.10, ...), kind=kOutput, calls=%fused_computation.1 | convolution fusion | flops 6484393984 | bytes 26214400 | tf_op jit(solution)/shard_map/dot_general | solution.py:101
  (46 shorter events, 1.6 us)
Async XLA Ops:
  0.6 12.9 %copy-start.1 = (bf16[384,2048]{1,0:T(8,128)(2,1)S(1)}, bf16[384,2048]{1,0:T(8,128)(2,1)}, u32[]{:S(2)}) copy-start(bf16[384,2048]{1,0:T(8,128)(2,1)} %param.6) | copy-start | bytes 4718596
  0.6 80.1 %collective-permute-start.2 = (bf16[192,1024]{1,0:T(8,128)(2,1)}, bf16[192,1024]{1,0:T(8,128)(2,1)}, u32[]{:S(2)}, u32[]{:S(2)}) collective-permute-start(bf16[192,1024]{1,0:T(8,128)(2,1)} %param.4), channel_id=1, source_target_pairs={{0,4},{4,0},{8,12},{12,8},{16,20},{20,16},{24,28},{28,24},{1,5},{5... | collective-permute-start | bytes 1179656 | tf_op jit(solution)/shard_map/ppermute | solution.py:71
  3.6 73.1 %collective-permute-start.3 = (bf16[192,1024]{1,0:T(8,128)(2,1)}, bf16[192,1024]{1,0:T(8,128)(2,1)}, u32[]{:S(2)}, u32[]{:S(2)}) collective-permute-start(bf16[192,1024]{1,0:T(8,128)(2,1)} %param.4), channel_id=1, source_target_pairs={{0,8},{4,12},{8,16},{12,20},{16,24},{20,28},{24,0},{28,4},{1,9},{5... | collective-permute-start | bytes 1179656 | tf_op jit(solution)/shard_map/ppermute | solution.py:75
  5.2 96.4 %collective-permute-start = (bf16[384,2048]{1,0:T(8,128)(2,1)}, bf16[384,2048]{1,0:T(8,128)(2,1)}, u32[]{:S(2)}, u32[]{:S(2)}) collective-permute-start(bf16[384,2048]{1,0:T(8,128)(2,1)} %param.6), channel_id=1, source_target_pairs={{0,2},{1,3},{2,0},{3,1},{4,6},{5,7},{6,4},{7,5},{8,10},{9,11},{10,... | collective-permute-start | bytes 4718600 | tf_op jit(solution)/shard_map/ppermute | solution.py:57
  13.5 61.2 %copy-start.4 = (bf16[192,1024]{1,0:T(8,128)(2,1)S(1)}, bf16[192,1024]{1,0:T(8,128)(2,1)}, u32[]{:S(2)}) copy-start(bf16[192,1024]{1,0:T(8,128)(2,1)} %param.4) | copy-start | bytes 1179652
  76.7 24.9 %copy-start.2 = (bf16[384,2048]{1,0:T(8,128)(2,1)S(1)}, bf16[384,2048]{1,0:T(8,128)(2,1)}, u32[]{:S(2)}) copy-start(bf16[384,2048]{1,0:T(8,128)(2,1)} %param.6) | copy-start | bytes 4718596
  76.7 13.9 %collective-permute-start.4 = (bf16[192,1024]{1,0:T(8,128)(2,1)}, bf16[192,1024]{1,0:T(8,128)(2,1)S(1)}, u32[]{:S(2)}, u32[]{:S(2)}) collective-permute-start(bf16[192,1024]{1,0:T(8,128)(2,1)} %collective-permute-done.3), channel_id=1, source_target_pairs={{0,4},{4,0},{8,12},{12,8},{16,20},{20,16},{24,28},{28,24},{1,5},{5... | collective-permute-start | bytes 1179656 | tf_op jit(solution)/shard_map/ppermute | solution.py:71
  79.0 10.8 %collective-permute-start.5 = (bf16[192,1024]{1,0:T(8,128)(2,1)}, bf16[192,1024]{1,0:T(8,128)(2,1)S(1)}, u32[]{:S(2)}, u32[]{:S(2)}) collective-permute-start(bf16[192,1024]{1,0:T(8,128)(2,1)} %collective-permute-done.3), channel_id=1, source_target_pairs={{0,8},{4,12},{8,16},{12,20},{16,24},{20,28},{24,0},{28,4},{1,9},{5... | collective-permute-start | bytes 1179656 | tf_op jit(solution)/shard_map/ppermute | solution.py:75
  89.9 11.6 %collective-permute-start.6 = (bf16[192,1024]{1,0:T(8,128)(2,1)S(1)}, bf16[192,1024]{1,0:T(8,128)(2,1)S(1)}, u32[]{:S(2)}, u32[]{:S(2)}) collective-permute-start(bf16[192,1024]{1,0:T(8,128)(2,1)S(1)} %collective-permute-done.5), channel_id=1, source_target_pairs={{0,4},{4,0},{8,12},{12,8},{16,20},{20,16},{24,28},{28,24},{1,5},{5... | collective-permute-start | bytes 1179656 | tf_op jit(solution)/shard_map/ppermute | solution.py:71
  90.6 10.1 %collective-permute-start.7 = (bf16[192,1024]{1,0:T(8,128)(2,1)S(1)}, bf16[192,1024]{1,0:T(8,128)(2,1)S(1)}, u32[]{:S(2)}, u32[]{:S(2)}) collective-permute-start(bf16[192,1024]{1,0:T(8,128)(2,1)S(1)} %collective-permute-done.5), channel_id=1, source_target_pairs={{0,8},{4,12},{8,16},{12,20},{16,24},{20,28},{24,0},{28,4},{1,9},{5... | collective-permute-start | bytes 1179656 | tf_op jit(solution)/shard_map/ppermute | solution.py:75
  100.7 7.8 %collective-permute-start.8 = (bf16[192,1024]{1,0:T(8,128)(2,1)S(1)}, bf16[192,1024]{1,0:T(8,128)(2,1)S(1)}, u32[]{:S(2)}, u32[]{:S(2)}) collective-permute-start(bf16[192,1024]{1,0:T(8,128)(2,1)S(1)} %collective-permute-done.7), channel_id=1, source_target_pairs={{0,4},{4,0},{8,12},{12,8},{16,20},{20,16},{24,28},{28,24},{1,5},{5... | collective-permute-start | bytes 1179656 | tf_op jit(solution)/shard_map/ppermute | solution.py:71
  104.8 52.7 %collective-permute-start.1 = (bf16[2,384,2048]{2,1,0:T(8,128)(2,1)S(1)}, bf16[2,384,2048]{2,1,0:T(8,128)(2,1)S(1)}, u32[]{:S(2)}, u32[]{:S(2)}) collective-permute-start(bf16[2,384,2048]{2,1,0:T(8,128)(2,1)S(1)} %fusion.1), channel_id=1, source_target_pairs={{0,1},{1,0},{2,3},{3,2},{4,5},{5,4},{6,7},{7,6},{8,9},{9,8},{10,11... | collective-permute-start | bytes 9437192 | tf_op jit(solution)/shard_map/ppermute | solution.py:93
  108.5 3.3 %copy-start.3 = (bf16[2048,1024]{1,0:T(8,128)(2,1)S(1)}, bf16[2048,1024]{1,0:T(8,128)(2,1)}, u32[]{:S(2)}) copy-start(bf16[2048,1024]{1,0:T(8,128)(2,1)} %param.5) | copy-start | bytes 12582916
  108.9 4.8 %copy-start.9 = (bf16[384,1024]{1,0:T(8,128)(2,1)}, bf16[384,1024]{1,0:T(8,128)(2,1)S(1)}, u32[]{:S(2)}) copy-start(bf16[384,1024]{1,0:T(8,128)(2,1)S(1)} %get-tuple-element.8) | copy-start | bytes 2359300
  108.9 7.3 %copy-start.7 = (bf16[384,1024]{1,0:T(8,128)(2,1)}, bf16[384,1024]{1,0:T(8,128)(2,1)S(1)}, u32[]{:S(2)}) copy-start(bf16[384,1024]{1,0:T(8,128)(2,1)S(1)} %get-tuple-element.7) | copy-start | bytes 2359300
  108.9 14.7 %copy-start.11 = (bf16[384,1024]{1,0:T(8,128)(2,1)}, bf16[384,1024]{1,0:T(8,128)(2,1)S(1)}, u32[]{:S(2)}) copy-start(bf16[384,1024]{1,0:T(8,128)(2,1)S(1)} %get-tuple-element.9) | copy-start | bytes 2359300
  108.9 16.0 %copy-start.5 = (bf16[384,1024]{1,0:T(8,128)(2,1)}, bf16[384,1024]{1,0:T(8,128)(2,1)S(1)}, u32[]{:S(2)}) copy-start(bf16[384,1024]{1,0:T(8,128)(2,1)S(1)} %get-tuple-element.6) | copy-start | bytes 2359300
  113.7 10.6 %collective-permute-start.9 = (f16[384,2048]{1,0:T(8,128)(2,1)S(1)}, f16[384,2048]{1,0:T(8,128)(2,1)S(1)}, u32[]{:S(2)}, u32[]{:S(2)}) collective-permute-start(f16[384,2048]{1,0:T(8,128)(2,1)S(1)} %multiply_convert_fusion), channel_id=1, source_target_pairs={{0,1},{1,0},{2,3},{3,2},{4,5},{5,4},{6,7},{7,6},{8,9},{9,8},{10,11... | collective-permute-start | bytes 4718600 | tf_op jit(solution)/shard_map/ppermute | solution.py:96
  114.4 3.3 %collective-permute-start.10 = (f16[384,512]{1,0:T(8,128)(2,1)S(1)}, f16[384,512]{1,0:T(8,128)(2,1)S(1)}, u32[]{:S(2)}, u32[]{:S(2)}) collective-permute-start(f16[384,512]{1,0:T(8,128)(2,1)S(1)} %fusion.27), channel_id=1, source_target_pairs={{0,1},{1,0},{2,3},{3,2},{4,5},{5,4},{6,7},{7,6},{8,9},{9,8},{10,11... | collective-permute-start | bytes 1179656 | tf_op jit(solution)/shard_map/ppermute | solution.py:88
  116.1 2.4 %collective-permute-start.16 = (f16[384,512]{1,0:T(8,128)(2,1)S(1)}, f16[384,512]{1,0:T(8,128)(2,1)S(1)}, u32[]{:S(2)}, u32[]{:S(2)}) collective-permute-start(f16[384,512]{1,0:T(8,128)(2,1)S(1)} %fusion.30), channel_id=1, source_target_pairs={{0,1},{1,0},{2,3},{3,2},{4,5},{5,4},{6,7},{7,6},{8,9},{9,8},{10,11... | collective-permute-start | bytes 1179656 | tf_op jit(solution)/shard_map/ppermute | solution.py:88
  116.9 3.9 %collective-permute-start.14 = (f16[384,512]{1,0:T(8,128)(2,1)S(1)}, f16[384,512]{1,0:T(8,128)(2,1)S(1)}, u32[]{:S(2)}, u32[]{:S(2)}) collective-permute-start(f16[384,512]{1,0:T(8,128)(2,1)S(1)} %fusion.29), channel_id=1, source_target_pairs={{0,1},{1,0},{2,3},{3,2},{4,5},{5,4},{6,7},{7,6},{8,9},{9,8},{10,11... | collective-permute-start | bytes 1179656 | tf_op jit(solution)/shard_map/ppermute | solution.py:88
  117.7 4.4 %collective-permute-start.12 = (f16[384,512]{1,0:T(8,128)(2,1)S(1)}, f16[384,512]{1,0:T(8,128)(2,1)S(1)}, u32[]{:S(2)}, u32[]{:S(2)}) collective-permute-start(f16[384,512]{1,0:T(8,128)(2,1)S(1)} %fusion.28), channel_id=1, source_target_pairs={{0,1},{1,0},{2,3},{3,2},{4,5},{5,4},{6,7},{7,6},{8,9},{9,8},{10,11... | collective-permute-start | bytes 1179656 | tf_op jit(solution)/shard_map/ppermute | solution.py:88
  118.5 12.0 %collective-permute-start.11 = (f16[384,512]{1,0:T(8,128)(2,1)S(1)}, f16[384,512]{1,0:T(8,128)(2,1)S(1)}, u32[]{:S(2)}, u32[]{:S(2)}) collective-permute-start(f16[384,512]{1,0:T(8,128)(2,1)S(1)} %add_convert_fusion.3), channel_id=1, source_target_pairs={{0,2},{1,3},{2,0},{3,1},{4,6},{5,7},{6,4},{7,5},{8,10},{9,11},{10,... | collective-permute-start | bytes 1179656 | tf_op jit(solution)/shard_map/ppermute | solution.py:90
  120.7 18.2 %collective-permute-start.17 = (f16[384,512]{1,0:T(8,128)(2,1)S(1)}, f16[384,512]{1,0:T(8,128)(2,1)S(1)}, u32[]{:S(2)}, u32[]{:S(2)}) collective-permute-start(f16[384,512]{1,0:T(8,128)(2,1)S(1)} %add_convert_fusion), channel_id=1, source_target_pairs={{0,2},{1,3},{2,0},{3,1},{4,6},{5,7},{6,4},{7,5},{8,10},{9,11},{10,... | collective-permute-start | bytes 1179656 | tf_op jit(solution)/shard_map/ppermute | solution.py:90
  122.1 25.3 %collective-permute-start.15 = (f16[384,512]{1,0:T(8,128)(2,1)S(1)}, f16[384,512]{1,0:T(8,128)(2,1)S(1)}, u32[]{:S(2)}, u32[]{:S(2)}) collective-permute-start(f16[384,512]{1,0:T(8,128)(2,1)S(1)} %add_convert_fusion.1), channel_id=1, source_target_pairs={{0,2},{1,3},{2,0},{3,1},{4,6},{5,7},{6,4},{7,5},{8,10},{9,11},{10,... | collective-permute-start | bytes 1179656 | tf_op jit(solution)/shard_map/ppermute | solution.py:90
  124.3 31.0 %collective-permute-start.13 = (f16[384,512]{1,0:T(8,128)(2,1)S(1)}, f16[384,512]{1,0:T(8,128)(2,1)S(1)}, u32[]{:S(2)}, u32[]{:S(2)}) collective-permute-start(f16[384,512]{1,0:T(8,128)(2,1)S(1)} %add_convert_fusion.2), channel_id=1, source_target_pairs={{0,2},{1,3},{2,0},{3,1},{4,6},{5,7},{6,4},{7,5},{8,10},{9,11},{10,... | collective-permute-start | bytes 1179656 | tf_op jit(solution)/shard_map/ppermute | solution.py:90
  124.9 30.3 %copy-start = (f32[384,2048]{1,0:T(8,128)S(1)}, f32[384,2048]{1,0:T(8,128)}, u32[]{:S(2)}) copy-start(f32[384,2048]{1,0:T(8,128)} %fusion.17) | copy-start | bytes 9437188
  157.6 1.1 copy-start.6
  157.6 1.4 copy-start.8
  157.6 1.6 copy-start.10
  157.6 1.8 %copy-start.12 = (bf16[384,1024]{1,0:T(8,128)(2,1)S(1)}, bf16[384,1024]{1,0:T(8,128)(2,1)}, u32[]{:S(2)}) copy-start(bf16[384,1024]{1,0:T(8,128)(2,1)} %copy-done.11) | copy-start | bytes 2359300

commit v2 on v1

--- a/solution.py
+++ b/solution.py
@@ -56,13 +56,11 @@
 
     pre_far = lax.ppermute(pre_act, "col", over_y)
 
-    tops = jnp.stack([
-        jnp.max(jnp.abs(grad_out.astype(jnp.float32))),
-        jnp.max(jnp.abs(w_down.astype(jnp.float32))),
-    ])
-    tops = lax.pmax(tops, ("row", "col"))
-    scale = F16_TOP / jnp.maximum(2.0 * feats * tops[0] * tops[1], 1e-30)
-    unscale = 1.0 / scale
+    def top(v):
+        return jnp.max(jnp.abs(v)).astype(jnp.float32)
+
+    w_top = top(w_down)
+    g_top = top(grad_out)
 
     shard = grad_out
     piece = jnp.zeros((4, 2, rows, feats), jnp.bfloat16)
@@ -71,9 +69,17 @@
         other = lax.ppermute(shard, "row", over_x)
         piece = lax.dynamic_update_slice(piece, shard[None, None], (zk, x, 0, 0))
         piece = lax.dynamic_update_slice(piece, other[None, None], (zk, 1 - x, 0, 0))
+        g_top = jnp.maximum(g_top, jnp.maximum(top(shard), top(other)))
         if k < 3:
             shard = lax.ppermute(shard, "row", next_z)
     piece = piece.reshape(4, 2 * rows, feats)
+
+    bound = jnp.full((8, 128), jnp.maximum(feats * g_top * w_top, 1e-30))
+    bound_sib = lax.ppermute(bound, "col", over_core)
+    bound_pair = bound + bound_sib
+    bound_far = lax.ppermute(bound_pair, "col", over_y)
+    scale, from_sib = F16_TOP / bound[0, 0], bound_sib[0, 0] / F16_TOP
+    to_far, from_far = F16_TOP / bound_pair[0, 0], bound_far[0, 0] / F16_TOP
 
     def block_of(b):
         return lax.dynamic_index_in_dim(piece, b, 0, keepdims=False)
@@ -81,20 +87,21 @@
     far_mine, far_sib = block_of(2 * (1 - y) + core), block_of(2 * (1 - y) + 1 - core)
     near_mine, near_sib = block_of(2 * y + core), block_of(2 * y + 1 - core)
     width = hidden // CHUNKS
-    arrived = []
+    pairs = []
     for j in range(CHUNKS):
         w = w_down[j * width:(j + 1) * width]
         out = (matmul_t(far_sib, w) * scale).astype(jnp.float16)
         back = lax.ppermute(out, "col", over_core)
-        pair = matmul_t(far_mine, w) * scale + back.astype(jnp.float32)
-        arrived.append(lax.ppermute(pair.astype(jnp.float16), "col", over_y))
+        pair = matmul_t(far_mine, w) + back.astype(jnp.float32) * from_sib
+        pairs.append((pair * to_far).astype(jnp.float16))
+    arrived = [lax.ppermute(pair, "col", over_y) for pair in pairs[:-1]]
 
     act = gelu_value(jnp.stack([pre_act, pre_far]).astype(jnp.float32)).astype(jnp.bfloat16)
     act_sib = lax.ppermute(act, "col", over_core)
 
     near_out = (matmul_t(near_sib, w_down) * scale).astype(jnp.float16)
     near_back = lax.ppermute(near_out, "col", over_core)
-    near = matmul_t(near_mine, w_down) * scale + near_back.astype(jnp.float32)
+    near = matmul_t(near_mine, w_down) + near_back.astype(jnp.float32) * from_sib
 
     act_full = jnp.concatenate([act[0], act[1], act_sib[0], act_sib[1]], axis=0)
     piece_full = jnp.concatenate([near_mine, far_mine, near_sib, far_sib], axis=0)
@@ -103,11 +110,14 @@
     )
     acc_new = acc_down + grad_w * float(total) ** (-0.5)
 
+    last, acc_new = lax.optimization_barrier((pairs[-1], acc_new))
+    arrived.append(lax.ppermute(last, "col", over_y))
+
     slope = gelu_slope(pre_act.astype(jnp.float32))
     parts = []
     for j in range(CHUNKS):
         cut = slice(j * width, (j + 1) * width)
-        both = (near[:, cut] + arrived[j].astype(jnp.float32)) * unscale
+        both = near[:, cut] + arrived[j].astype(jnp.float32) * from_far
         parts.append((both * slope[:, cut]).astype(jnp.bfloat16))
     return (acc_new, jnp.concatenate(parts, axis=1))
 

time: 174 us -> 112 us (0.64)
  blocking collectives: 58.3 us -> 0 us
  waiting for transfers between devices: 49.1 us -> 15.1 us
  other arithmetic: 14.7 us -> 25.1 us
  local copies, waits for them, and re-layouts: 8.62 us -> 16.1 us
  matrix products: 22.7 us -> 29.7 us
  between operations: 2.39 us -> 8.69 us
    pmax x1 -> x0, blocking collectives: 58.3 us -> none  [on_device_paired(): tops = lax.pmax(tops, ('row', 'col'))]
    ppermute x4 -> x6, waiting for transfers between devices: 28.5 us -> 6.32 us  [the longest x1 6.31 us: on_device_paired(): arrived.append(lax.ppermute(last, 'col', over_y))]
    ppermute x3, waiting for transfers between devices: 17 us -> 5.79 us  [on_device_paired(): shard = lax.ppermute(shard, 'row', next_z)]
    reduce_max x2 -> x9, other arithmetic: 5.41 us -> 14.4 us  [top(): return jnp.max(jnp.abs(v)).astype(jnp.float32)]
    dot_general x10, matrix products: 8.79 us -> 14.5 us  [matmul_t(): lax.dot_general(a, b, (((1,), (1,)), ((), ())), preferred_element_type=jn...]
    unnamed x26 -> x18, local copies, waits for them, and re-layouts: 4.55 us -> 0.04 us
    squeeze x2, local copies, waits for them, and re-layouts: 0.44 us -> 4.92 us  [on_device_paired(): act_full = jnp.concatenate([act[0], act[1], act_sib[0], act_sib[1]], axis=0)]
    squeeze x1, local copies, waits for them, and re-layouts: 0.36 us -> 3.22 us  [block_of(): return lax.dynamic_index_in_dim(piece, b, 0, keepdims=False)]
  transfers between devices with their start and end apart: 18 -> 20, of which waited for: 8 -> 4; matrix products, arithmetic and copies ran while one was open for 16% -> 60% of each run, Pallas kernels for 0% -> 0%
where the time goes in v2:
time: 112 us
  matrix products  29.7 us (27%)
  other arithmetic  25.1 us (22%)
  starting transfers between devices  16.9 us (15%)
  local copies, waits for them, and re-layouts  16.1 us (14%)
  waiting for transfers between devices  15.1 us (13%)
  between operations  8.69 us (8%)
    dot_general x1, matrix products, on_device_paired(): lax.dot_general(act_full, piece_full, (((0,), (0,)), ((), ())), preferred...  15.2 us
    dot_general x10, matrix products, matmul_t(): lax.dot_general(a, b, (((1,), (1,)), ((), ())), preferred_element_type=jn...  14.5 us
    reduce_max x9, other arithmetic, top(): return jnp.max(jnp.abs(v)).astype(jnp.float32)  14.4 us
    ppermute x1, waiting for transfers between devices, on_device_paired(): arrived.append(lax.ppermute(last, 'col', over_y))  6.31 us
    ppermute x4, starting transfers between devices, on_device_paired(): other = lax.ppermute(shard, 'row', over_x)  5.94 us
    ppermute x3, waiting for transfers between devices, on_device_paired(): shard = lax.ppermute(shard, 'row', next_z)  5.79 us
    squeeze x2, local copies, waits for them, and re-layouts, on_device_paired(): act_full = jnp.concatenate([act[0], act[1], act_sib[0], act_sib[1]], axis=0)  4.92 us
    dynamic_update_slice x4, local copies, waits for them, and re-layouts, on_device_paired(): lax.dynamic_update_slice(piece, other[None, None], (zk, 1 - x, 0, 0))  3.86 us
  transfers between devices with their start and end apart: 20, of which 4 were waited for; matrix products, arithmetic and copies ran while one was open for 60% of the time, Pallas kernels for 0%

profile of v2, /device:TPU:0, one launch (start us, length us, event | category | flops | bytes accessed | tf_op | source)
XLA Modules:
  0.0 111.6 jit_solution(6728889913449579168)
XLA Ops:
  0.6 3.0 %collective-permute-start = (bf16[192,1024]{1,0:T(8,128)(2,1)}, bf16[192,1024]{1,0:T(8,128)(2,1)}, u32[]{:S(2)}, u32[]{:S(2)}) collective-permute-start(bf16[192,1024]{1,0:T(8,128)(2,1)} %param.4), channel_id=1, source_target_pairs={{0,4},{4,0},{8,12},{12,8},{16,20},{20,16},{24,28},{28,24},{1,5},{5... | collective-permute-start | bytes 1179656 | tf_op jit(solution)/shard_map/ppermute | solution.py:69
  3.6 1.6 %collective-permute-start.1 = (bf16[192,1024]{1,0:T(8,128)(2,1)}, bf16[192,1024]{1,0:T(8,128)(2,1)}, u32[]{:S(2)}, u32[]{:S(2)}) collective-permute-start(bf16[192,1024]{1,0:T(8,128)(2,1)} %param.4), channel_id=1, source_target_pairs={{0,8},{4,12},{8,16},{12,20},{16,24},{20,28},{24,0},{28,4},{1,9},{5... | collective-permute-start | bytes 1179656 | tf_op jit(solution)/shard_map/ppermute | solution.py:74
  5.2 1.5 %collective-permute-start.9 = (bf16[384,2048]{1,0:T(8,128)(2,1)}, bf16[384,2048]{1,0:T(8,128)(2,1)}, u32[]{:S(2)}, u32[]{:S(2)}) collective-permute-start(bf16[384,2048]{1,0:T(8,128)(2,1)} %param.6), channel_id=1, source_target_pairs={{0,2},{1,3},{2,0},{3,1},{4,6},{5,7},{6,4},{7,5},{8,10},{9,11},{10,... | collective-permute-start | bytes 4718600 | tf_op jit(solution)/shard_map/ppermute | solution.py:57
  6.7 3.6 %fusion.17 = f32[384,2048]{1,0:T(8,128)} fusion(bf16[384,2048]{1,0:T(8,128)(2,1)} %param.6), kind=kLoop, calls=%fused_computation.23 | loop fusion | flops 7077888 | bytes 4718592 | tf_op jit(solution)/shard_map/add | solution.py:17
  10.8 0.7 abs_reduce_fusion.8
  11.5 3.8 %abs_reduce_fusion = bf16[]{:T(256)} fusion(bf16[2048,1024]{1,0:T(8,128)(2,1)} %param.5), kind=kLoop, calls=%fused_computation.19 | loop fusion | flops 4194303 | bytes 4194306 | tf_op jit(solution)/shard_map/reduce_max | solution.py:60
  15.2 1.2 %collective-permute-done.1 = bf16[192,1024]{1,0:T(8,128)(2,1)} collective-permute-done((bf16[192,1024]{1,0:T(8,128)(2,1)}, bf16[192,1024]{1,0:T(8,128)(2,1)}, u32[]{:S(2)}, u32[]{:S(2)}) %collective-permute-start.1) | collective-permute-done | bytes 393248 | tf_op jit(solution)/shard_map/ppermute | solution.py:74
  16.4 0.5 collective-permute-start.2
  17.3 1.0 bitcast_dynamic-update-slice_fusion.6
  18.4 1.7 %abs_reduce_fusion.7 = bf16[]{:T(256)} fusion(bf16[192,1024]{1,0:T(8,128)(2,1)} %collective-permute-done), kind=kLoop, calls=%fused_computation.94 | loop fusion | flops 393215 | bytes 393218 | tf_op jit(solution)/shard_map/reduce_max | solution.py:60
  20.0 1.0 bitcast_dynamic-update-slice_fusion.5
  21.1 1.7 %abs_reduce_fusion.6 = bf16[]{:T(256)} fusion(bf16[192,1024]{1,0:T(8,128)(2,1)} %collective-permute-done.1), kind=kLoop, calls=%fused_computation.93 | loop fusion | flops 393215 | bytes 393218 | tf_op jit(solution)/shard_map/reduce_max | solution.py:60
  24.1 4.6 %collective-permute-done.3 = bf16[192,1024]{1,0:T(8,128)(2,1)S(1)} collective-permute-done((bf16[192,1024]{1,0:T(8,128)(2,1)}, bf16[192,1024]{1,0:T(8,128)(2,1)S(1)}, u32[]{:S(2)}, u32[]{:S(2)}) %collective-permute-start.3) | collective-permute-done | bytes 393248 | tf_op jit(solution)/shard_map/ppermute | solution.py:74
  28.7 1.3 %collective-permute-start.4 = (bf16[192,1024]{1,0:T(8,128)(2,1)S(1)}, bf16[192,1024]{1,0:T(8,128)(2,1)}, u32[]{:S(2)}, u32[]{:S(2)}) collective-permute-start(bf16[192,1024]{1,0:T(8,128)(2,1)S(1)} %collective-permute-done.3), channel_id=1, source_target_pairs={{0,4},{4,0},{8,12},{12,8},{16,20},{20,16},{24,28},{28,24},{1,5},{5... | collective-permute-start | bytes 1179656 | tf_op jit(solution)/shard_map/ppermute | solution.py:69
  29.9 1.0 bitcast_dynamic-update-slice_fusion.4
  31.0 1.7 %abs_reduce_fusion.5 = bf16[]{:T(256)} fusion(bf16[192,1024]{1,0:T(8,128)(2,1)} %collective-permute-done.2), kind=kLoop, calls=%fused_computation.92 | loop fusion | flops 393215 | bytes 393218 | tf_op jit(solution)/shard_map/reduce_max | solution.py:60
  32.6 0.7 abs_reduce_fusion.4
  34.6 2.9 %collective-permute-done.4 = bf16[192,1024]{1,0:T(8,128)(2,1)} collective-permute-done((bf16[192,1024]{1,0:T(8,128)(2,1)S(1)}, bf16[192,1024]{1,0:T(8,128)(2,1)}, u32[]{:S(2)}, u32[]{:S(2)}) %collective-permute-start.4) | collective-permute-done | bytes 393248 | tf_op jit(solution)/shard_map/ppermute | solution.py:69
  37.5 1.7 %abs_reduce_fusion.3 = bf16[]{:T(256)} fusion(bf16[192,1024]{1,0:T(8,128)(2,1)} %collective-permute-done.4), kind=kLoop, calls=%fused_computation.90 | loop fusion | flops 393215 | bytes 393218 | tf_op jit(solution)/shard_map/reduce_max | solution.py:60
  40.5 1.1 %collective-permute-start.6 = (bf16[192,1024]{1,0:T(8,128)(2,1)}, bf16[192,1024]{1,0:T(8,128)(2,1)S(1)}, u32[]{:S(2)}, u32[]{:S(2)}) collective-permute-start(bf16[192,1024]{1,0:T(8,128)(2,1)} %collective-permute-done.5), channel_id=1, source_target_pairs={{0,4},{4,0},{8,12},{12,8},{16,20},{20,16},{24,28},{28,24},{1,5},{5... | collective-permute-start | bytes 1179656 | tf_op jit(solution)/shard_map/ppermute | solution.py:69
  41.7 1.0 bitcast_dynamic-update-slice_fusion.2
  42.7 1.0 bitcast_dynamic-update-slice_fusion.1
  43.7 1.9 %abs_reduce_fusion.2 = bf16[]{:T(256)} fusion(bf16[192,1024]{1,0:T(8,128)(2,1)} %collective-permute-done.5), kind=kLoop, calls=%fused_computation.89 | loop fusion | flops 393215 | bytes 393218 | tf_op jit(solution)/shard_map/reduce_max | solution.py:60
  45.7 3.5 %fusion.1 = bf16[2,384,2048]{2,1,0:T(8,128)(2,1)S(1)} fusion(bf16[1,384,2048]{2,1,0:T(8,128)(2,1)} %bitcast.14, bf16[1,384,2048]{2,1,0:T(8,128)(2,1)} %bitcast.51), kind=kLoop, calls=%fused_computation.4 | loop fusion | flops 14155776 | bytes 6291456 | tf_op jit(solution)/shard_map/convert_element_type | solution.py:99
  49.3 0.7 abs_reduce_fusion.1
  51.9 0.8 bitcast_dynamic-update-slice_fusion
  52.7 3.2 %dynamic-slice_bitcast_fusion.1 = (bf16[384,1024]{1,0:T(8,128)(2,1)}, bf16[384,1024]{1,0:T(8,128)(2,1)S(1)}, bf16[384,1024]{1,0:T(8,128)(2,1)S(1)}, bf16[384,1024]{1,0:T(8,128)(2,1)S(1)}) fusion(bf16[4,384,1024]{2,1,0:T(8,128)(2,1)} %bitcast.50, s32[]{:T(128)S(6)} %select_n.91, s32[]{:T(128)S(6)} %select_n.92, s32[]{:T(128)S(6)} %select_n.90, s32[]{:T(128)S(6)} %select_n.89), kind=kLoop, calls=%fused_computation.76 | loop fusion | bytes 6291472 | tf_op jit(solution)/shard_map/jit(dynamic_index_in_dim)/squeeze | solution.py:85
  55.9 0.7 fusion.27
  56.6 0.7 fusion.30
  57.2 0.6 collective-permute-start.7
  57.9 3.0 %multiply_convert_fusion = f16[384,2048]{1,0:T(8,128)(2,1)} fusion(bf16[384,1024]{1,0:T(8,128)(2,1)S(1)} %get-tuple-element.11, bf16[2048,1024]{1,0:T(8,128)(2,1)S(1)} %copy-done.2, f32[]{:T(128)S(6)} %div.58), kind=kOutput, calls=%fused_computation.34 | convolution fusion | flops 1612185600 | bytes 6553604 | tf_op jit(solution)/shard_map/dot_general | solution.py:41
  60.9 1.4 %slice_bitcast_fusion.3 = (bf16[384,2048]{1,0:T(8,128)(2,1)S(1)}, bf16[384,2048]{1,0:T(8,128)(2,1)}) fusion(bf16[2,384,2048]{2,1,0:T(8,128)(2,1)S(1)} %fusion.1), kind=kLoop, calls=%fused_computation.38 | loop fusion | bytes 6291456 | tf_op jit(solution)/shard_map/squeeze | solution.py:106
  62.2 0.7 fusion.28
  63.5 1.5 %collective-permute-start.14 = (f32[8,128]{1,0:T(8,128)S(1)}, f32[8,128]{1,0:T(8,128)S(1)}, u32[]{:S(2)}, u32[]{:S(2)}) collective-permute-start(f32[8,128]{1,0:T(8,128)S(1)} %broadcast_add_fusion), channel_id=1, source_target_pairs={{0,2},{1,3},{2,0},{3,1},{4,6},{5,7},{6,4},{7,5},{8,10},{9,11},{10,... | collective-permute-start | bytes 12296 | tf_op jit(solution)/shard_map/ppermute | solution.py:80
  65.0 0.7 fusion.29
  65.7 0.5 slice.60
  69.9 1.4 %multiply_convert_fusion.3 = f16[384,512]{1,0:T(8,128)(2,1)} fusion(f16[384,512]{1,0:T(8,128)(2,1)S(1)} %collective-permute-done.12, f32[]{:T(128)} %bitcast.12, f32[]{:T(128)} %bitcast.11, bf16[384,1024]{1,0:T(8,128)(2,1)S(1)} %get-tuple-element.13, bf16[2048,1024]{1,0:T(8,128)(2,1)S(1)} %copy-done.2), kind=kOutput, calls=%fused_computation.74 | convolution fusion | flops 403636224 | bytes 2621448 | tf_op jit(solution)/shard_map/dot_general | solution.py:41
  71.8 1.4 %multiply_convert_fusion.1 = f16[384,512]{1,0:T(8,128)(2,1)} fusion(f16[384,512]{1,0:T(8,128)(2,1)S(1)} %collective-permute-done.17, f32[]{:T(128)} %bitcast.12, f32[]{:T(128)} %bitcast.11, bf16[384,1024]{1,0:T(8,128)(2,1)S(1)} %get-tuple-element.13, bf16[2048,1024]{1,0:T(8,128)(2,1)S(1)} %copy-done.2), kind=kOutput, calls=%fused_computation.72 | convolution fusion | flops 403636224 | bytes 2621448 | tf_op jit(solution)/shard_map/dot_general | solution.py:41
  73.2 1.5 %collective-permute-start.18 = (f16[384,512]{1,0:T(8,128)(2,1)}, f16[384,512]{1,0:T(8,128)(2,1)}, u32[]{:S(2)}, u32[]{:S(2)}) collective-permute-start(f16[384,512]{1,0:T(8,128)(2,1)} %multiply_convert_fusion.1), channel_id=1, source_target_pairs={{0,2},{1,3},{2,0},{3,1},{4,6},{5,7},{6,4},{7,5},{8,10},{9,11},{10,... | collective-permute-start | bytes 1179656 | tf_op jit(solution)/shard_map/ppermute | solution.py:97
  74.7 1.4 %multiply_convert_fusion.2 = f16[384,512]{1,0:T(8,128)(2,1)} fusion(f16[384,512]{1,0:T(8,128)(2,1)S(1)} %collective-permute-done.15, f32[]{:T(128)} %bitcast.12, f32[]{:T(128)} %bitcast.11, bf16[384,1024]{1,0:T(8,128)(2,1)S(1)} %get-tuple-element.13, bf16[2048,1024]{1,0:T(8,128)(2,1)S(1)} %copy-done.2), kind=kOutput, calls=%fused_computation.73 | convolution fusion | flops 403636224 | bytes 2621448 | tf_op jit(solution)/shard_map/dot_general | solution.py:41
  76.7 1.4 %multiply_convert_fusion.4 = f16[384,512]{1,0:T(8,128)(2,1)} fusion(f16[384,512]{1,0:T(8,128)(2,1)S(1)} %collective-permute-done.7, f32[]{:T(128)} %bitcast.12, f32[]{:T(128)} %bitcast.11, bf16[384,1024]{1,0:T(8,128)(2,1)S(1)} %get-tuple-element.13, bf16[2048,1024]{1,0:T(8,128)(2,1)S(1)} %copy-done.2), kind=kOutput, calls=%fused_computation.77 | convolution fusion | flops 403636224 | bytes 2621448 | tf_op jit(solution)/shard_map/dot_general | solution.py:41
  78.1 3.6 %slice_bitcast_fusion.1 = (bf16[384,2048]{1,0:T(8,128)(2,1)S(1)}, bf16[384,2048]{1,0:T(8,128)(2,1)}) fusion(bf16[2,384,2048]{2,1,0:T(8,128)(2,1)} %collective-permute-done.10), kind=kLoop, calls=%fused_computation.36 | loop fusion | bytes 6291456 | tf_op jit(solution)/shard_map/squeeze | solution.py:106
  81.7 15.2 %multiply_add_fusion = f32[2048,1024]{1,0:T(8,128)} fusion(f32[2048,1024]{1,0:T(8,128)} %param.7, bf16[384,2048]{1,0:T(8,128)(2,1)} %get-tuple-element.17, bf16[384,2048]{1,0:T(8,128)(2,1)S(1)} %get-tuple-element.16, bf16[384,2048]{1,0:T(8,128)(2,1)S(1)} %copy-done.4, bf16[384,2048]{1,0:T(8,128)(2,1)S(1)} %get-tuple-element.14, ...), kind=kOutput, calls=%fused_computation | convolution fusion | flops 6484393984 | bytes 26214400 | tf_op jit(solution)/shard_map/dot_general | solution.py:108
  96.8 1.5 %collective-permute-start.19 = (f16[384,512]{1,0:T(8,128)(2,1)}, f16[384,512]{1,0:T(8,128)(2,1)S(1)}, u32[]{:S(2)}, u32[]{:S(2)}) collective-permute-start(f16[384,512]{1,0:T(8,128)(2,1)} %multiply_convert_fusion.4), channel_id=1, source_target_pairs={{0,2},{1,3},{2,0},{3,1},{4,6},{5,7},{6,4},{7,5},{8,10},{9,11},{10,... | collective-permute-start | bytes 1179656 | tf_op jit(solution)/shard_map/ppermute | solution.py:114
  98.4 3.2 %multiply_add_fusion.1 = f32[384,2048]{1,0:T(8,128)S(1)} fusion(f16[384,2048]{1,0:T(8,128)(2,1)} %collective-permute-done.11, f32[]{:T(128)} %bitcast.11, bf16[384,1024]{1,0:T(8,128)(2,1)S(1)} %copy-done.5, bf16[2048,1024]{1,0:T(8,128)(2,1)S(1)} %copy-done.2), kind=kOutput, calls=%fused_computation.33 | convolution fusion | flops 1612972032 | bytes 9699332 | tf_op jit(solution)/shard_map/dot_general | solution.py:41
  101.7 6.3 %collective-permute-done.19 = f16[384,512]{1,0:T(8,128)(2,1)S(1)} collective-permute-done((f16[384,512]{1,0:T(8,128)(2,1)}, f16[384,512]{1,0:T(8,128)(2,1)S(1)}, u32[]{:S(2)}, u32[]{:S(2)}) %collective-permute-start.19) | collective-permute-done | bytes 393248 | tf_op jit(solution)/shard_map/ppermute | solution.py:114
  108.0 2.3 %fusion.46 = (bf16[384,512]{1,0:T(8,128)(2,1)S(1)}, bf16[384,512]{1,0:T(8,128)(2,1)S(1)}, bf16[384,512]{1,0:T(8,128)(2,1)S(1)}, bf16[384,512]{1,0:T(8,128)(2,1)S(1)}) fusion(f32[384,2048]{1,0:T(8,128)S(1)} %copy-done.1, f32[384,2048]{1,0:T(8,128)S(1)} %multiply_add_fusion.1, f16[384,512]{1,0:T(8,128)(2,1)} %collective-permute-done.13, f32[]{:T(128)} %bitcast.21, ...), kind=kLoop, calls=%fused_computation.70 | loop fusion | flops 3932160 | bytes 9437188 | tf_op jit(solution)/shard_map/convert_element_type | solution.py:121
  110.3 1.3 %pad_maximum_fusion = bf16[384,2048]{1,0:T(8,128)(2,1)} fusion(bf16[384,512]{1,0:T(8,128)(2,1)S(1)} %get-tuple-element.7, bf16[384,512]{1,0:T(8,128)(2,1)S(1)} %get-tuple-element.8, bf16[384,512]{1,0:T(8,128)(2,1)S(1)} %get-tuple-element.9, bf16[384,512]{1,0:T(8,128)(2,1)S(1)} %get-tuple-element.6), kind=kLoop, calls=%fused_computation.39 | loop fusion | flops 6291456 | bytes 3145728 | tf_op jit(solution)/shard_map/concatenate | solution.py:122
  (51 shorter events, 4.4 us)
Async XLA Ops:
  0.6 16.7 %collective-permute-start = (bf16[192,1024]{1,0:T(8,128)(2,1)}, bf16[192,1024]{1,0:T(8,128)(2,1)}, u32[]{:S(2)}, u32[]{:S(2)}) collective-permute-start(bf16[192,1024]{1,0:T(8,128)(2,1)} %param.4), channel_id=1, source_target_pairs={{0,4},{4,0},{8,12},{12,8},{16,20},{20,16},{24,28},{28,24},{1,5},{5... | collective-permute-start | bytes 1179656 | tf_op jit(solution)/shard_map/ppermute | solution.py:69
  3.6 12.8 %collective-permute-start.1 = (bf16[192,1024]{1,0:T(8,128)(2,1)}, bf16[192,1024]{1,0:T(8,128)(2,1)}, u32[]{:S(2)}, u32[]{:S(2)}) collective-permute-start(bf16[192,1024]{1,0:T(8,128)(2,1)} %param.4), channel_id=1, source_target_pairs={{0,8},{4,12},{8,16},{12,20},{16,24},{20,28},{24,0},{28,4},{1,9},{5... | collective-permute-start | bytes 1179656 | tf_op jit(solution)/shard_map/ppermute | solution.py:74
  5.2 40.5 %collective-permute-start.9 = (bf16[384,2048]{1,0:T(8,128)(2,1)}, bf16[384,2048]{1,0:T(8,128)(2,1)}, u32[]{:S(2)}, u32[]{:S(2)}) collective-permute-start(bf16[384,2048]{1,0:T(8,128)(2,1)} %param.6), channel_id=1, source_target_pairs={{0,2},{1,3},{2,0},{3,1},{4,6},{5,7},{6,4},{7,5},{8,10},{9,11},{10,... | collective-permute-start | bytes 4718600 | tf_op jit(solution)/shard_map/ppermute | solution.py:57
  6.7 4.0 %copy-start.3 = (bf16[192,1024]{1,0:T(8,128)(2,1)S(1)}, bf16[192,1024]{1,0:T(8,128)(2,1)}, u32[]{:S(2)}) copy-start(bf16[192,1024]{1,0:T(8,128)(2,1)} %param.4) | copy-start | bytes 1179652
  16.4 13.5 %collective-permute-start.2 = (bf16[192,1024]{1,0:T(8,128)(2,1)}, bf16[192,1024]{1,0:T(8,128)(2,1)}, u32[]{:S(2)}, u32[]{:S(2)}) collective-permute-start(bf16[192,1024]{1,0:T(8,128)(2,1)} %collective-permute-done.1), channel_id=1, source_target_pairs={{0,4},{4,0},{8,12},{12,8},{16,20},{20,16},{24,28},{28,24},{1,5},{5... | collective-permute-start | bytes 1179656 | tf_op jit(solution)/shard_map/ppermute | solution.py:69
  16.9 11.7 %collective-permute-start.3 = (bf16[192,1024]{1,0:T(8,128)(2,1)}, bf16[192,1024]{1,0:T(8,128)(2,1)S(1)}, u32[]{:S(2)}, u32[]{:S(2)}) collective-permute-start(bf16[192,1024]{1,0:T(8,128)(2,1)} %collective-permute-done.1), channel_id=1, source_target_pairs={{0,8},{4,12},{8,16},{12,20},{16,24},{20,28},{24,0},{28,4},{1,9},{5... | collective-permute-start | bytes 1179656 | tf_op jit(solution)/shard_map/ppermute | solution.py:74
  28.7 8.9 %collective-permute-start.4 = (bf16[192,1024]{1,0:T(8,128)(2,1)S(1)}, bf16[192,1024]{1,0:T(8,128)(2,1)}, u32[]{:S(2)}, u32[]{:S(2)}) collective-permute-start(bf16[192,1024]{1,0:T(8,128)(2,1)S(1)} %collective-permute-done.3), channel_id=1, source_target_pairs={{0,4},{4,0},{8,12},{12,8},{16,20},{20,16},{24,28},{28,24},{1,5},{5... | collective-permute-start | bytes 1179656 | tf_op jit(solution)/shard_map/ppermute | solution.py:69
  29.9 10.6 %collective-permute-start.5 = (bf16[192,1024]{1,0:T(8,128)(2,1)S(1)}, bf16[192,1024]{1,0:T(8,128)(2,1)}, u32[]{:S(2)}, u32[]{:S(2)}) collective-permute-start(bf16[192,1024]{1,0:T(8,128)(2,1)S(1)} %collective-permute-done.3), channel_id=1, source_target_pairs={{0,8},{4,12},{8,16},{12,20},{16,24},{20,28},{24,0},{28,4},{1,9},{5... | collective-permute-start | bytes 1179656 | tf_op jit(solution)/shard_map/ppermute | solution.py:74
  40.5 8.7 %collective-permute-start.6 = (bf16[192,1024]{1,0:T(8,128)(2,1)}, bf16[192,1024]{1,0:T(8,128)(2,1)S(1)}, u32[]{:S(2)}, u32[]{:S(2)}) collective-permute-start(bf16[192,1024]{1,0:T(8,128)(2,1)} %collective-permute-done.5), channel_id=1, source_target_pairs={{0,4},{4,0},{8,12},{12,8},{16,20},{20,16},{24,28},{28,24},{1,5},{5... | collective-permute-start | bytes 1179656 | tf_op jit(solution)/shard_map/ppermute | solution.py:69
  43.7 2.0 %copy-start = (bf16[4,2,192,1024]{3,2,1,0:T(8,128)(2,1)}, bf16[4,2,192,1024]{3,2,1,0:T(8,128)(2,1)S(1)}, u32[]{:S(2)}) copy-start(bf16[4,2,192,1024]{3,2,1,0:T(8,128)(2,1)S(1)} %bitcast_dynamic-update-slice_fusion.1) | copy-start | bytes 9437188
  49.2 28.9 %collective-permute-start.10 = (bf16[2,384,2048]{2,1,0:T(8,128)(2,1)S(1)}, bf16[2,384,2048]{2,1,0:T(8,128)(2,1)}, u32[]{:S(2)}, u32[]{:S(2)}) collective-permute-start(bf16[2,384,2048]{2,1,0:T(8,128)(2,1)S(1)} %fusion.1), channel_id=1, source_target_pairs={{0,1},{1,0},{2,3},{3,2},{4,5},{5,4},{6,7},{7,6},{8,9},{9,8},{10,11... | collective-permute-start | bytes 9437192 | tf_op jit(solution)/shard_map/ppermute | solution.py:100
  52.7 3.2 %copy-start.2 = (bf16[2048,1024]{1,0:T(8,128)(2,1)S(1)}, bf16[2048,1024]{1,0:T(8,128)(2,1)}, u32[]{:S(2)}) copy-start(bf16[2048,1024]{1,0:T(8,128)(2,1)} %param.5) | copy-start | bytes 12582916
  55.9 2.0 %copy-start.6 = (bf16[384,1024]{1,0:T(8,128)(2,1)}, bf16[384,1024]{1,0:T(8,128)(2,1)S(1)}, u32[]{:S(2)}) copy-start(bf16[384,1024]{1,0:T(8,128)(2,1)S(1)} %get-tuple-element.11) | copy-start | bytes 2359300
  55.9 9.1 %copy-start.7 = (bf16[384,1024]{1,0:T(8,128)(2,1)}, bf16[384,1024]{1,0:T(8,128)(2,1)S(1)}, u32[]{:S(2)}) copy-start(bf16[384,1024]{1,0:T(8,128)(2,1)S(1)} %get-tuple-element.12) | copy-start | bytes 2359300
  55.9 20.7 %copy-start.8 = (bf16[384,1024]{1,0:T(8,128)(2,1)}, bf16[384,1024]{1,0:T(8,128)(2,1)S(1)}, u32[]{:S(2)}) copy-start(bf16[384,1024]{1,0:T(8,128)(2,1)S(1)} %get-tuple-element.13) | copy-start | bytes 2359300
  57.2 18.9 %collective-permute-start.7 = (f16[384,512]{1,0:T(8,128)(2,1)S(1)}, f16[384,512]{1,0:T(8,128)(2,1)S(1)}, u32[]{:S(2)}, u32[]{:S(2)}) collective-permute-start(f16[384,512]{1,0:T(8,128)(2,1)S(1)} %fusion.27), channel_id=1, source_target_pairs={{0,1},{1,0},{2,3},{3,2},{4,5},{5,4},{6,7},{7,6},{8,9},{9,8},{10,11... | collective-permute-start | bytes 1179656 | tf_op jit(solution)/shard_map/ppermute | solution.py:94
  57.8 5.7 %collective-permute-start.8 = (f32[8,128]{1,0:T(8,128)S(1)}, f32[8,128]{1,0:T(8,128)S(1)}, u32[]{:S(2)}, u32[]{:S(2)}) collective-permute-start(f32[8,128]{1,0:T(8,128)S(1)} %broadcast_in_dim.39), channel_id=1, source_target_pairs={{0,1},{1,0},{2,3},{3,2},{4,5},{5,4},{6,7},{7,6},{8,9},{9,8},{10,11... | collective-permute-start | bytes 12296 | tf_op jit(solution)/shard_map/ppermute | solution.py:78
  62.9 6.5 %collective-permute-start.12 = (f16[384,512]{1,0:T(8,128)(2,1)S(1)}, f16[384,512]{1,0:T(8,128)(2,1)S(1)}, u32[]{:S(2)}, u32[]{:S(2)}) collective-permute-start(f16[384,512]{1,0:T(8,128)(2,1)S(1)} %fusion.28), channel_id=1, source_target_pairs={{0,1},{1,0},{2,3},{3,2},{4,5},{5,4},{6,7},{7,6},{8,9},{9,8},{10,11... | collective-permute-start | bytes 1179656 | tf_op jit(solution)/shard_map/ppermute | solution.py:94
  63.4 7.9 %collective-permute-start.17 = (f16[384,512]{1,0:T(8,128)(2,1)S(1)}, f16[384,512]{1,0:T(8,128)(2,1)S(1)}, u32[]{:S(2)}, u32[]{:S(2)}) collective-permute-start(f16[384,512]{1,0:T(8,128)(2,1)S(1)} %fusion.30), channel_id=1, source_target_pairs={{0,1},{1,0},{2,3},{3,2},{4,5},{5,4},{6,7},{7,6},{8,9},{9,8},{10,11... | collective-permute-start | bytes 1179656 | tf_op jit(solution)/shard_map/ppermute | solution.py:94
  63.5 4.6 %collective-permute-start.14 = (f32[8,128]{1,0:T(8,128)S(1)}, f32[8,128]{1,0:T(8,128)S(1)}, u32[]{:S(2)}, u32[]{:S(2)}) collective-permute-start(f32[8,128]{1,0:T(8,128)S(1)} %broadcast_add_fusion), channel_id=1, source_target_pairs={{0,2},{1,3},{2,0},{3,1},{4,6},{5,7},{6,4},{7,5},{8,10},{9,11},{10,... | collective-permute-start | bytes 12296 | tf_op jit(solution)/shard_map/ppermute | solution.py:80
  68.1 30.3 %collective-permute-start.11 = (f16[384,2048]{1,0:T(8,128)(2,1)}, f16[384,2048]{1,0:T(8,128)(2,1)}, u32[]{:S(2)}, u32[]{:S(2)}) collective-permute-start(f16[384,2048]{1,0:T(8,128)(2,1)} %multiply_convert_fusion), channel_id=1, source_target_pairs={{0,1},{1,0},{2,3},{3,2},{4,5},{5,4},{6,7},{7,6},{8,9},{9,8},{10,11... | collective-permute-start | bytes 4718600 | tf_op jit(solution)/shard_map/ppermute | solution.py:103
  69.5 3.8 %collective-permute-start.15 = (f16[384,512]{1,0:T(8,128)(2,1)S(1)}, f16[384,512]{1,0:T(8,128)(2,1)S(1)}, u32[]{:S(2)}, u32[]{:S(2)}) collective-permute-start(f16[384,512]{1,0:T(8,128)(2,1)S(1)} %fusion.29), channel_id=1, source_target_pairs={{0,1},{1,0},{2,3},{3,2},{4,5},{5,4},{6,7},{7,6},{8,9},{9,8},{10,11... | collective-permute-start | bytes 1179656 | tf_op jit(solution)/shard_map/ppermute | solution.py:94
  71.3 30.3 %collective-permute-start.13 = (f16[384,512]{1,0:T(8,128)(2,1)}, f16[384,512]{1,0:T(8,128)(2,1)}, u32[]{:S(2)}, u32[]{:S(2)}) collective-permute-start(f16[384,512]{1,0:T(8,128)(2,1)} %multiply_convert_fusion.3), channel_id=1, source_target_pairs={{0,2},{1,3},{2,0},{3,1},{4,6},{5,7},{6,4},{7,5},{8,10},{9,11},{10,... | collective-permute-start | bytes 1179656 | tf_op jit(solution)/shard_map/ppermute | solution.py:97
  73.2 28.4 %collective-permute-start.18 = (f16[384,512]{1,0:T(8,128)(2,1)}, f16[384,512]{1,0:T(8,128)(2,1)}, u32[]{:S(2)}, u32[]{:S(2)}) collective-permute-start(f16[384,512]{1,0:T(8,128)(2,1)} %multiply_convert_fusion.1), channel_id=1, source_target_pairs={{0,2},{1,3},{2,0},{3,1},{4,6},{5,7},{6,4},{7,5},{8,10},{9,11},{10,... | collective-permute-start | bytes 1179656 | tf_op jit(solution)/shard_map/ppermute | solution.py:97
  76.2 25.5 %collective-permute-start.16 = (f16[384,512]{1,0:T(8,128)(2,1)}, f16[384,512]{1,0:T(8,128)(2,1)}, u32[]{:S(2)}, u32[]{:S(2)}) collective-permute-start(f16[384,512]{1,0:T(8,128)(2,1)} %multiply_convert_fusion.2), channel_id=1, source_target_pairs={{0,2},{1,3},{2,0},{3,1},{4,6},{5,7},{6,4},{7,5},{8,10},{9,11},{10,... | collective-permute-start | bytes 1179656 | tf_op jit(solution)/shard_map/ppermute | solution.py:97
  78.1 3.6 %copy-start.4 = (bf16[384,2048]{1,0:T(8,128)(2,1)S(1)}, bf16[384,2048]{1,0:T(8,128)(2,1)}, u32[]{:S(2)}) copy-start(bf16[384,2048]{1,0:T(8,128)(2,1)} %get-tuple-element.15) | copy-start | bytes 4718596
  78.1 3.6 %copy-start.5 = (bf16[384,1024]{1,0:T(8,128)(2,1)S(1)}, bf16[384,1024]{1,0:T(8,128)(2,1)}, u32[]{:S(2)}) copy-start(bf16[384,1024]{1,0:T(8,128)(2,1)} %get-tuple-element.10) | copy-start | bytes 2359300
  96.8 11.1 %copy-start.1 = (f32[384,2048]{1,0:T(8,128)S(1)}, f32[384,2048]{1,0:T(8,128)}, u32[]{:S(2)}) copy-start(f32[384,2048]{1,0:T(8,128)} %fusion.17) | copy-start | bytes 9437188
  96.8 11.1 %collective-permute-start.19 = (f16[384,512]{1,0:T(8,128)(2,1)}, f16[384,512]{1,0:T(8,128)(2,1)S(1)}, u32[]{:S(2)}, u32[]{:S(2)}) collective-permute-start(f16[384,512]{1,0:T(8,128)(2,1)} %multiply_convert_fusion.4), channel_id=1, source_target_pairs={{0,2},{1,3},{2,0},{3,1},{4,6},{5,7},{6,4},{7,5},{8,10},{9,11},{10,... | collective-permute-start | bytes 1179656 | tf_op jit(solution)/shard_map/ppermute | solution.py:114

commit v3 on v2

--- a/solution.py
+++ b/solution.py
@@ -62,17 +62,21 @@
     w_top = top(w_down)
     g_top = top(grad_out)
 
+    act_near = gelu_value(pre_act.astype(jnp.float32)).astype(jnp.bfloat16)
+    act_near_sib = lax.ppermute(act_near, "col", over_core)
+
     shard = grad_out
     piece = jnp.zeros((4, 2, rows, feats), jnp.bfloat16)
     for k in range(4):
         zk = (z + 4 - k) % 4
+        place = jnp.where(zk // 2 == y, 2, 0) + jnp.where(zk % 2 == core, 1, 0)
         other = lax.ppermute(shard, "row", over_x)
-        piece = lax.dynamic_update_slice(piece, shard[None, None], (zk, x, 0, 0))
-        piece = lax.dynamic_update_slice(piece, other[None, None], (zk, 1 - x, 0, 0))
+        piece = lax.dynamic_update_slice(piece, shard[None, None], (place, x, 0, 0))
+        piece = lax.dynamic_update_slice(piece, other[None, None], (place, 1 - x, 0, 0))
         g_top = jnp.maximum(g_top, jnp.maximum(top(shard), top(other)))
         if k < 3:
             shard = lax.ppermute(shard, "row", next_z)
-    piece = piece.reshape(4, 2 * rows, feats)
+    piece = piece.reshape(4 * tokens, feats)
 
     bound = jnp.full((8, 128), jnp.maximum(feats * g_top * w_top, 1e-30))
     bound_sib = lax.ppermute(bound, "col", over_core)
@@ -81,11 +85,8 @@
     scale, from_sib = F16_TOP / bound[0, 0], bound_sib[0, 0] / F16_TOP
     to_far, from_far = F16_TOP / bound_pair[0, 0], bound_far[0, 0] / F16_TOP
 
-    def block_of(b):
-        return lax.dynamic_index_in_dim(piece, b, 0, keepdims=False)
-
-    far_mine, far_sib = block_of(2 * (1 - y) + core), block_of(2 * (1 - y) + 1 - core)
-    near_mine, near_sib = block_of(2 * y + core), block_of(2 * y + 1 - core)
+    far_sib, far_mine = piece[:tokens], piece[tokens:2 * tokens]
+    near_sib, near_mine = piece[2 * tokens:3 * tokens], piece[3 * tokens:]
     width = hidden // CHUNKS
     pairs = []
     for j in range(CHUNKS):
@@ -96,17 +97,17 @@
         pairs.append((pair * to_far).astype(jnp.float16))
     arrived = [lax.ppermute(pair, "col", over_y) for pair in pairs[:-1]]
 
-    act = gelu_value(jnp.stack([pre_act, pre_far]).astype(jnp.float32)).astype(jnp.bfloat16)
-    act_sib = lax.ppermute(act, "col", over_core)
+    act_far = gelu_value(pre_far.astype(jnp.float32)).astype(jnp.bfloat16)
+    act_far, near_sib, _ = lax.optimization_barrier((act_far, near_sib, pairs[1]))
+    act_far_sib = lax.ppermute(act_far, "col", over_core)
 
     near_out = (matmul_t(near_sib, w_down) * scale).astype(jnp.float16)
     near_back = lax.ppermute(near_out, "col", over_core)
     near = matmul_t(near_mine, w_down) + near_back.astype(jnp.float32) * from_sib
 
-    act_full = jnp.concatenate([act[0], act[1], act_sib[0], act_sib[1]], axis=0)
-    piece_full = jnp.concatenate([near_mine, far_mine, near_sib, far_sib], axis=0)
+    act_full = jnp.concatenate([act_far_sib, act_far, act_near_sib, act_near], axis=0)
     grad_w = lax.dot_general(
-        act_full, piece_full, (((0,), (0,)), ((), ())), preferred_element_type=jnp.float32
+        act_full, piece, (((0,), (0,)), ((), ())), preferred_element_type=jnp.float32
     )
     acc_new = acc_down + grad_w * float(total) ** (-0.5)
 
@@ -117,8 +118,11 @@
     parts = []
     for j in range(CHUNKS):
         cut = slice(j * width, (j + 1) * width)
-        both = near[:, cut] + arrived[j].astype(jnp.float32) * from_far
-        parts.append((both * slope[:, cut]).astype(jnp.bfloat16))
+        mine, factor, there = near[:, cut], slope[:, cut], arrived[j]
+        if j == CHUNKS - 1:
+            mine, factor, there, *parts = lax.optimization_barrier((mine, factor, there, *parts))
+        both = mine + there.astype(jnp.float32) * from_far
+        parts.append((both * factor).astype(jnp.bfloat16))
     return (acc_new, jnp.concatenate(parts, axis=1))
 
 

time: 112 us -> 107 us (0.955)
  waiting for transfers between devices: 15.1 us -> 27.3 us
  matrix products: 29.7 us -> 20.4 us
  local copies, waits for them, and re-layouts: 16.1 us -> 11 us
  starting transfers between devices: 16.9 us -> 15.2 us
  other arithmetic: 25.1 us -> 23.6 us
    squeeze x3 -> x0, local copies, waits for them, and re-layouts: 8.14 us -> none  [the longest x2 4.92 us: on_device_paired(): act_full = jnp.concatenate([act[0], act[1], act_sib[0], act_sib[1]], axis=0)]
    ppermute x3, waiting for transfers between devices: 0.01 us -> 7.09 us  [on_device_paired(): arrived = [lax.ppermute(pair, 'col', over_y) for pair in pairs[:-1]]]
    dot_general x10, matrix products: 14.5 us -> 8.56 us  [matmul_t(): lax.dot_general(a, b, (((1,), (1,)), ((), ())), preferred_element_type=jn...]
    ppermute x3, waiting for transfers between devices: 5.79 us -> 11 us  [on_device_paired(): shard = lax.ppermute(shard, 'row', next_z)]
    dot_general x1, matrix products: 15.2 us -> 11.8 us  [on_device_paired(): lax.dot_general(act_full, piece, (((0,), (0,)), ((), ())), preferred_elem...]
    convert_element_type x2 -> x3, other arithmetic: 5.77 us -> 3.06 us  [the longest x1 1.83 us: on_device_paired(): act_far = gelu_value(pre_far.astype(jnp.float32)).astype(jnp.bfloat16)]
    unnamed x18 -> x6, local copies, waits for them, and re-layouts: 0.04 us -> 2.31 us
    ppermute x3, starting transfers between devices: 2.54 us -> 4.24 us  [on_device_paired(): arrived = [lax.ppermute(pair, 'col', over_y) for pair in pairs[:-1]]]
  transfers between devices with their start and end apart: 20 -> 21, of which waited for: 4 -> 7; matrix products, arithmetic and copies ran while one was open for 60% -> 48% of each run, Pallas kernels for 0% -> 0%
where the time goes in v3:
time: 107 us; the launch traced here: 106 us
  waiting for transfers between devices  27.3 us (26%)
  other arithmetic  23.6 us (22%)
  matrix products  20.4 us (19%)
  starting transfers between devices  15.2 us (14%)
  local copies, waits for them, and re-layouts  11 us (10%)
  between operations  8.76 us (8%)
    reduce_max x9, other arithmetic, top(): return jnp.max(jnp.abs(v)).astype(jnp.float32)  15.1 us
    dot_general x1, matrix products, on_device_paired(): lax.dot_general(act_full, piece, (((0,), (0,)), ((), ())), preferred_elem...  11.8 us
    ppermute x3, waiting for transfers between devices, on_device_paired(): shard = lax.ppermute(shard, 'row', next_z)  11 us
    dot_general x10, matrix products, matmul_t(): lax.dot_general(a, b, (((1,), (1,)), ((), ())), preferred_element_type=jn...  8.56 us
    ppermute x3, waiting for transfers between devices, on_device_paired(): arrived = [lax.ppermute(pair, 'col', over_y) for pair in pairs[:-1]]  7.09 us
    ppermute x1, waiting for transfers between devices, on_device_paired(): arrived.append(lax.ppermute(last, 'col', over_y))  6.85 us
    ppermute x4, starting transfers between devices, on_device_paired(): other = lax.ppermute(shard, 'row', over_x)  4.61 us
    ppermute x3, starting transfers between devices, on_device_paired(): arrived = [lax.ppermute(pair, 'col', over_y) for pair in pairs[:-1]]  4.24 us
  transfers between devices with their start and end apart: 21, of which 7 were waited for; matrix products, arithmetic and copies ran while one was open for 48% of the time, Pallas kernels for 0%

profile of v3, /device:TPU:0, one launch (start us, length us, event | category | flops | bytes accessed | tf_op | source)
XLA Modules:
  0.0 106.2 jit_solution(14590499334027972855)
XLA Ops:
  0.6 3.0 %collective-permute-start = (bf16[192,1024]{1,0:T(8,128)(2,1)}, bf16[192,1024]{1,0:T(8,128)(2,1)}, u32[]{:S(2)}, u32[]{:S(2)}) collective-permute-start(bf16[192,1024]{1,0:T(8,128)(2,1)} %param.4), channel_id=1, source_target_pairs={{0,4},{4,0},{8,12},{12,8},{16,20},{20,16},{24,28},{28,24},{1,5},{5... | collective-permute-start | bytes 1179656 | tf_op jit(solution)/shard_map/ppermute | solution.py:73
  3.6 1.6 %collective-permute-start.1 = (bf16[192,1024]{1,0:T(8,128)(2,1)}, bf16[192,1024]{1,0:T(8,128)(2,1)}, u32[]{:S(2)}, u32[]{:S(2)}) collective-permute-start(bf16[192,1024]{1,0:T(8,128)(2,1)} %param.4), channel_id=1, source_target_pairs={{0,8},{4,12},{8,16},{12,20},{16,24},{20,28},{24,0},{28,4},{1,9},{5... | collective-permute-start | bytes 1179656 | tf_op jit(solution)/shard_map/ppermute | solution.py:78
  5.2 1.5 %collective-permute-start.9 = (bf16[384,2048]{1,0:T(8,128)(2,1)}, bf16[384,2048]{1,0:T(8,128)(2,1)}, u32[]{:S(2)}, u32[]{:S(2)}) collective-permute-start(bf16[384,2048]{1,0:T(8,128)(2,1)} %param.6), channel_id=1, source_target_pairs={{0,2},{1,3},{2,0},{3,1},{4,6},{5,7},{6,4},{7,5},{8,10},{9,11},{10,... | collective-permute-start | bytes 4718600 | tf_op jit(solution)/shard_map/ppermute | solution.py:57
  6.7 4.1 %fusion.20 = (f32[384,2048]{1,0:T(8,128)}, bf16[384,2048]{1,0:T(8,128)(2,1)}) fusion(bf16[384,2048]{1,0:T(8,128)(2,1)} %param.6), kind=kLoop, calls=%fused_computation.27 | loop fusion | flops 9437184 | bytes 6291456 | tf_op jit(solution)/shard_map/add | solution.py:17
  11.9 0.7 abs_reduce_fusion.8
  12.5 3.8 %abs_reduce_fusion = bf16[]{:T(256)} fusion(bf16[2048,1024]{1,0:T(8,128)(2,1)} %param.5), kind=kLoop, calls=%fused_computation.14 | loop fusion | flops 4194303 | bytes 4194306 | tf_op jit(solution)/shard_map/reduce_max | solution.py:60
  16.4 1.5 %collective-permute-start.3 = (bf16[192,1024]{1,0:T(8,128)(2,1)}, bf16[192,1024]{1,0:T(8,128)(2,1)S(1)}, u32[]{:S(2)}, u32[]{:S(2)}) collective-permute-start(bf16[192,1024]{1,0:T(8,128)(2,1)} %collective-permute-done.1), channel_id=1, source_target_pairs={{0,8},{4,12},{8,16},{12,20},{16,24},{20,28},{24,0},{28,4},{1,9},{5... | collective-permute-start | bytes 1179656 | tf_op jit(solution)/shard_map/ppermute | solution.py:78
  18.4 1.0 bitcast_dynamic-update-slice_fusion.6
  19.5 1.7 %abs_reduce_fusion.7 = bf16[]{:T(256)} fusion(bf16[192,1024]{1,0:T(8,128)(2,1)} %collective-permute-done), kind=kLoop, calls=%fused_computation.83 | loop fusion | flops 393215 | bytes 393218 | tf_op jit(solution)/shard_map/reduce_max | solution.py:60
  22.3 1.7 %abs_reduce_fusion.6 = bf16[]{:T(256)} fusion(bf16[192,1024]{1,0:T(8,128)(2,1)} %collective-permute-done.1), kind=kLoop, calls=%fused_computation.82 | loop fusion | flops 393215 | bytes 393218 | tf_op jit(solution)/shard_map/reduce_max | solution.py:60
  24.0 1.0 bitcast_dynamic-update-slice_fusion.5
  25.0 4.2 %collective-permute-done.3 = bf16[192,1024]{1,0:T(8,128)(2,1)S(1)} collective-permute-done((bf16[192,1024]{1,0:T(8,128)(2,1)}, bf16[192,1024]{1,0:T(8,128)(2,1)S(1)}, u32[]{:S(2)}, u32[]{:S(2)}) %collective-permute-start.3) | collective-permute-done | bytes 393248 | tf_op jit(solution)/shard_map/ppermute | solution.py:78
  29.3 0.5 collective-permute-start.4
  29.8 1.0 bitcast_dynamic-update-slice_fusion.4
  30.8 1.7 %abs_reduce_fusion.5 = bf16[]{:T(256)} fusion(bf16[192,1024]{1,0:T(8,128)(2,1)} %collective-permute-done.2), kind=kLoop, calls=%fused_computation.81 | loop fusion | flops 393215 | bytes 393218 | tf_op jit(solution)/shard_map/reduce_max | solution.py:60
  33.8 0.7 abs_reduce_fusion.4
  34.5 6.6 %collective-permute-done.5 = bf16[192,1024]{1,0:T(8,128)(2,1)} collective-permute-done((bf16[192,1024]{1,0:T(8,128)(2,1)S(1)}, bf16[192,1024]{1,0:T(8,128)(2,1)}, u32[]{:S(2)}, u32[]{:S(2)}) %collective-permute-start.5) | collective-permute-done | bytes 393248 | tf_op jit(solution)/shard_map/ppermute | solution.py:78
  41.1 0.5 collective-permute-start.6
  41.7 1.0 bitcast_dynamic-update-slice_fusion.2
  42.7 1.7 %abs_reduce_fusion.2 = bf16[]{:T(256)} fusion(bf16[192,1024]{1,0:T(8,128)(2,1)} %collective-permute-done.5), kind=kLoop, calls=%fused_computation.78 | loop fusion | flops 393215 | bytes 393218 | tf_op jit(solution)/shard_map/reduce_max | solution.py:60
  44.4 1.0 bitcast_dynamic-update-slice_fusion.1
  45.4 1.7 %abs_reduce_fusion.3 = bf16[]{:T(256)} fusion(bf16[192,1024]{1,0:T(8,128)(2,1)} %collective-permute-done.4), kind=kLoop, calls=%fused_computation.79 | loop fusion | flops 393215 | bytes 393218 | tf_op jit(solution)/shard_map/reduce_max | solution.py:60
  48.3 2.2 %collective-permute-done.6 = bf16[192,1024]{1,0:T(8,128)(2,1)} collective-permute-done((bf16[192,1024]{1,0:T(8,128)(2,1)}, bf16[192,1024]{1,0:T(8,128)(2,1)}, u32[]{:S(2)}, u32[]{:S(2)}) %collective-permute-start.6) | collective-permute-done | bytes 393248 | tf_op jit(solution)/shard_map/ppermute | solution.py:73
  50.5 1.7 %abs_reduce_fusion.1 = bf16[]{:T(256)} fusion(bf16[192,1024]{1,0:T(8,128)(2,1)} %collective-permute-done.6), kind=kLoop, calls=%fused_computation.77 | loop fusion | flops 393215 | bytes 393218 | tf_op jit(solution)/shard_map/reduce_max | solution.py:60
  54.2 1.0 bitcast_dynamic-update-slice_fusion
  55.6 1.8 %copy-done.1 = bf16[2048,1024]{1,0:T(8,128)(2,1)S(1)} copy-done((bf16[2048,1024]{1,0:T(8,128)(2,1)S(1)}, bf16[2048,1024]{1,0:T(8,128)(2,1)}, u32[]{:S(2)}) %copy-start.1) | copy-done | bytes 4194328
  57.4 0.6 fusion.30
  58.0 0.6 collective-permute-start.10
  58.6 0.6 fusion.31
  59.3 0.6 fusion.32
  59.9 0.6 collective-permute-start.19
  60.5 1.8 %fusion.11 = bf16[384,2048]{1,0:T(8,128)(2,1)S(1)} fusion(bf16[384,2048]{1,0:T(8,128)(2,1)} %collective-permute-done.9), kind=kLoop, calls=%fused_computation.18 | loop fusion | flops 4718592 | bytes 3145728 | tf_op jit(solution)/shard_map/convert_element_type | solution.py:100
  62.3 0.6 slice.76
  64.8 0.6 fusion.27
  65.7 0.6 fusion.29
  66.7 0.6 slice.86
  68.0 2.1 %collective-permute-start.18 = (f16[384,512]{1,0:T(8,128)(2,1)S(1)}, f16[384,512]{1,0:T(8,128)(2,1)S(1)}, u32[]{:S(2)}, u32[]{:S(2)}) collective-permute-start(f16[384,512]{1,0:T(8,128)(2,1)S(1)} %fusion.27), channel_id=1, source_target_pairs={{0,2},{1,3},{2,0},{3,1},{4,6},{5,7},{6,4},{7,5},{8,10},{9,11},{10,... | collective-permute-start | bytes 1179656 | tf_op jit(solution)/shard_map/ppermute | solution.py:98
  70.0 0.6 fusion.26
  70.8 0.6 fusion.25
  71.4 2.1 %collective-permute-start.20 = (f16[384,512]{1,0:T(8,128)(2,1)S(1)}, f16[384,512]{1,0:T(8,128)(2,1)S(1)}, u32[]{:S(2)}, u32[]{:S(2)}) collective-permute-start(f16[384,512]{1,0:T(8,128)(2,1)S(1)} %fusion.25), channel_id=1, source_target_pairs={{0,2},{1,3},{2,0},{3,1},{4,6},{5,7},{6,4},{7,5},{8,10},{9,11},{10,... | collective-permute-start | bytes 1179656 | tf_op jit(solution)/shard_map/ppermute | solution.py:98
  73.5 0.6 fusion.28
  74.1 1.8 %multiply_convert_fusion = f16[384,2048]{1,0:T(8,128)(2,1)S(1)} fusion(bf16[384,1024]{1,0:T(8,128)(2,1)S(1)} %bitcast.39, bf16[2048,1024]{1,0:T(8,128)(2,1)S(1)} %copy-done.1, f32[]{:T(128)S(6)} %div.93), kind=kOutput, calls=%fused_computation.29 | convolution fusion | flops 1612185600 | bytes 6553604 | tf_op jit(solution)/shard_map/dot_general | solution.py:41
  76.0 11.8 %multiply_add_fusion = f32[2048,1024]{1,0:T(8,128)} fusion(f32[2048,1024]{1,0:T(8,128)} %param.7, bf16[1536,1024]{1,0:T(8,128)(2,1)S(1)} %bitcast.37, bf16[384,2048]{1,0:T(8,128)(2,1)} %get-tuple-element.32, bf16[384,2048]{1,0:T(8,128)(2,1)} %collective-permute-done.12, bf16[384,2048]{1,0:T(8,128)(2,1)S(1)} %fusion.11, ...), kind=kOutput, calls=%fused_computation | convolution fusion | flops 6471811072 | bytes 26214400 | tf_op jit(solution)/shard_map/dot_general | solution.py:109
  87.9 1.8 %multiply_add_fusion.1 = f32[384,2048]{1,0:T(8,128)S(1)} fusion(f16[384,2048]{1,0:T(8,128)(2,1)S(1)} %collective-permute-done.13, bf16[384,1024]{1,0:T(8,128)(2,1)S(1)} %bitcast.38, bf16[2048,1024]{1,0:T(8,128)(2,1)S(1)} %copy-done.1, f32[]{:T(128)} %bitcast.10), kind=kOutput, calls=%fused_computation.28 | convolution fusion | flops 1612972032 | bytes 9699332 | tf_op jit(solution)/shard_map/dot_general | solution.py:41
  89.7 7.1 %collective-permute-done.20 = f16[384,512]{1,0:T(8,128)(2,1)S(1)} collective-permute-done((f16[384,512]{1,0:T(8,128)(2,1)S(1)}, f16[384,512]{1,0:T(8,128)(2,1)S(1)}, u32[]{:S(2)}, u32[]{:S(2)}) %collective-permute-start.20) | collective-permute-done | bytes 393248 | tf_op jit(solution)/shard_map/ppermute | solution.py:98
  96.8 1.0 fusion.41
  97.8 6.9 %collective-permute-done.14 = f16[384,512]{1,0:T(8,128)(2,1)S(1)} collective-permute-done((f16[384,512]{1,0:T(8,128)(2,1)S(1)}, f16[384,512]{1,0:T(8,128)(2,1)S(1)}, u32[]{:S(2)}, u32[]{:S(2)}) %collective-permute-start.14) | collective-permute-done | bytes 393248 | tf_op jit(solution)/shard_map/ppermute | solution.py:115
  104.9 1.3 %pad_maximum_fusion = bf16[384,2048]{1,0:T(8,128)(2,1)} fusion(bf16[384,512]{1,0:T(8,128)(2,1)S(1)} %multiply_convert_fusion.1, bf16[384,512]{1,0:T(8,128)(2,1)S(1)} %get-tuple-element.18, bf16[384,512]{1,0:T(8,128)(2,1)S(1)} %get-tuple-element.17, bf16[384,512]{1,0:T(8,128)(2,1)S(1)} %get-tuple-element.16), kind=kLoop, calls=%fused_computation.30 | loop fusion | flops 6291456 | bytes 3145728 | tf_op jit(solution)/shard_map/concatenate | solution.py:126
  (40 shorter events, 3.8 us)
Async XLA Ops:
  0.6 17.8 %collective-permute-start = (bf16[192,1024]{1,0:T(8,128)(2,1)}, bf16[192,1024]{1,0:T(8,128)(2,1)}, u32[]{:S(2)}, u32[]{:S(2)}) collective-permute-start(bf16[192,1024]{1,0:T(8,128)(2,1)} %param.4), channel_id=1, source_target_pairs={{0,4},{4,0},{8,12},{12,8},{16,20},{20,16},{24,28},{28,24},{1,5},{5... | collective-permute-start | bytes 1179656 | tf_op jit(solution)/shard_map/ppermute | solution.py:73
  3.6 12.8 %collective-permute-start.1 = (bf16[192,1024]{1,0:T(8,128)(2,1)}, bf16[192,1024]{1,0:T(8,128)(2,1)}, u32[]{:S(2)}, u32[]{:S(2)}) collective-permute-start(bf16[192,1024]{1,0:T(8,128)(2,1)} %param.4), channel_id=1, source_target_pairs={{0,8},{4,12},{8,16},{12,20},{16,24},{20,28},{24,0},{28,4},{1,9},{5... | collective-permute-start | bytes 1179656 | tf_op jit(solution)/shard_map/ppermute | solution.py:78
  5.2 54.7 %collective-permute-start.9 = (bf16[384,2048]{1,0:T(8,128)(2,1)}, bf16[384,2048]{1,0:T(8,128)(2,1)}, u32[]{:S(2)}, u32[]{:S(2)}) collective-permute-start(bf16[384,2048]{1,0:T(8,128)(2,1)} %param.6), channel_id=1, source_target_pairs={{0,2},{1,3},{2,0},{3,1},{4,6},{5,7},{6,4},{7,5},{8,10},{9,11},{10,... | collective-permute-start | bytes 4718600 | tf_op jit(solution)/shard_map/ppermute | solution.py:57
  10.8 1.0 copy-start.2
  10.8 65.1 %collective-permute-start.12 = (bf16[384,2048]{1,0:T(8,128)(2,1)}, bf16[384,2048]{1,0:T(8,128)(2,1)}, u32[]{:S(2)}, u32[]{:S(2)}) collective-permute-start(bf16[384,2048]{1,0:T(8,128)(2,1)} %get-tuple-element.32), channel_id=1, source_target_pairs={{0,1},{1,0},{2,3},{3,2},{4,5},{5,4},{6,7},{7,6},{8,9},{9,8},{10,11... | collective-permute-start | bytes 4718600 | tf_op jit(solution)/shard_map/ppermute | solution.py:66
  16.4 12.8 %collective-permute-start.3 = (bf16[192,1024]{1,0:T(8,128)(2,1)}, bf16[192,1024]{1,0:T(8,128)(2,1)S(1)}, u32[]{:S(2)}, u32[]{:S(2)}) collective-permute-start(bf16[192,1024]{1,0:T(8,128)(2,1)} %collective-permute-done.1), channel_id=1, source_target_pairs={{0,8},{4,12},{8,16},{12,20},{16,24},{20,28},{24,0},{28,4},{1,9},{5... | collective-permute-start | bytes 1179656 | tf_op jit(solution)/shard_map/ppermute | solution.py:78
  17.9 11.9 %collective-permute-start.2 = (bf16[192,1024]{1,0:T(8,128)(2,1)}, bf16[192,1024]{1,0:T(8,128)(2,1)}, u32[]{:S(2)}, u32[]{:S(2)}) collective-permute-start(bf16[192,1024]{1,0:T(8,128)(2,1)} %collective-permute-done.1), channel_id=1, source_target_pairs={{0,4},{4,0},{8,12},{12,8},{16,20},{20,16},{24,28},{28,24},{1,5},{5... | collective-permute-start | bytes 1179656 | tf_op jit(solution)/shard_map/ppermute | solution.py:73
  29.3 11.9 %collective-permute-start.5 = (bf16[192,1024]{1,0:T(8,128)(2,1)S(1)}, bf16[192,1024]{1,0:T(8,128)(2,1)}, u32[]{:S(2)}, u32[]{:S(2)}) collective-permute-start(bf16[192,1024]{1,0:T(8,128)(2,1)S(1)} %collective-permute-done.3), channel_id=1, source_target_pairs={{0,8},{4,12},{8,16},{12,20},{16,24},{20,28},{24,0},{28,4},{1,9},{5... | collective-permute-start | bytes 1179656 | tf_op jit(solution)/shard_map/ppermute | solution.py:78
  29.3 12.4 %collective-permute-start.4 = (bf16[192,1024]{1,0:T(8,128)(2,1)S(1)}, bf16[192,1024]{1,0:T(8,128)(2,1)}, u32[]{:S(2)}, u32[]{:S(2)}) collective-permute-start(bf16[192,1024]{1,0:T(8,128)(2,1)S(1)} %collective-permute-done.3), channel_id=1, source_target_pairs={{0,4},{4,0},{8,12},{12,8},{16,20},{20,16},{24,28},{28,24},{1,5},{5... | collective-permute-start | bytes 1179656 | tf_op jit(solution)/shard_map/ppermute | solution.py:73
  41.1 9.4 %collective-permute-start.6 = (bf16[192,1024]{1,0:T(8,128)(2,1)}, bf16[192,1024]{1,0:T(8,128)(2,1)}, u32[]{:S(2)}, u32[]{:S(2)}) collective-permute-start(bf16[192,1024]{1,0:T(8,128)(2,1)} %collective-permute-done.5), channel_id=1, source_target_pairs={{0,4},{4,0},{8,12},{12,8},{16,20},{20,16},{24,28},{28,24},{1,5},{5... | collective-permute-start | bytes 1179656 | tf_op jit(solution)/shard_map/ppermute | solution.py:73
  54.1 8.2 %collective-permute-start.8 = (f32[8,128]{1,0:T(8,128)S(1)}, f32[8,128]{1,0:T(8,128)S(1)}, u32[]{:S(2)}, u32[]{:S(2)}) collective-permute-start(f32[8,128]{1,0:T(8,128)S(1)} %broadcast_in_dim.39), channel_id=1, source_target_pairs={{0,1},{1,0},{2,3},{3,2},{4,5},{5,4},{6,7},{7,6},{8,9},{9,8},{10,11... | collective-permute-start | bytes 12296 | tf_op jit(solution)/shard_map/ppermute | solution.py:82
  55.2 2.2 %copy-start.1 = (bf16[2048,1024]{1,0:T(8,128)(2,1)S(1)}, bf16[2048,1024]{1,0:T(8,128)(2,1)}, u32[]{:S(2)}) copy-start(bf16[2048,1024]{1,0:T(8,128)(2,1)} %param.5) | copy-start | bytes 12582916
  58.0 6.8 %collective-permute-start.10 = (f16[384,512]{1,0:T(8,128)(2,1)S(1)}, f16[384,512]{1,0:T(8,128)(2,1)S(1)}, u32[]{:S(2)}, u32[]{:S(2)}) collective-permute-start(f16[384,512]{1,0:T(8,128)(2,1)S(1)} %fusion.30), channel_id=1, source_target_pairs={{0,1},{1,0},{2,3},{3,2},{4,5},{5,4},{6,7},{7,6},{8,9},{9,8},{10,11... | collective-permute-start | bytes 1179656 | tf_op jit(solution)/shard_map/ppermute | solution.py:95
  59.2 8.7 %collective-permute-start.15 = (f16[384,512]{1,0:T(8,128)(2,1)S(1)}, f16[384,512]{1,0:T(8,128)(2,1)S(1)}, u32[]{:S(2)}, u32[]{:S(2)}) collective-permute-start(f16[384,512]{1,0:T(8,128)(2,1)S(1)} %fusion.31), channel_id=1, source_target_pairs={{0,1},{1,0},{2,3},{3,2},{4,5},{5,4},{6,7},{7,6},{8,9},{9,8},{10,11... | collective-permute-start | bytes 1179656 | tf_op jit(solution)/shard_map/ppermute | solution.py:95
  59.9 10.7 %collective-permute-start.19 = (f16[384,512]{1,0:T(8,128)(2,1)S(1)}, f16[384,512]{1,0:T(8,128)(2,1)S(1)}, u32[]{:S(2)}, u32[]{:S(2)}) collective-permute-start(f16[384,512]{1,0:T(8,128)(2,1)S(1)} %fusion.32), channel_id=1, source_target_pairs={{0,1},{1,0},{2,3},{3,2},{4,5},{5,4},{6,7},{7,6},{8,9},{9,8},{10,11... | collective-permute-start | bytes 1179656 | tf_op jit(solution)/shard_map/ppermute | solution.py:95
  62.9 3.6 %collective-permute-start.17 = (f32[8,128]{1,0:T(8,128)S(1)}, f32[8,128]{1,0:T(8,128)S(1)}, u32[]{:S(2)}, u32[]{:S(2)}) collective-permute-start(f32[8,128]{1,0:T(8,128)S(1)} %broadcast_add_fusion), channel_id=1, source_target_pairs={{0,2},{1,3},{2,0},{3,1},{4,6},{5,7},{6,4},{7,5},{8,10},{9,11},{10,... | collective-permute-start | bytes 12296 | tf_op jit(solution)/shard_map/ppermute | solution.py:84
  65.4 10.6 %collective-permute-start.11 = (bf16[384,2048]{1,0:T(8,128)(2,1)S(1)}, bf16[384,2048]{1,0:T(8,128)(2,1)S(1)}, u32[]{:S(2)}, u32[]{:S(2)}) collective-permute-start(bf16[384,2048]{1,0:T(8,128)(2,1)S(1)} %fusion.11), channel_id=1, source_target_pairs={{0,1},{1,0},{2,3},{3,2},{4,5},{5,4},{6,7},{7,6},{8,9},{9,8},{10,11... | collective-permute-start | bytes 4718600 | tf_op jit(solution)/shard_map/ppermute | solution.py:102
  66.5 4.9 %collective-permute-start.7 = (f16[384,512]{1,0:T(8,128)(2,1)S(1)}, f16[384,512]{1,0:T(8,128)(2,1)S(1)}, u32[]{:S(2)}, u32[]{:S(2)}) collective-permute-start(f16[384,512]{1,0:T(8,128)(2,1)S(1)} %fusion.29), channel_id=1, source_target_pairs={{0,1},{1,0},{2,3},{3,2},{4,5},{5,4},{6,7},{7,6},{8,9},{9,8},{10,11... | collective-permute-start | bytes 1179656 | tf_op jit(solution)/shard_map/ppermute | solution.py:95
  68.0 21.8 %collective-permute-start.18 = (f16[384,512]{1,0:T(8,128)(2,1)S(1)}, f16[384,512]{1,0:T(8,128)(2,1)S(1)}, u32[]{:S(2)}, u32[]{:S(2)}) collective-permute-start(f16[384,512]{1,0:T(8,128)(2,1)S(1)} %fusion.27), channel_id=1, source_target_pairs={{0,2},{1,3},{2,0},{3,1},{4,6},{5,7},{6,4},{7,5},{8,10},{9,11},{10,... | collective-permute-start | bytes 1179656 | tf_op jit(solution)/shard_map/ppermute | solution.py:98
  70.7 19.0 %collective-permute-start.16 = (f16[384,512]{1,0:T(8,128)(2,1)S(1)}, f16[384,512]{1,0:T(8,128)(2,1)S(1)}, u32[]{:S(2)}, u32[]{:S(2)}) collective-permute-start(f16[384,512]{1,0:T(8,128)(2,1)S(1)} %fusion.26), channel_id=1, source_target_pairs={{0,2},{1,3},{2,0},{3,1},{4,6},{5,7},{6,4},{7,5},{8,10},{9,11},{10,... | collective-permute-start | bytes 1179656 | tf_op jit(solution)/shard_map/ppermute | solution.py:98
  71.4 25.4 %collective-permute-start.20 = (f16[384,512]{1,0:T(8,128)(2,1)S(1)}, f16[384,512]{1,0:T(8,128)(2,1)S(1)}, u32[]{:S(2)}, u32[]{:S(2)}) collective-permute-start(f16[384,512]{1,0:T(8,128)(2,1)S(1)} %fusion.25), channel_id=1, source_target_pairs={{0,2},{1,3},{2,0},{3,1},{4,6},{5,7},{6,4},{7,5},{8,10},{9,11},{10,... | collective-permute-start | bytes 1179656 | tf_op jit(solution)/shard_map/ppermute | solution.py:98
  75.9 11.9 %collective-permute-start.13 = (f16[384,2048]{1,0:T(8,128)(2,1)S(1)}, f16[384,2048]{1,0:T(8,128)(2,1)S(1)}, u32[]{:S(2)}, u32[]{:S(2)}) collective-permute-start(f16[384,2048]{1,0:T(8,128)(2,1)S(1)} %multiply_convert_fusion), channel_id=1, source_target_pairs={{0,1},{1,0},{2,3},{3,2},{4,5},{5,4},{6,7},{7,6},{8,9},{9,8},{10,11... | collective-permute-start | bytes 4718600 | tf_op jit(solution)/shard_map/ppermute | solution.py:105
  87.8 16.8 %collective-permute-start.14 = (f16[384,512]{1,0:T(8,128)(2,1)S(1)}, f16[384,512]{1,0:T(8,128)(2,1)S(1)}, u32[]{:S(2)}, u32[]{:S(2)}) collective-permute-start(f16[384,512]{1,0:T(8,128)(2,1)S(1)} %fusion.28), channel_id=1, source_target_pairs={{0,2},{1,3},{2,0},{3,1},{4,6},{5,7},{6,4},{7,5},{8,10},{9,11},{10,... | collective-permute-start | bytes 1179656 | tf_op jit(solution)/shard_map/ppermute | solution.py:115
  87.9 9.0 %copy-start = (f32[384,2048]{1,0:T(8,128)S(1)}, f32[384,2048]{1,0:T(8,128)}, u32[]{:S(2)}) copy-start(f32[384,2048]{1,0:T(8,128)} %get-tuple-element.31) | copy-start | bytes 9437188

commit v4 on v3

--- a/solution.py
+++ b/solution.py
@@ -59,31 +59,41 @@
     def top(v):
         return jnp.max(jnp.abs(v)).astype(jnp.float32)
 
-    w_top = top(w_down)
-    g_top = top(grad_out)
+    upper = lax.broadcasted_iota(jnp.int32, (8, 128), 0) < 4
+    tops = jnp.where(upper, top(grad_out), top(w_down))
+    for axis, perm in (
+        ("col", over_core),
+        ("row", next_z),
+        ("row", [(i, (i + 4) % 8) for i in range(8)]),
+        ("row", over_x),
+        ("col", over_y),
+    ):
+        tops = jnp.maximum(tops, lax.ppermute(tops, axis, perm))
+    bound = jnp.maximum(2.0 * feats * tops[0, 0] * tops[7, 0], 1e-30)
+    scale, unscale = F16_TOP / bound, bound / F16_TOP
 
     act_near = gelu_value(pre_act.astype(jnp.float32)).astype(jnp.bfloat16)
     act_near_sib = lax.ppermute(act_near, "col", over_core)
 
-    shard = grad_out
+    shard, other = grad_out, None
+    half = rows // 2
     piece = jnp.zeros((4, 2, rows, feats), jnp.bfloat16)
     for k in range(4):
         zk = (z + 4 - k) % 4
         place = jnp.where(zk // 2 == y, 2, 0) + jnp.where(zk % 2 == core, 1, 0)
-        other = lax.ppermute(shard, "row", over_x)
-        piece = lax.dynamic_update_slice(piece, shard[None, None], (place, x, 0, 0))
-        piece = lax.dynamic_update_slice(piece, other[None, None], (place, 1 - x, 0, 0))
-        g_top = jnp.maximum(g_top, jnp.maximum(top(shard), top(other)))
         if k < 3:
-            shard = lax.ppermute(shard, "row", next_z)
+            after = lax.ppermute(shard, "row", next_z)
+            other = lax.ppermute(shard, "row", over_x)
+            piece = lax.dynamic_update_slice(piece, shard[None, None], (place, x, 0, 0))
+            piece = lax.dynamic_update_slice(piece, other[None, None], (place, 1 - x, 0, 0))
+            shard = after
+        else:
+            first = lax.ppermute(shard[:half], "row", over_x)
+            second = lax.ppermute(other[half:], "row", next_z)
+            piece = lax.dynamic_update_slice(piece, shard[None, None], (place, x, 0, 0))
+            piece = lax.dynamic_update_slice(piece, first[None, None], (place, 1 - x, 0, 0))
+            piece = lax.dynamic_update_slice(piece, second[None, None], (place, 1 - x, half, 0))
     piece = piece.reshape(4 * tokens, feats)
-
-    bound = jnp.full((8, 128), jnp.maximum(feats * g_top * w_top, 1e-30))
-    bound_sib = lax.ppermute(bound, "col", over_core)
-    bound_pair = bound + bound_sib
-    bound_far = lax.ppermute(bound_pair, "col", over_y)
-    scale, from_sib = F16_TOP / bound[0, 0], bound_sib[0, 0] / F16_TOP
-    to_far, from_far = F16_TOP / bound_pair[0, 0], bound_far[0, 0] / F16_TOP
 
     far_sib, far_mine = piece[:tokens], piece[tokens:2 * tokens]
     near_sib, near_mine = piece[2 * tokens:3 * tokens], piece[3 * tokens:]
@@ -93,8 +103,8 @@
         w = w_down[j * width:(j + 1) * width]
         out = (matmul_t(far_sib, w) * scale).astype(jnp.float16)
         back = lax.ppermute(out, "col", over_core)
-        pair = matmul_t(far_mine, w) + back.astype(jnp.float32) * from_sib
-        pairs.append((pair * to_far).astype(jnp.float16))
+        pair = matmul_t(far_mine, w) * scale + back.astype(jnp.float32)
+        pairs.append(pair.astype(jnp.float16))
     arrived = [lax.ppermute(pair, "col", over_y) for pair in pairs[:-1]]
 
     act_far = gelu_value(pre_far.astype(jnp.float32)).astype(jnp.bfloat16)
@@ -103,7 +113,7 @@
 
     near_out = (matmul_t(near_sib, w_down) * scale).astype(jnp.float16)
     near_back = lax.ppermute(near_out, "col", over_core)
-    near = matmul_t(near_mine, w_down) + near_back.astype(jnp.float32) * from_sib
+    near = matmul_t(near_mine, w_down) + near_back.astype(jnp.float32) * unscale
 
     act_full = jnp.concatenate([act_far_sib, act_far, act_near_sib, act_near], axis=0)
     grad_w = lax.dot_general(
@@ -121,7 +131,7 @@
         mine, factor, there = near[:, cut], slope[:, cut], arrived[j]
         if j == CHUNKS - 1:
             mine, factor, there, *parts = lax.optimization_barrier((mine, factor, there, *parts))
-        both = mine + there.astype(jnp.float32) * from_far
+        both = mine + there.astype(jnp.float32) * unscale
         parts.append((both * factor).astype(jnp.bfloat16))
     return (acc_new, jnp.concatenate(parts, axis=1))
 

time: 107 us -> 128 us (1.20)
  waiting for transfers between devices: 27.3 us -> 65.4 us
  other arithmetic: 23.6 us -> 13.3 us
  local copies, waits for them, and re-layouts: 11 us -> 5.51 us
  between operations: 8.76 us -> 3.63 us
  starting transfers between devices: 15.2 us -> 19.5 us
    ppermute x5 -> x10, waiting for transfers between devices: 11.2 us -> 51.5 us  [the longest x5 26 us: on_device_paired(): tops = jnp.maximum(tops, lax.ppermute(tops, axis, perm))]
    reduce_max x9 -> x2, other arithmetic: 15.1 us -> 4.47 us  [top(): return jnp.max(jnp.abs(v)).astype(jnp.float32)]
    ppermute x5 -> x10, starting transfers between devices: 3.13 us -> 8.69 us  [the longest x5 4.82 us: on_device_paired(): tops = jnp.maximum(tops, lax.ppermute(tops, axis, perm))]
    dynamic_update_slice x4 -> x3, local copies, waits for them, and re-layouts: 4.11 us -> 1.1 us  [on_device_paired(): lax.dynamic_update_slice(piece, other[None, None], (place, 1 - x, 0, 0))]
    ppermute x4 -> x3, waiting for transfers between devices: 2.17 us -> 0.01 us  [on_device_paired(): other = lax.ppermute(shard, 'row', over_x)]
    ppermute x4 -> x3, starting transfers between devices: 4.61 us -> 3.63 us  [on_device_paired(): other = lax.ppermute(shard, 'row', over_x)]
  transfers between devices with their start and end apart: 21 -> 25, of which waited for: 7 -> 10; matrix products, arithmetic and copies ran while one was open for 48% -> 24% of each run, Pallas kernels for 0% -> 0%
where the time goes in v4:
time: 128 us
  waiting for transfers between devices  65.4 us (51%)
  matrix products  20.4 us (16%)
  starting transfers between devices  19.5 us (15%)
  other arithmetic  13.3 us (10%)
  local copies, waits for them, and re-layouts  5.51 us (4%)
  between operations  3.63 us (3%)
    ppermute x5, waiting for transfers between devices, on_device_paired(): tops = jnp.maximum(tops, lax.ppermute(tops, axis, perm))  26 us
    ppermute x3, waiting for transfers between devices, on_device_paired(): after = lax.ppermute(shard, 'row', next_z)  18.2 us
    dot_general x1, matrix products, on_device_paired(): lax.dot_general(act_full, piece, (((0,), (0,)), ((), ())), preferred_elem...  11.8 us
    dot_general x10, matrix products, matmul_t(): lax.dot_general(a, b, (((1,), (1,)), ((), ())), preferred_element_type=jn...  8.61 us
    ppermute x3, waiting for transfers between devices, on_device_paired(): arrived = [lax.ppermute(pair, 'col', over_y) for pair in pairs[:-1]]  7.07 us
    ppermute x1, waiting for transfers between devices, on_device_paired(): arrived.append(lax.ppermute(last, 'col', over_y))  6.81 us
    ppermute x1, waiting for transfers between devices, on_device_paired(): first = lax.ppermute(shard[:half], 'row', over_x)  4.95 us
    ppermute x5, starting transfers between devices, on_device_paired(): tops = jnp.maximum(tops, lax.ppermute(tops, axis, perm))  4.82 us
  transfers between devices with their start and end apart: 25, of which 10 were waited for; matrix products, arithmetic and copies ran while one was open for 24% of the time, Pallas kernels for 0%

profile of v4, /device:TPU:0, one launch (start us, length us, event | category | flops | bytes accessed | tf_op | source)
XLA Modules:
  0.0 127.7 jit_solution(5749658030891526552)
XLA Ops:
  0.6 3.8 %abs_reduce_fusion = bf16[]{:T(256)} fusion(bf16[2048,1024]{1,0:T(8,128)(2,1)} %param.5), kind=kLoop, calls=%fused_computation.14 | loop fusion | flops 4194303 | bytes 4194306 | tf_op jit(solution)/shard_map/reduce_max | solution.py:60
  5.1 0.7 abs_reduce_fusion.1
  6.5 0.5 collective-permute-start.8
  7.0 2.6 %collective-permute-start = (bf16[192,1024]{1,0:T(8,128)(2,1)S(1)}, bf16[192,1024]{1,0:T(8,128)(2,1)}, u32[]{:S(2)}, u32[]{:S(2)}) collective-permute-start(bf16[192,1024]{1,0:T(8,128)(2,1)S(1)} %copy-done.2), channel_id=1, source_target_pairs={{0,4},{4,0},{8,12},{12,8},{16,20},{20,16},{24,28},{28,24},{1,5},{5... | collective-permute-start | bytes 1179656 | tf_op jit(solution)/shard_map/ppermute | solution.py:86
  9.5 1.6 %collective-permute-start.1 = (bf16[192,1024]{1,0:T(8,128)(2,1)S(1)}, bf16[192,1024]{1,0:T(8,128)(2,1)}, u32[]{:S(2)}, u32[]{:S(2)}) collective-permute-start(bf16[192,1024]{1,0:T(8,128)(2,1)S(1)} %copy-done.2), channel_id=1, source_target_pairs={{0,8},{4,12},{8,16},{12,20},{16,24},{20,28},{24,0},{28,4},{1,9},{5... | collective-permute-start | bytes 1179656 | tf_op jit(solution)/shard_map/ppermute | solution.py:85
  11.1 1.5 %collective-permute-start.14 = (bf16[384,2048]{1,0:T(8,128)(2,1)}, bf16[384,2048]{1,0:T(8,128)(2,1)}, u32[]{:S(2)}, u32[]{:S(2)}) collective-permute-start(bf16[384,2048]{1,0:T(8,128)(2,1)} %param.6), channel_id=1, source_target_pairs={{0,2},{1,3},{2,0},{3,1},{4,6},{5,7},{6,4},{7,5},{8,10},{9,11},{10,... | collective-permute-start | bytes 4718600 | tf_op jit(solution)/shard_map/ppermute | solution.py:57
  12.7 1.6 %collective-permute-start.9 = (f32[8,128]{1,0:T(8,128)S(1)}, f32[8,128]{1,0:T(8,128)S(1)}, u32[]{:S(2)}, u32[]{:S(2)}) collective-permute-start(f32[8,128]{1,0:T(8,128)S(1)} %broadcast_maximum_fusion), channel_id=1, source_target_pairs={{0,8},{4,12},{8,16},{12,20},{16,24},{20,28},{24,0},{28,4},{1,9},{5... | collective-permute-start | bytes 12296 | tf_op jit(solution)/shard_map/ppermute | solution.py:71
  14.3 4.0 %fusion.20 = (f32[384,2048]{1,0:T(8,128)}, bf16[384,2048]{1,0:T(8,128)(2,1)}) fusion(bf16[384,2048]{1,0:T(8,128)(2,1)} %param.6), kind=kLoop, calls=%fused_computation.27 | loop fusion | flops 9437184 | bytes 6291456 | tf_op jit(solution)/shard_map/add | solution.py:17
  18.3 4.4 %collective-permute-done.9 = f32[8,128]{1,0:T(8,128)S(1)} collective-permute-done((f32[8,128]{1,0:T(8,128)S(1)}, f32[8,128]{1,0:T(8,128)S(1)}, u32[]{:S(2)}, u32[]{:S(2)}) %collective-permute-start.9) | collective-permute-done | bytes 4128 | tf_op jit(solution)/shard_map/ppermute | solution.py:71
  22.8 0.7 collective-permute-start.10
  23.5 3.8 %collective-permute-done.10 = f32[8,128]{1,0:T(8,128)S(1)} collective-permute-done((f32[8,128]{1,0:T(8,128)S(1)}, f32[8,128]{1,0:T(8,128)S(1)}, u32[]{:S(2)}, u32[]{:S(2)}) %collective-permute-start.10) | collective-permute-done | bytes 4128 | tf_op jit(solution)/shard_map/ppermute | solution.py:71
  27.3 0.5 collective-permute-start.11
  28.4 2.6 %collective-permute-done.11 = f32[8,128]{1,0:T(8,128)S(1)} collective-permute-done((f32[8,128]{1,0:T(8,128)S(1)}, f32[8,128]{1,0:T(8,128)S(1)}, u32[]{:S(2)}, u32[]{:S(2)}) %collective-permute-start.11) | collective-permute-done | bytes 4128 | tf_op jit(solution)/shard_map/ppermute | solution.py:71
  30.9 1.5 %collective-permute-start.12 = (f32[8,128]{1,0:T(8,128)S(1)}, f32[8,128]{1,0:T(8,128)S(1)}, u32[]{:S(2)}, u32[]{:S(2)}) collective-permute-start(f32[8,128]{1,0:T(8,128)S(1)} %max.22), channel_id=1, source_target_pairs={{0,2},{1,3},{2,0},{3,1},{4,6},{5,7},{6,4},{7,5},{8,10},{9,11},{10,... | collective-permute-start | bytes 12296 | tf_op jit(solution)/shard_map/ppermute | solution.py:71
  32.4 15.2 %collective-permute-done.12 = f32[8,128]{1,0:T(8,128)S(1)} collective-permute-done((f32[8,128]{1,0:T(8,128)S(1)}, f32[8,128]{1,0:T(8,128)S(1)}, u32[]{:S(2)}, u32[]{:S(2)}) %collective-permute-start.12) | collective-permute-done | bytes 4128 | tf_op jit(solution)/shard_map/ppermute | solution.py:71
  47.7 0.5 fusion.46
  49.5 1.6 %collective-permute-start.3 = (bf16[192,1024]{1,0:T(8,128)(2,1)}, bf16[192,1024]{1,0:T(8,128)(2,1)S(1)}, u32[]{:S(2)}, u32[]{:S(2)}) collective-permute-start(bf16[192,1024]{1,0:T(8,128)(2,1)} %collective-permute-done.1), channel_id=1, source_target_pairs={{0,8},{4,12},{8,16},{12,20},{16,24},{20,28},{24,0},{28,4},{1,9},{5... | collective-permute-start | bytes 1179656 | tf_op jit(solution)/shard_map/ppermute | solution.py:85
  51.2 0.5 collective-permute-start.2
  51.7 1.0 bitcast_dynamic-update-slice_fusion.5
  52.7 1.0 bitcast_dynamic-update-slice_fusion.4
  53.8 7.9 %collective-permute-done.3 = bf16[192,1024]{1,0:T(8,128)(2,1)S(1)} collective-permute-done((bf16[192,1024]{1,0:T(8,128)(2,1)}, bf16[192,1024]{1,0:T(8,128)(2,1)S(1)}, u32[]{:S(2)}, u32[]{:S(2)}) %collective-permute-start.3) | collective-permute-done | bytes 393248 | tf_op jit(solution)/shard_map/ppermute | solution.py:85
  61.7 0.5 collective-permute-start.4
  62.3 10.3 %collective-permute-done.5 = bf16[192,1024]{1,0:T(8,128)(2,1)S(1)} collective-permute-done((bf16[192,1024]{1,0:T(8,128)(2,1)S(1)}, bf16[192,1024]{1,0:T(8,128)(2,1)S(1)}, u32[]{:S(2)}, u32[]{:S(2)}) %collective-permute-start.5) | collective-permute-done | bytes 393248 | tf_op jit(solution)/shard_map/ppermute | solution.py:85
  72.6 0.6 collective-permute-start.6
  73.4 5.0 %collective-permute-done.6 = bf16[96,1024]{1,0:T(8,128)(2,1)S(1)} collective-permute-done((bf16[96,1024]{1,0:T(8,128)(2,1)S(1)}, bf16[96,1024]{1,0:T(8,128)(2,1)S(1)}, u32[]{:S(2)}, u32[]{:S(2)}) %collective-permute-start.6) | collective-permute-done | bytes 196640 | tf_op jit(solution)/shard_map/ppermute | solution.py:91
  78.4 2.4 %collective-permute-done.7 = bf16[96,1024]{1,0:T(8,128)(2,1)S(1)} collective-permute-done((bf16[96,1024]{1,0:T(8,128)(2,1)S(1)}, bf16[96,1024]{1,0:T(8,128)(2,1)S(1)}, u32[]{:S(2)}, u32[]{:S(2)}) %collective-permute-start.7) | collective-permute-done | bytes 196640 | tf_op jit(solution)/shard_map/ppermute | solution.py:92
  81.2 1.8 %copy-done.1 = bf16[2048,1024]{1,0:T(8,128)(2,1)S(1)} copy-done((bf16[2048,1024]{1,0:T(8,128)(2,1)S(1)}, bf16[2048,1024]{1,0:T(8,128)(2,1)}, u32[]{:S(2)}) %copy-start.1) | copy-done | bytes 4194328
  83.0 0.6 fusion.30
  83.7 0.6 fusion.31
  84.3 0.6 collective-permute-start.20
  84.9 0.6 fusion.32
  85.6 2.0 %fusion.11 = bf16[384,2048]{1,0:T(8,128)(2,1)S(1)} fusion(bf16[384,2048]{1,0:T(8,128)(2,1)} %collective-permute-done.14), kind=kLoop, calls=%fused_computation.18 | loop fusion | flops 4718592 | bytes 3145728 | tf_op jit(solution)/shard_map/convert_element_type | solution.py:110
  87.6 0.6 fusion.27
  88.6 0.6 fusion.29
  89.5 1.5 %collective-permute-start.22 = (f16[384,512]{1,0:T(8,128)(2,1)S(1)}, f16[384,512]{1,0:T(8,128)(2,1)S(1)}, u32[]{:S(2)}, u32[]{:S(2)}) collective-permute-start(f16[384,512]{1,0:T(8,128)(2,1)S(1)} %fusion.27), channel_id=1, source_target_pairs={{0,2},{1,3},{2,0},{3,1},{4,6},{5,7},{6,4},{7,5},{8,10},{9,11},{10,... | collective-permute-start | bytes 1179656 | tf_op jit(solution)/shard_map/ppermute | solution.py:108
  91.0 0.6 fusion.26
  91.7 0.6 collective-permute-start.21
  92.2 0.6 fusion.25
  92.9 1.6 %collective-permute-start.24 = (f16[384,512]{1,0:T(8,128)(2,1)S(1)}, f16[384,512]{1,0:T(8,128)(2,1)S(1)}, u32[]{:S(2)}, u32[]{:S(2)}) collective-permute-start(f16[384,512]{1,0:T(8,128)(2,1)S(1)} %fusion.25), channel_id=1, source_target_pairs={{0,2},{1,3},{2,0},{3,1},{4,6},{5,7},{6,4},{7,5},{8,10},{9,11},{10,... | collective-permute-start | bytes 1179656 | tf_op jit(solution)/shard_map/ppermute | solution.py:108
  94.5 0.6 fusion.28
  95.1 1.8 %multiply_convert_fusion = f16[384,2048]{1,0:T(8,128)(2,1)S(1)} fusion(bf16[384,1024]{1,0:T(8,128)(2,1)S(1)} %bitcast.40, bf16[2048,1024]{1,0:T(8,128)(2,1)S(1)} %copy-done.1, f32[]{:T(128)} %bitcast.10), kind=kOutput, calls=%fused_computation.29 | convolution fusion | flops 1612185600 | bytes 6553604 | tf_op jit(solution)/shard_map/dot_general | solution.py:41
  97.1 11.8 %multiply_add_fusion = f32[2048,1024]{1,0:T(8,128)} fusion(f32[2048,1024]{1,0:T(8,128)} %param.7, bf16[1536,1024]{1,0:T(8,128)(2,1)S(1)} %bitcast.38, bf16[384,2048]{1,0:T(8,128)(2,1)} %get-tuple-element.32, bf16[384,2048]{1,0:T(8,128)(2,1)} %collective-permute-done.17, bf16[384,2048]{1,0:T(8,128)(2,1)S(1)} %fusion.11, ...), kind=kOutput, calls=%fused_computation | convolution fusion | flops 6471811072 | bytes 26214400 | tf_op jit(solution)/shard_map/dot_general | solution.py:119
  108.9 0.5 collective-permute-start.19
  109.4 1.8 %multiply_add_fusion.1 = f32[384,2048]{1,0:T(8,128)S(1)} fusion(f16[384,2048]{1,0:T(8,128)(2,1)S(1)} %collective-permute-done.18, bf16[384,1024]{1,0:T(8,128)(2,1)S(1)} %bitcast.39, bf16[2048,1024]{1,0:T(8,128)(2,1)S(1)} %copy-done.1, f32[]{:T(128)} %bitcast.15), kind=kOutput, calls=%fused_computation.28 | convolution fusion | flops 1612972032 | bytes 9699332 | tf_op jit(solution)/shard_map/dot_general | solution.py:41
  111.2 7.1 %collective-permute-done.24 = f16[384,512]{1,0:T(8,128)(2,1)S(1)} collective-permute-done((f16[384,512]{1,0:T(8,128)(2,1)S(1)}, f16[384,512]{1,0:T(8,128)(2,1)S(1)}, u32[]{:S(2)}, u32[]{:S(2)}) %collective-permute-start.24) | collective-permute-done | bytes 393248 | tf_op jit(solution)/shard_map/ppermute | solution.py:108
  118.3 1.0 fusion.41
  119.3 6.8 %collective-permute-done.19 = f16[384,512]{1,0:T(8,128)(2,1)S(1)} collective-permute-done((f16[384,512]{1,0:T(8,128)(2,1)S(1)}, f16[384,512]{1,0:T(8,128)(2,1)S(1)}, u32[]{:S(2)}, u32[]{:S(2)}) %collective-permute-start.19) | collective-permute-done | bytes 393248 | tf_op jit(solution)/shard_map/ppermute | solution.py:125
  126.4 1.3 %pad_maximum_fusion = bf16[384,2048]{1,0:T(8,128)(2,1)} fusion(bf16[384,512]{1,0:T(8,128)(2,1)S(1)} %multiply_convert_fusion.1, bf16[384,512]{1,0:T(8,128)(2,1)S(1)} %get-tuple-element.18, bf16[384,512]{1,0:T(8,128)(2,1)S(1)} %get-tuple-element.17, bf16[384,512]{1,0:T(8,128)(2,1)S(1)} %get-tuple-element.16), kind=kLoop, calls=%fused_computation.30 | loop fusion | flops 6291456 | bytes 3145728 | tf_op jit(solution)/shard_map/concatenate | solution.py:136
  (47 shorter events, 2.5 us)
Async XLA Ops:
  0.6 4.5 %copy-start.2 = (bf16[192,1024]{1,0:T(8,128)(2,1)S(1)}, bf16[192,1024]{1,0:T(8,128)(2,1)}, u32[]{:S(2)}) copy-start(bf16[192,1024]{1,0:T(8,128)(2,1)} %param.4) | copy-start | bytes 1179652
  6.5 6.1 %collective-permute-start.8 = (f32[8,128]{1,0:T(8,128)S(1)}, f32[8,128]{1,0:T(8,128)S(1)}, u32[]{:S(2)}, u32[]{:S(2)}) collective-permute-start(f32[8,128]{1,0:T(8,128)S(1)} %iota.7), channel_id=1, source_target_pairs={{0,1},{1,0},{2,3},{3,2},{4,5},{5,4},{6,7},{7,6},{8,9},{9,8},{10,11... | collective-permute-start | bytes 12296 | tf_op jit(solution)/shard_map/ppermute | solution.py:71
  7.0 44.7 %collective-permute-start = (bf16[192,1024]{1,0:T(8,128)(2,1)S(1)}, bf16[192,1024]{1,0:T(8,128)(2,1)}, u32[]{:S(2)}, u32[]{:S(2)}) collective-permute-start(bf16[192,1024]{1,0:T(8,128)(2,1)S(1)} %copy-done.2), channel_id=1, source_target_pairs={{0,4},{4,0},{8,12},{12,8},{16,20},{20,16},{24,28},{28,24},{1,5},{5... | collective-permute-start | bytes 1179656 | tf_op jit(solution)/shard_map/ppermute | solution.py:86
  9.5 40.0 %collective-permute-start.1 = (bf16[192,1024]{1,0:T(8,128)(2,1)S(1)}, bf16[192,1024]{1,0:T(8,128)(2,1)}, u32[]{:S(2)}, u32[]{:S(2)}) collective-permute-start(bf16[192,1024]{1,0:T(8,128)(2,1)S(1)} %copy-done.2), channel_id=1, source_target_pairs={{0,8},{4,12},{8,16},{12,20},{16,24},{20,28},{24,0},{28,4},{1,9},{5... | collective-permute-start | bytes 1179656 | tf_op jit(solution)/shard_map/ppermute | solution.py:85
  11.1 74.5 %collective-permute-start.14 = (bf16[384,2048]{1,0:T(8,128)(2,1)}, bf16[384,2048]{1,0:T(8,128)(2,1)}, u32[]{:S(2)}, u32[]{:S(2)}) collective-permute-start(bf16[384,2048]{1,0:T(8,128)(2,1)} %param.6), channel_id=1, source_target_pairs={{0,2},{1,3},{2,0},{3,1},{4,6},{5,7},{6,4},{7,5},{8,10},{9,11},{10,... | collective-permute-start | bytes 4718600 | tf_op jit(solution)/shard_map/ppermute | solution.py:57
  12.7 10.0 %collective-permute-start.9 = (f32[8,128]{1,0:T(8,128)S(1)}, f32[8,128]{1,0:T(8,128)S(1)}, u32[]{:S(2)}, u32[]{:S(2)}) collective-permute-start(f32[8,128]{1,0:T(8,128)S(1)} %broadcast_maximum_fusion), channel_id=1, source_target_pairs={{0,8},{4,12},{8,16},{12,20},{16,24},{20,28},{24,0},{28,4},{1,9},{5... | collective-permute-start | bytes 12296 | tf_op jit(solution)/shard_map/ppermute | solution.py:71
  18.3 78.6 %collective-permute-start.17 = (bf16[384,2048]{1,0:T(8,128)(2,1)}, bf16[384,2048]{1,0:T(8,128)(2,1)}, u32[]{:S(2)}, u32[]{:S(2)}) collective-permute-start(bf16[384,2048]{1,0:T(8,128)(2,1)} %get-tuple-element.32), channel_id=1, source_target_pairs={{0,1},{1,0},{2,3},{3,2},{4,5},{5,4},{6,7},{7,6},{8,9},{9,8},{10,11... | collective-permute-start | bytes 4718600 | tf_op jit(solution)/shard_map/ppermute | solution.py:76
  22.8 4.5 %collective-permute-start.10 = (f32[8,128]{1,0:T(8,128)S(1)}, f32[8,128]{1,0:T(8,128)S(1)}, u32[]{:S(2)}, u32[]{:S(2)}) collective-permute-start(f32[8,128]{1,0:T(8,128)S(1)} %fusion.60), channel_id=1, source_target_pairs={{0,16},{4,20},{8,24},{12,28},{16,0},{20,4},{24,8},{28,12},{1,17},{... | collective-permute-start | bytes 12296 | tf_op jit(solution)/shard_map/ppermute | solution.py:71
  27.3 3.6 %collective-permute-start.11 = (f32[8,128]{1,0:T(8,128)S(1)}, f32[8,128]{1,0:T(8,128)S(1)}, u32[]{:S(2)}, u32[]{:S(2)}) collective-permute-start(f32[8,128]{1,0:T(8,128)S(1)} %max.21), channel_id=1, source_target_pairs={{0,4},{4,0},{8,12},{12,8},{16,20},{20,16},{24,28},{28,24},{1,5},{5... | collective-permute-start | bytes 12296 | tf_op jit(solution)/shard_map/ppermute | solution.py:71
  30.9 16.7 %collective-permute-start.12 = (f32[8,128]{1,0:T(8,128)S(1)}, f32[8,128]{1,0:T(8,128)S(1)}, u32[]{:S(2)}, u32[]{:S(2)}) collective-permute-start(f32[8,128]{1,0:T(8,128)S(1)} %max.22), channel_id=1, source_target_pairs={{0,2},{1,3},{2,0},{3,1},{4,6},{5,7},{6,4},{7,5},{8,10},{9,11},{10,... | collective-permute-start | bytes 12296 | tf_op jit(solution)/shard_map/ppermute | solution.py:71
  49.5 12.1 %collective-permute-start.3 = (bf16[192,1024]{1,0:T(8,128)(2,1)}, bf16[192,1024]{1,0:T(8,128)(2,1)S(1)}, u32[]{:S(2)}, u32[]{:S(2)}) collective-permute-start(bf16[192,1024]{1,0:T(8,128)(2,1)} %collective-permute-done.1), channel_id=1, source_target_pairs={{0,8},{4,12},{8,16},{12,20},{16,24},{20,28},{24,0},{28,4},{1,9},{5... | collective-permute-start | bytes 1179656 | tf_op jit(solution)/shard_map/ppermute | solution.py:85
  51.2 11.1 %collective-permute-start.2 = (bf16[192,1024]{1,0:T(8,128)(2,1)}, bf16[192,1024]{1,0:T(8,128)(2,1)S(1)}, u32[]{:S(2)}, u32[]{:S(2)}) collective-permute-start(bf16[192,1024]{1,0:T(8,128)(2,1)} %collective-permute-done.1), channel_id=1, source_target_pairs={{0,4},{4,0},{8,12},{12,8},{16,20},{20,16},{24,28},{28,24},{1,5},{5... | collective-permute-start | bytes 1179656 | tf_op jit(solution)/shard_map/ppermute | solution.py:86
  61.7 11.0 %collective-permute-start.5 = (bf16[192,1024]{1,0:T(8,128)(2,1)S(1)}, bf16[192,1024]{1,0:T(8,128)(2,1)S(1)}, u32[]{:S(2)}, u32[]{:S(2)}) collective-permute-start(bf16[192,1024]{1,0:T(8,128)(2,1)S(1)} %collective-permute-done.3), channel_id=1, source_target_pairs={{0,8},{4,12},{8,16},{12,20},{16,24},{20,28},{24,0},{28,4},{1,9},{5... | collective-permute-start | bytes 1179656 | tf_op jit(solution)/shard_map/ppermute | solution.py:85
  61.7 11.6 %collective-permute-start.4 = (bf16[192,1024]{1,0:T(8,128)(2,1)S(1)}, bf16[192,1024]{1,0:T(8,128)(2,1)S(1)}, u32[]{:S(2)}, u32[]{:S(2)}) collective-permute-start(bf16[192,1024]{1,0:T(8,128)(2,1)S(1)} %collective-permute-done.3), channel_id=1, source_target_pairs={{0,4},{4,0},{8,12},{12,8},{16,20},{20,16},{24,28},{28,24},{1,5},{5... | collective-permute-start | bytes 1179656 | tf_op jit(solution)/shard_map/ppermute | solution.py:86
  72.6 5.7 %collective-permute-start.6 = (bf16[96,1024]{1,0:T(8,128)(2,1)S(1)}, bf16[96,1024]{1,0:T(8,128)(2,1)S(1)}, u32[]{:S(2)}, u32[]{:S(2)}) collective-permute-start(bf16[96,1024]{1,0:T(8,128)(2,1)S(1)} %slice.96), channel_id=1, source_target_pairs={{0,4},{4,0},{8,12},{12,8},{16,20},{20,16},{24,28},{28,24},{1,5},{5... | collective-permute-start | bytes 589832 | tf_op jit(solution)/shard_map/ppermute | solution.py:91
  73.3 7.5 %collective-permute-start.7 = (bf16[96,1024]{1,0:T(8,128)(2,1)S(1)}, bf16[96,1024]{1,0:T(8,128)(2,1)S(1)}, u32[]{:S(2)}, u32[]{:S(2)}) collective-permute-start(bf16[96,1024]{1,0:T(8,128)(2,1)S(1)} %slice.97), channel_id=1, source_target_pairs={{0,8},{4,12},{8,16},{12,20},{16,24},{20,28},{24,0},{28,4},{1,9},{5... | collective-permute-start | bytes 589832 | tf_op jit(solution)/shard_map/ppermute | solution.py:92
  80.8 2.2 %copy-start.1 = (bf16[2048,1024]{1,0:T(8,128)(2,1)S(1)}, bf16[2048,1024]{1,0:T(8,128)(2,1)}, u32[]{:S(2)}) copy-start(bf16[2048,1024]{1,0:T(8,128)(2,1)} %param.5) | copy-start | bytes 12582916
  83.6 4.0 %collective-permute-start.15 = (f16[384,512]{1,0:T(8,128)(2,1)S(1)}, f16[384,512]{1,0:T(8,128)(2,1)S(1)}, u32[]{:S(2)}, u32[]{:S(2)}) collective-permute-start(f16[384,512]{1,0:T(8,128)(2,1)S(1)} %fusion.30), channel_id=1, source_target_pairs={{0,1},{1,0},{2,3},{3,2},{4,5},{5,4},{6,7},{7,6},{8,9},{9,8},{10,11... | collective-permute-start | bytes 1179656 | tf_op jit(solution)/shard_map/ppermute | solution.py:105
  84.3 5.2 %collective-permute-start.20 = (f16[384,512]{1,0:T(8,128)(2,1)S(1)}, f16[384,512]{1,0:T(8,128)(2,1)S(1)}, u32[]{:S(2)}, u32[]{:S(2)}) collective-permute-start(f16[384,512]{1,0:T(8,128)(2,1)S(1)} %fusion.31), channel_id=1, source_target_pairs={{0,1},{1,0},{2,3},{3,2},{4,5},{5,4},{6,7},{7,6},{8,9},{9,8},{10,11... | collective-permute-start | bytes 1179656 | tf_op jit(solution)/shard_map/ppermute | solution.py:105
  85.5 6.2 %collective-permute-start.23 = (f16[384,512]{1,0:T(8,128)(2,1)S(1)}, f16[384,512]{1,0:T(8,128)(2,1)S(1)}, u32[]{:S(2)}, u32[]{:S(2)}) collective-permute-start(f16[384,512]{1,0:T(8,128)(2,1)S(1)} %fusion.32), channel_id=1, source_target_pairs={{0,1},{1,0},{2,3},{3,2},{4,5},{5,4},{6,7},{7,6},{8,9},{9,8},{10,11... | collective-permute-start | bytes 1179656 | tf_op jit(solution)/shard_map/ppermute | solution.py:105
  88.2 8.8 %collective-permute-start.16 = (bf16[384,2048]{1,0:T(8,128)(2,1)S(1)}, bf16[384,2048]{1,0:T(8,128)(2,1)S(1)}, u32[]{:S(2)}, u32[]{:S(2)}) collective-permute-start(bf16[384,2048]{1,0:T(8,128)(2,1)S(1)} %fusion.11), channel_id=1, source_target_pairs={{0,1},{1,0},{2,3},{3,2},{4,5},{5,4},{6,7},{7,6},{8,9},{9,8},{10,11... | collective-permute-start | bytes 4718600 | tf_op jit(solution)/shard_map/ppermute | solution.py:112
  89.2 3.7 %collective-permute-start.13 = (f16[384,512]{1,0:T(8,128)(2,1)S(1)}, f16[384,512]{1,0:T(8,128)(2,1)S(1)}, u32[]{:S(2)}, u32[]{:S(2)}) collective-permute-start(f16[384,512]{1,0:T(8,128)(2,1)S(1)} %fusion.29), channel_id=1, source_target_pairs={{0,1},{1,0},{2,3},{3,2},{4,5},{5,4},{6,7},{7,6},{8,9},{9,8},{10,11... | collective-permute-start | bytes 1179656 | tf_op jit(solution)/shard_map/ppermute | solution.py:105
  89.5 21.7 %collective-permute-start.22 = (f16[384,512]{1,0:T(8,128)(2,1)S(1)}, f16[384,512]{1,0:T(8,128)(2,1)S(1)}, u32[]{:S(2)}, u32[]{:S(2)}) collective-permute-start(f16[384,512]{1,0:T(8,128)(2,1)S(1)} %fusion.27), channel_id=1, source_target_pairs={{0,2},{1,3},{2,0},{3,1},{4,6},{5,7},{6,4},{7,5},{8,10},{9,11},{10,... | collective-permute-start | bytes 1179656 | tf_op jit(solution)/shard_map/ppermute | solution.py:108
  91.7 19.5 %collective-permute-start.21 = (f16[384,512]{1,0:T(8,128)(2,1)S(1)}, f16[384,512]{1,0:T(8,128)(2,1)S(1)}, u32[]{:S(2)}, u32[]{:S(2)}) collective-permute-start(f16[384,512]{1,0:T(8,128)(2,1)S(1)} %fusion.26), channel_id=1, source_target_pairs={{0,2},{1,3},{2,0},{3,1},{4,6},{5,7},{6,4},{7,5},{8,10},{9,11},{10,... | collective-permute-start | bytes 1179656 | tf_op jit(solution)/shard_map/ppermute | solution.py:108
  92.9 25.4 %collective-permute-start.24 = (f16[384,512]{1,0:T(8,128)(2,1)S(1)}, f16[384,512]{1,0:T(8,128)(2,1)S(1)}, u32[]{:S(2)}, u32[]{:S(2)}) collective-permute-start(f16[384,512]{1,0:T(8,128)(2,1)S(1)} %fusion.25), channel_id=1, source_target_pairs={{0,2},{1,3},{2,0},{3,1},{4,6},{5,7},{6,4},{7,5},{8,10},{9,11},{10,... | collective-permute-start | bytes 1179656 | tf_op jit(solution)/shard_map/ppermute | solution.py:108
  97.0 12.4 %collective-permute-start.18 = (f16[384,2048]{1,0:T(8,128)(2,1)S(1)}, f16[384,2048]{1,0:T(8,128)(2,1)S(1)}, u32[]{:S(2)}, u32[]{:S(2)}) collective-permute-start(f16[384,2048]{1,0:T(8,128)(2,1)S(1)} %multiply_convert_fusion), channel_id=1, source_target_pairs={{0,1},{1,0},{2,3},{3,2},{4,5},{5,4},{6,7},{7,6},{8,9},{9,8},{10,11... | collective-permute-start | bytes 4718600 | tf_op jit(solution)/shard_map/ppermute | solution.py:115
  108.9 17.2 %collective-permute-start.19 = (f16[384,512]{1,0:T(8,128)(2,1)S(1)}, f16[384,512]{1,0:T(8,128)(2,1)S(1)}, u32[]{:S(2)}, u32[]{:S(2)}) collective-permute-start(f16[384,512]{1,0:T(8,128)(2,1)S(1)} %fusion.28), channel_id=1, source_target_pairs={{0,2},{1,3},{2,0},{3,1},{4,6},{5,7},{6,4},{7,5},{8,10},{9,11},{10,... | collective-permute-start | bytes 1179656 | tf_op jit(solution)/shard_map/ppermute | solution.py:125
  109.4 8.9 %copy-start = (f32[384,2048]{1,0:T(8,128)S(1)}, f32[384,2048]{1,0:T(8,128)}, u32[]{:S(2)}) copy-start(f32[384,2048]{1,0:T(8,128)} %get-tuple-element.31) | copy-start | bytes 9437188

commit v5 on v3

--- a/solution.py
+++ b/solution.py
@@ -65,17 +65,26 @@
     act_near = gelu_value(pre_act.astype(jnp.float32)).astype(jnp.bfloat16)
     act_near_sib = lax.ppermute(act_near, "col", over_core)
 
-    shard = grad_out
+    shard, other = grad_out, None
+    half = rows // 2
     piece = jnp.zeros((4, 2, rows, feats), jnp.bfloat16)
     for k in range(4):
         zk = (z + 4 - k) % 4
         place = jnp.where(zk // 2 == y, 2, 0) + jnp.where(zk % 2 == core, 1, 0)
-        other = lax.ppermute(shard, "row", over_x)
-        piece = lax.dynamic_update_slice(piece, shard[None, None], (place, x, 0, 0))
-        piece = lax.dynamic_update_slice(piece, other[None, None], (place, 1 - x, 0, 0))
-        g_top = jnp.maximum(g_top, jnp.maximum(top(shard), top(other)))
         if k < 3:
-            shard = lax.ppermute(shard, "row", next_z)
+            after = lax.ppermute(shard, "row", next_z)
+            other = lax.ppermute(shard, "row", over_x)
+            piece = lax.dynamic_update_slice(piece, shard[None, None], (place, x, 0, 0))
+            piece = lax.dynamic_update_slice(piece, other[None, None], (place, 1 - x, 0, 0))
+            g_top = jnp.maximum(g_top, jnp.maximum(top(after), top(other)))
+            shard = after
+        else:
+            first = lax.ppermute(shard[:half], "row", over_x)
+            second = lax.ppermute(other[half:], "row", next_z)
+            piece = lax.dynamic_update_slice(piece, shard[None, None], (place, x, 0, 0))
+            piece = lax.dynamic_update_slice(piece, first[None, None], (place, 1 - x, 0, 0))
+            piece = lax.dynamic_update_slice(piece, second[None, None], (place, 1 - x, half, 0))
+            g_top = jnp.maximum(g_top, jnp.maximum(top(first), top(second)))
     piece = piece.reshape(4 * tokens, feats)
 
     bound = jnp.full((8, 128), jnp.maximum(feats * g_top * w_top, 1e-30))
@@ -98,7 +107,7 @@
     arrived = [lax.ppermute(pair, "col", over_y) for pair in pairs[:-1]]
 
     act_far = gelu_value(pre_far.astype(jnp.float32)).astype(jnp.bfloat16)
-    act_far, near_sib, _ = lax.optimization_barrier((act_far, near_sib, pairs[1]))
+    act_far, near_sib, _ = lax.optimization_barrier((act_far, near_sib, pairs[2]))
     act_far_sib = lax.ppermute(act_far, "col", over_core)
 
     near_out = (matmul_t(near_sib, w_down) * scale).astype(jnp.float16)

time: 107 us -> 109 us (1.019)
  waiting for transfers between devices: 27.3 us -> 30.4 us
  local copies, waits for them, and re-layouts: 11 us -> 9.52 us
  other arithmetic: 23.6 us -> 22.5 us
    ppermute x3 -> x5, waiting for transfers between devices: 11 us -> 16.4 us  [the longest x3 13.3 us: on_device_paired(): after = lax.ppermute(shard, 'row', next_z)]
    ppermute x4 -> x3, waiting for transfers between devices: 2.17 us -> 0.01 us  [on_device_paired(): other = lax.ppermute(shard, 'row', over_x)]
    dynamic_update_slice x4 -> x3, local copies, waits for them, and re-layouts: 4.11 us -> 2.09 us  [on_device_paired(): lax.dynamic_update_slice(piece, other[None, None], (place, 1 - x, 0, 0))]
    reduce_max x9 -> x10, other arithmetic: 15.1 us -> 13.9 us  [top(): return jnp.max(jnp.abs(v)).astype(jnp.float32)]
    ppermute x3 -> x5, starting transfers between devices: 3.05 us -> 4.25 us  [the longest x3 3.66 us: on_device_paired(): after = lax.ppermute(shard, 'row', next_z)]
    ppermute x4 -> x3, starting transfers between devices: 4.61 us -> 4.07 us  [on_device_paired(): other = lax.ppermute(shard, 'row', over_x)]
  transfers between devices with their start and end apart: 21 -> 22, of which waited for: 7 -> 8; matrix products, arithmetic and copies ran while one was open for 48% -> 45% of each run, Pallas kernels for 0% -> 0%
where the time goes in v5:
time: 109 us; the launch traced here: 108 us
  waiting for transfers between devices  30.4 us (28%)
  other arithmetic  22.5 us (21%)
  matrix products  20.4 us (19%)
  starting transfers between devices  15.8 us (14%)
  local copies, waits for them, and re-layouts  9.52 us (9%)
  between operations  9.32 us (9%)
    reduce_max x10, other arithmetic, top(): return jnp.max(jnp.abs(v)).astype(jnp.float32)  13.9 us
    ppermute x3, waiting for transfers between devices, on_device_paired(): after = lax.ppermute(shard, 'row', next_z)  13.3 us
    dot_general x1, matrix products, on_device_paired(): lax.dot_general(act_full, piece, (((0,), (0,)), ((), ())), preferred_elem...  11.8 us
    dot_general x10, matrix products, matmul_t(): lax.dot_general(a, b, (((1,), (1,)), ((), ())), preferred_element_type=jn...  8.56 us
    ppermute x3, waiting for transfers between devices, on_device_paired(): arrived = [lax.ppermute(pair, 'col', over_y) for pair in pairs[:-1]]  7.14 us
    ppermute x1, waiting for transfers between devices, on_device_paired(): arrived.append(lax.ppermute(last, 'col', over_y))  6.67 us
    add x1, other arithmetic, gelu_slope(): 0.5 * (1.0 + lax.erf(v / math.sqrt(2.0)))  4.09 us
    ppermute x3, starting transfers between devices, on_device_paired(): other = lax.ppermute(shard, 'row', over_x)  4.07 us
  transfers between devices with their start and end apart: 22, of which 8 were waited for; matrix products, arithmetic and copies ran while one was open for 45% of the time, Pallas kernels for 0%

profile of v5, /device:TPU:0, one launch (start us, length us, event | category | flops | bytes accessed | tf_op | source)
XLA Modules:
  0.0 108.0 jit_solution(17059426041597139900)
XLA Ops:
  0.6 3.0 %collective-permute-start = (bf16[192,1024]{1,0:T(8,128)(2,1)}, bf16[192,1024]{1,0:T(8,128)(2,1)}, u32[]{:S(2)}, u32[]{:S(2)}) collective-permute-start(bf16[192,1024]{1,0:T(8,128)(2,1)} %param.4), channel_id=1, source_target_pairs={{0,4},{4,0},{8,12},{12,8},{16,20},{20,16},{24,28},{28,24},{1,5},{5... | collective-permute-start | bytes 1179656 | tf_op jit(solution)/shard_map/ppermute | solution.py:76
  3.6 1.6 %collective-permute-start.1 = (bf16[192,1024]{1,0:T(8,128)(2,1)}, bf16[192,1024]{1,0:T(8,128)(2,1)}, u32[]{:S(2)}, u32[]{:S(2)}) collective-permute-start(bf16[192,1024]{1,0:T(8,128)(2,1)} %param.4), channel_id=1, source_target_pairs={{0,8},{4,12},{8,16},{12,20},{16,24},{20,28},{24,0},{28,4},{1,9},{5... | collective-permute-start | bytes 1179656 | tf_op jit(solution)/shard_map/ppermute | solution.py:75
  5.2 1.5 %collective-permute-start.10 = (bf16[384,2048]{1,0:T(8,128)(2,1)}, bf16[384,2048]{1,0:T(8,128)(2,1)}, u32[]{:S(2)}, u32[]{:S(2)}) collective-permute-start(bf16[384,2048]{1,0:T(8,128)(2,1)} %param.6), channel_id=1, source_target_pairs={{0,2},{1,3},{2,0},{3,1},{4,6},{5,7},{6,4},{7,5},{8,10},{9,11},{10,... | collective-permute-start | bytes 4718600 | tf_op jit(solution)/shard_map/ppermute | solution.py:57
  6.7 4.1 %fusion.20 = (f32[384,2048]{1,0:T(8,128)}, bf16[384,2048]{1,0:T(8,128)(2,1)}) fusion(bf16[384,2048]{1,0:T(8,128)(2,1)} %param.6), kind=kLoop, calls=%fused_computation.27 | loop fusion | flops 9437184 | bytes 6291456 | tf_op jit(solution)/shard_map/add | solution.py:17
  11.9 0.7 abs_reduce_fusion.7
  12.5 3.8 %abs_reduce_fusion = bf16[]{:T(256)} fusion(bf16[2048,1024]{1,0:T(8,128)(2,1)} %param.5), kind=kLoop, calls=%fused_computation.14 | loop fusion | flops 4194303 | bytes 4194306 | tf_op jit(solution)/shard_map/reduce_max | solution.py:60
  16.4 1.5 %collective-permute-start.3 = (bf16[192,1024]{1,0:T(8,128)(2,1)}, bf16[192,1024]{1,0:T(8,128)(2,1)S(1)}, u32[]{:S(2)}, u32[]{:S(2)}) collective-permute-start(bf16[192,1024]{1,0:T(8,128)(2,1)} %collective-permute-done.1), channel_id=1, source_target_pairs={{0,8},{4,12},{8,16},{12,20},{16,24},{20,28},{24,0},{28,4},{1,9},{5... | collective-permute-start | bytes 1179656 | tf_op jit(solution)/shard_map/ppermute | solution.py:75
  17.9 0.5 collective-permute-start.2
  18.5 1.0 bitcast_dynamic-update-slice_fusion.5
  19.5 1.7 %abs_reduce_fusion.5 = bf16[]{:T(256)} fusion(bf16[192,1024]{1,0:T(8,128)(2,1)} %collective-permute-done), kind=kLoop, calls=%fused_computation.80 | loop fusion | flops 393215 | bytes 393218 | tf_op jit(solution)/shard_map/reduce_max | solution.py:60
  21.2 1.7 %abs_reduce_fusion.6 = bf16[]{:T(256)} fusion(bf16[192,1024]{1,0:T(8,128)(2,1)} %collective-permute-done.1), kind=kLoop, calls=%fused_computation.81 | loop fusion | flops 393215 | bytes 393218 | tf_op jit(solution)/shard_map/reduce_max | solution.py:60
  24.7 1.0 bitcast_dynamic-update-slice_fusion.4
  25.7 3.6 %collective-permute-done.3 = bf16[192,1024]{1,0:T(8,128)(2,1)S(1)} collective-permute-done((bf16[192,1024]{1,0:T(8,128)(2,1)}, bf16[192,1024]{1,0:T(8,128)(2,1)S(1)}, u32[]{:S(2)}, u32[]{:S(2)}) %collective-permute-start.3) | collective-permute-done | bytes 393248 | tf_op jit(solution)/shard_map/ppermute | solution.py:75
  29.3 0.7 abs_reduce_fusion.4
  30.0 1.7 %abs_reduce_fusion.3 = bf16[]{:T(256)} fusion(bf16[192,1024]{1,0:T(8,128)(2,1)} %collective-permute-done.2), kind=kLoop, calls=%fused_computation.78 | loop fusion | flops 393215 | bytes 393218 | tf_op jit(solution)/shard_map/reduce_max | solution.py:60
  32.9 0.6 collective-permute-start.5
  33.4 0.5 collective-permute-start.4
  34.0 1.0 bitcast_dynamic-update-slice_fusion.3
  35.0 9.7 %collective-permute-done.5 = bf16[192,1024]{1,0:T(8,128)(2,1)S(1)} collective-permute-done((bf16[192,1024]{1,0:T(8,128)(2,1)S(1)}, bf16[192,1024]{1,0:T(8,128)(2,1)S(1)}, u32[]{:S(2)}, u32[]{:S(2)}) %collective-permute-start.5) | collective-permute-done | bytes 393248 | tf_op jit(solution)/shard_map/ppermute | solution.py:75
  44.7 0.7 slice.101
  45.4 0.5 collective-permute-start.6
  46.1 0.7 abs_reduce_fusion.2
  46.9 0.7 abs_reduce_fusion.1
  48.9 2.5 %collective-permute-done.6 = bf16[96,1024]{1,0:T(8,128)(2,1)} collective-permute-done((bf16[96,1024]{1,0:T(8,128)(2,1)}, bf16[96,1024]{1,0:T(8,128)(2,1)}, u32[]{:S(2)}, u32[]{:S(2)}) %collective-permute-start.6) | collective-permute-done | bytes 196640 | tf_op jit(solution)/shard_map/ppermute | solution.py:82
  51.4 1.6 %abs_reduce_fusion.9 = bf16[]{:T(256)} fusion(bf16[96,1024]{1,0:T(8,128)(2,1)} %collective-permute-done.6), kind=kLoop, calls=%fused_computation.86 | loop fusion | flops 196607 | bytes 196610 | tf_op jit(solution)/shard_map/reduce_max | solution.py:60
  53.5 0.7 abs_reduce_fusion.8
  56.3 0.9 bitcast_dynamic-update-slice_fusion.8
  57.7 1.8 %copy-done.1 = bf16[2048,1024]{1,0:T(8,128)(2,1)S(1)} copy-done((bf16[2048,1024]{1,0:T(8,128)(2,1)S(1)}, bf16[2048,1024]{1,0:T(8,128)(2,1)}, u32[]{:S(2)}) %copy-start.1) | copy-done | bytes 4194328
  59.5 0.6 fusion.32
  60.1 0.6 fusion.31
  60.7 0.6 fusion.30
  61.3 0.6 collective-permute-start.11
  62.4 0.5 slice.84
  64.9 2.0 %fusion.11 = bf16[384,2048]{1,0:T(8,128)(2,1)S(1)} fusion(bf16[384,2048]{1,0:T(8,128)(2,1)} %collective-permute-done.10), kind=kLoop, calls=%fused_computation.18 | loop fusion | flops 4718592 | bytes 3145728 | tf_op jit(solution)/shard_map/convert_element_type | solution.py:109
  66.9 0.6 fusion.27
  67.7 0.6 fusion.29
  69.8 1.9 %collective-permute-start.21 = (f16[384,512]{1,0:T(8,128)(2,1)S(1)}, f16[384,512]{1,0:T(8,128)(2,1)S(1)}, u32[]{:S(2)}, u32[]{:S(2)}) collective-permute-start(f16[384,512]{1,0:T(8,128)(2,1)S(1)} %fusion.27), channel_id=1, source_target_pairs={{0,2},{1,3},{2,0},{3,1},{4,6},{5,7},{6,4},{7,5},{8,10},{9,11},{10,... | collective-permute-start | bytes 1179656 | tf_op jit(solution)/shard_map/ppermute | solution.py:107
  71.7 0.6 fusion.26
  72.6 0.6 fusion.25
  73.2 1.9 %collective-permute-start.20 = (f16[384,512]{1,0:T(8,128)(2,1)S(1)}, f16[384,512]{1,0:T(8,128)(2,1)S(1)}, u32[]{:S(2)}, u32[]{:S(2)}) collective-permute-start(f16[384,512]{1,0:T(8,128)(2,1)S(1)} %fusion.25), channel_id=1, source_target_pairs={{0,2},{1,3},{2,0},{3,1},{4,6},{5,7},{6,4},{7,5},{8,10},{9,11},{10,... | collective-permute-start | bytes 1179656 | tf_op jit(solution)/shard_map/ppermute | solution.py:107
  75.1 0.6 fusion.28
  75.8 1.8 %multiply_convert_fusion = f16[384,2048]{1,0:T(8,128)(2,1)S(1)} fusion(bf16[384,1024]{1,0:T(8,128)(2,1)S(1)} %bitcast.41, bf16[2048,1024]{1,0:T(8,128)(2,1)S(1)} %copy-done.1, f32[]{:T(128)S(6)} %div.93), kind=kOutput, calls=%fused_computation.29 | convolution fusion | flops 1612185600 | bytes 6553604 | tf_op jit(solution)/shard_map/dot_general | solution.py:41
  77.7 11.8 %multiply_add_fusion = f32[2048,1024]{1,0:T(8,128)} fusion(f32[2048,1024]{1,0:T(8,128)} %param.7, bf16[1536,1024]{1,0:T(8,128)(2,1)S(1)} %bitcast.39, bf16[384,2048]{1,0:T(8,128)(2,1)} %get-tuple-element.32, bf16[384,2048]{1,0:T(8,128)(2,1)} %collective-permute-done.13, bf16[384,2048]{1,0:T(8,128)(2,1)S(1)} %fusion.11, ...), kind=kOutput, calls=%fused_computation | convolution fusion | flops 6471811072 | bytes 26214400 | tf_op jit(solution)/shard_map/dot_general | solution.py:118
  89.7 1.8 %multiply_add_fusion.1 = f32[384,2048]{1,0:T(8,128)S(1)} fusion(f16[384,2048]{1,0:T(8,128)(2,1)S(1)} %collective-permute-done.14, bf16[384,1024]{1,0:T(8,128)(2,1)S(1)} %bitcast.40, bf16[2048,1024]{1,0:T(8,128)(2,1)S(1)} %copy-done.1, f32[]{:T(128)} %bitcast.11), kind=kOutput, calls=%fused_computation.28 | convolution fusion | flops 1612972032 | bytes 9699332 | tf_op jit(solution)/shard_map/dot_general | solution.py:41
  91.6 7.1 %collective-permute-done.20 = f16[384,512]{1,0:T(8,128)(2,1)S(1)} collective-permute-done((f16[384,512]{1,0:T(8,128)(2,1)S(1)}, f16[384,512]{1,0:T(8,128)(2,1)S(1)}, u32[]{:S(2)}, u32[]{:S(2)}) %collective-permute-start.20) | collective-permute-done | bytes 393248 | tf_op jit(solution)/shard_map/ppermute | solution.py:107
  98.7 1.0 fusion.41
  99.7 6.7 %collective-permute-done.15 = f16[384,512]{1,0:T(8,128)(2,1)S(1)} collective-permute-done((f16[384,512]{1,0:T(8,128)(2,1)S(1)}, f16[384,512]{1,0:T(8,128)(2,1)S(1)}, u32[]{:S(2)}, u32[]{:S(2)}) %collective-permute-start.15) | collective-permute-done | bytes 393248 | tf_op jit(solution)/shard_map/ppermute | solution.py:124
  106.6 1.3 %pad_maximum_fusion = bf16[384,2048]{1,0:T(8,128)(2,1)} fusion(bf16[384,512]{1,0:T(8,128)(2,1)S(1)} %multiply_convert_fusion.1, bf16[384,512]{1,0:T(8,128)(2,1)S(1)} %get-tuple-element.18, bf16[384,512]{1,0:T(8,128)(2,1)S(1)} %get-tuple-element.17, bf16[384,512]{1,0:T(8,128)(2,1)S(1)} %get-tuple-element.16), kind=kLoop, calls=%fused_computation.30 | loop fusion | flops 6291456 | bytes 3145728 | tf_op jit(solution)/shard_map/concatenate | solution.py:135
  (46 shorter events, 5.2 us)
Async XLA Ops:
  0.6 17.8 %collective-permute-start = (bf16[192,1024]{1,0:T(8,128)(2,1)}, bf16[192,1024]{1,0:T(8,128)(2,1)}, u32[]{:S(2)}, u32[]{:S(2)}) collective-permute-start(bf16[192,1024]{1,0:T(8,128)(2,1)} %param.4), channel_id=1, source_target_pairs={{0,4},{4,0},{8,12},{12,8},{16,20},{20,16},{24,28},{28,24},{1,5},{5... | collective-permute-start | bytes 1179656 | tf_op jit(solution)/shard_map/ppermute | solution.py:76
  3.6 12.8 %collective-permute-start.1 = (bf16[192,1024]{1,0:T(8,128)(2,1)}, bf16[192,1024]{1,0:T(8,128)(2,1)}, u32[]{:S(2)}, u32[]{:S(2)}) collective-permute-start(bf16[192,1024]{1,0:T(8,128)(2,1)} %param.4), channel_id=1, source_target_pairs={{0,8},{4,12},{8,16},{12,20},{16,24},{20,28},{24,0},{28,4},{1,9},{5... | collective-permute-start | bytes 1179656 | tf_op jit(solution)/shard_map/ppermute | solution.py:75
  5.2 59.6 %collective-permute-start.10 = (bf16[384,2048]{1,0:T(8,128)(2,1)}, bf16[384,2048]{1,0:T(8,128)(2,1)}, u32[]{:S(2)}, u32[]{:S(2)}) collective-permute-start(bf16[384,2048]{1,0:T(8,128)(2,1)} %param.6), channel_id=1, source_target_pairs={{0,2},{1,3},{2,0},{3,1},{4,6},{5,7},{6,4},{7,5},{8,10},{9,11},{10,... | collective-permute-start | bytes 4718600 | tf_op jit(solution)/shard_map/ppermute | solution.py:57
  10.8 1.0 copy-start.2
  10.8 66.8 %collective-permute-start.13 = (bf16[384,2048]{1,0:T(8,128)(2,1)}, bf16[384,2048]{1,0:T(8,128)(2,1)}, u32[]{:S(2)}, u32[]{:S(2)}) collective-permute-start(bf16[384,2048]{1,0:T(8,128)(2,1)} %get-tuple-element.32), channel_id=1, source_target_pairs={{0,1},{1,0},{2,3},{3,2},{4,5},{5,4},{6,7},{7,6},{8,9},{9,8},{10,11... | collective-permute-start | bytes 4718600 | tf_op jit(solution)/shard_map/ppermute | solution.py:66
  16.4 12.9 %collective-permute-start.3 = (bf16[192,1024]{1,0:T(8,128)(2,1)}, bf16[192,1024]{1,0:T(8,128)(2,1)S(1)}, u32[]{:S(2)}, u32[]{:S(2)}) collective-permute-start(bf16[192,1024]{1,0:T(8,128)(2,1)} %collective-permute-done.1), channel_id=1, source_target_pairs={{0,8},{4,12},{8,16},{12,20},{16,24},{20,28},{24,0},{28,4},{1,9},{5... | collective-permute-start | bytes 1179656 | tf_op jit(solution)/shard_map/ppermute | solution.py:75
  17.9 12.0 %collective-permute-start.2 = (bf16[192,1024]{1,0:T(8,128)(2,1)}, bf16[192,1024]{1,0:T(8,128)(2,1)}, u32[]{:S(2)}, u32[]{:S(2)}) collective-permute-start(bf16[192,1024]{1,0:T(8,128)(2,1)} %collective-permute-done.1), channel_id=1, source_target_pairs={{0,4},{4,0},{8,12},{12,8},{16,20},{20,16},{24,28},{28,24},{1,5},{5... | collective-permute-start | bytes 1179656 | tf_op jit(solution)/shard_map/ppermute | solution.py:76
  32.9 11.9 %collective-permute-start.5 = (bf16[192,1024]{1,0:T(8,128)(2,1)S(1)}, bf16[192,1024]{1,0:T(8,128)(2,1)S(1)}, u32[]{:S(2)}, u32[]{:S(2)}) collective-permute-start(bf16[192,1024]{1,0:T(8,128)(2,1)S(1)} %collective-permute-done.3), channel_id=1, source_target_pairs={{0,8},{4,12},{8,16},{12,20},{16,24},{20,28},{24,0},{28,4},{1,9},{5... | collective-permute-start | bytes 1179656 | tf_op jit(solution)/shard_map/ppermute | solution.py:75
  33.4 12.5 %collective-permute-start.4 = (bf16[192,1024]{1,0:T(8,128)(2,1)S(1)}, bf16[192,1024]{1,0:T(8,128)(2,1)S(1)}, u32[]{:S(2)}, u32[]{:S(2)}) collective-permute-start(bf16[192,1024]{1,0:T(8,128)(2,1)S(1)} %collective-permute-done.3), channel_id=1, source_target_pairs={{0,4},{4,0},{8,12},{12,8},{16,20},{20,16},{24,28},{28,24},{1,5},{5... | collective-permute-start | bytes 1179656 | tf_op jit(solution)/shard_map/ppermute | solution.py:76
  45.4 6.0 %collective-permute-start.6 = (bf16[96,1024]{1,0:T(8,128)(2,1)}, bf16[96,1024]{1,0:T(8,128)(2,1)}, u32[]{:S(2)}, u32[]{:S(2)}) collective-permute-start(bf16[96,1024]{1,0:T(8,128)(2,1)} %slice.101), channel_id=1, source_target_pairs={{0,4},{4,0},{8,12},{12,8},{16,20},{20,16},{24,28},{28,24},{1,5},{5... | collective-permute-start | bytes 589832 | tf_op jit(solution)/shard_map/ppermute | solution.py:82
  46.0 7.5 %collective-permute-start.7 = (bf16[96,1024]{1,0:T(8,128)(2,1)S(1)}, bf16[96,1024]{1,0:T(8,128)(2,1)S(1)}, u32[]{:S(2)}, u32[]{:S(2)}) collective-permute-start(bf16[96,1024]{1,0:T(8,128)(2,1)S(1)} %slice.102), channel_id=1, source_target_pairs={{0,8},{4,12},{8,16},{12,20},{16,24},{20,28},{24,0},{28,4},{1,9},{5... | collective-permute-start | bytes 589832 | tf_op jit(solution)/shard_map/ppermute | solution.py:83
  56.2 5.7 %collective-permute-start.9 = (f32[8,128]{1,0:T(8,128)S(1)}, f32[8,128]{1,0:T(8,128)S(1)}, u32[]{:S(2)}, u32[]{:S(2)}) collective-permute-start(f32[8,128]{1,0:T(8,128)S(1)} %broadcast_in_dim.43), channel_id=1, source_target_pairs={{0,1},{1,0},{2,3},{3,2},{4,5},{5,4},{6,7},{7,6},{8,9},{9,8},{10,11... | collective-permute-start | bytes 12296 | tf_op jit(solution)/shard_map/ppermute | solution.py:91
  57.3 2.2 %copy-start.1 = (bf16[2048,1024]{1,0:T(8,128)(2,1)S(1)}, bf16[2048,1024]{1,0:T(8,128)(2,1)}, u32[]{:S(2)}) copy-start(bf16[2048,1024]{1,0:T(8,128)(2,1)} %param.5) | copy-start | bytes 12582916
  61.3 5.6 %collective-permute-start.11 = (f16[384,512]{1,0:T(8,128)(2,1)S(1)}, f16[384,512]{1,0:T(8,128)(2,1)S(1)}, u32[]{:S(2)}, u32[]{:S(2)}) collective-permute-start(f16[384,512]{1,0:T(8,128)(2,1)S(1)} %fusion.30), channel_id=1, source_target_pairs={{0,1},{1,0},{2,3},{3,2},{4,5},{5,4},{6,7},{7,6},{8,9},{9,8},{10,11... | collective-permute-start | bytes 1179656 | tf_op jit(solution)/shard_map/ppermute | solution.py:104
  61.9 8.0 %collective-permute-start.16 = (f16[384,512]{1,0:T(8,128)(2,1)S(1)}, f16[384,512]{1,0:T(8,128)(2,1)S(1)}, u32[]{:S(2)}, u32[]{:S(2)}) collective-permute-start(f16[384,512]{1,0:T(8,128)(2,1)S(1)} %fusion.31), channel_id=1, source_target_pairs={{0,1},{1,0},{2,3},{3,2},{4,5},{5,4},{6,7},{7,6},{8,9},{9,8},{10,11... | collective-permute-start | bytes 1179656 | tf_op jit(solution)/shard_map/ppermute | solution.py:104
  62.0 10.4 %collective-permute-start.19 = (f16[384,512]{1,0:T(8,128)(2,1)S(1)}, f16[384,512]{1,0:T(8,128)(2,1)S(1)}, u32[]{:S(2)}, u32[]{:S(2)}) collective-permute-start(f16[384,512]{1,0:T(8,128)(2,1)S(1)} %fusion.32), channel_id=1, source_target_pairs={{0,1},{1,0},{2,3},{3,2},{4,5},{5,4},{6,7},{7,6},{8,9},{9,8},{10,11... | collective-permute-start | bytes 1179656 | tf_op jit(solution)/shard_map/ppermute | solution.py:104
  64.8 3.7 %collective-permute-start.18 = (f32[8,128]{1,0:T(8,128)S(1)}, f32[8,128]{1,0:T(8,128)S(1)}, u32[]{:S(2)}, u32[]{:S(2)}) collective-permute-start(f32[8,128]{1,0:T(8,128)S(1)} %broadcast_add_fusion), channel_id=1, source_target_pairs={{0,2},{1,3},{2,0},{3,1},{4,6},{5,7},{6,4},{7,5},{8,10},{9,11},{10,... | collective-permute-start | bytes 12296 | tf_op jit(solution)/shard_map/ppermute | solution.py:93
  67.5 10.2 %collective-permute-start.12 = (bf16[384,2048]{1,0:T(8,128)(2,1)S(1)}, bf16[384,2048]{1,0:T(8,128)(2,1)S(1)}, u32[]{:S(2)}, u32[]{:S(2)}) collective-permute-start(bf16[384,2048]{1,0:T(8,128)(2,1)S(1)} %fusion.11), channel_id=1, source_target_pairs={{0,1},{1,0},{2,3},{3,2},{4,5},{5,4},{6,7},{7,6},{8,9},{9,8},{10,11... | collective-permute-start | bytes 4718600 | tf_op jit(solution)/shard_map/ppermute | solution.py:111
  68.5 4.8 %collective-permute-start.8 = (f16[384,512]{1,0:T(8,128)(2,1)S(1)}, f16[384,512]{1,0:T(8,128)(2,1)S(1)}, u32[]{:S(2)}, u32[]{:S(2)}) collective-permute-start(f16[384,512]{1,0:T(8,128)(2,1)S(1)} %fusion.29), channel_id=1, source_target_pairs={{0,1},{1,0},{2,3},{3,2},{4,5},{5,4},{6,7},{7,6},{8,9},{9,8},{10,11... | collective-permute-start | bytes 1179656 | tf_op jit(solution)/shard_map/ppermute | solution.py:104
  69.8 21.7 %collective-permute-start.21 = (f16[384,512]{1,0:T(8,128)(2,1)S(1)}, f16[384,512]{1,0:T(8,128)(2,1)S(1)}, u32[]{:S(2)}, u32[]{:S(2)}) collective-permute-start(f16[384,512]{1,0:T(8,128)(2,1)S(1)} %fusion.27), channel_id=1, source_target_pairs={{0,2},{1,3},{2,0},{3,1},{4,6},{5,7},{6,4},{7,5},{8,10},{9,11},{10,... | collective-permute-start | bytes 1179656 | tf_op jit(solution)/shard_map/ppermute | solution.py:107
  72.4 19.2 %collective-permute-start.17 = (f16[384,512]{1,0:T(8,128)(2,1)S(1)}, f16[384,512]{1,0:T(8,128)(2,1)S(1)}, u32[]{:S(2)}, u32[]{:S(2)}) collective-permute-start(f16[384,512]{1,0:T(8,128)(2,1)S(1)} %fusion.26), channel_id=1, source_target_pairs={{0,2},{1,3},{2,0},{3,1},{4,6},{5,7},{6,4},{7,5},{8,10},{9,11},{10,... | collective-permute-start | bytes 1179656 | tf_op jit(solution)/shard_map/ppermute | solution.py:107
  73.2 25.5 %collective-permute-start.20 = (f16[384,512]{1,0:T(8,128)(2,1)S(1)}, f16[384,512]{1,0:T(8,128)(2,1)S(1)}, u32[]{:S(2)}, u32[]{:S(2)}) collective-permute-start(f16[384,512]{1,0:T(8,128)(2,1)S(1)} %fusion.25), channel_id=1, source_target_pairs={{0,2},{1,3},{2,0},{3,1},{4,6},{5,7},{6,4},{7,5},{8,10},{9,11},{10,... | collective-permute-start | bytes 1179656 | tf_op jit(solution)/shard_map/ppermute | solution.py:107
  77.6 12.1 %collective-permute-start.14 = (f16[384,2048]{1,0:T(8,128)(2,1)S(1)}, f16[384,2048]{1,0:T(8,128)(2,1)S(1)}, u32[]{:S(2)}, u32[]{:S(2)}) collective-permute-start(f16[384,2048]{1,0:T(8,128)(2,1)S(1)} %multiply_convert_fusion), channel_id=1, source_target_pairs={{0,1},{1,0},{2,3},{3,2},{4,5},{5,4},{6,7},{7,6},{8,9},{9,8},{10,11... | collective-permute-start | bytes 4718600 | tf_op jit(solution)/shard_map/ppermute | solution.py:114
  89.5 16.9 %collective-permute-start.15 = (f16[384,512]{1,0:T(8,128)(2,1)S(1)}, f16[384,512]{1,0:T(8,128)(2,1)S(1)}, u32[]{:S(2)}, u32[]{:S(2)}) collective-permute-start(f16[384,512]{1,0:T(8,128)(2,1)S(1)} %fusion.28), channel_id=1, source_target_pairs={{0,2},{1,3},{2,0},{3,1},{4,6},{5,7},{6,4},{7,5},{8,10},{9,11},{10,... | collective-permute-start | bytes 1179656 | tf_op jit(solution)/shard_map/ppermute | solution.py:124
  89.7 9.0 %copy-start = (f32[384,2048]{1,0:T(8,128)S(1)}, f32[384,2048]{1,0:T(8,128)}, u32[]{:S(2)}) copy-start(f32[384,2048]{1,0:T(8,128)} %get-tuple-element.31) | copy-start | bytes 9437188

commit v6 on v3

--- a/solution.py
+++ b/solution.py
@@ -91,9 +91,9 @@
     pairs = []
     for j in range(CHUNKS):
         w = w_down[j * width:(j + 1) * width]
-        out = (matmul_t(far_sib, w) * scale).astype(jnp.float16)
+        out = matmul_t(far_sib, w)
         back = lax.ppermute(out, "col", over_core)
-        pair = matmul_t(far_mine, w) + back.astype(jnp.float32) * from_sib
+        pair = matmul_t(far_mine, w) + back
         pairs.append((pair * to_far).astype(jnp.float16))
     arrived = [lax.ppermute(pair, "col", over_y) for pair in pairs[:-1]]
 

time: 107 us -> 115 us (1.075)
  matrix products: 20.4 us -> 30.7 us
  waiting for transfers between devices: 27.3 us -> 23.8 us
    dot_general x10, matrix products: 8.56 us -> 18.4 us  [matmul_t(): lax.dot_general(a, b, (((1,), (1,)), ((), ())), preferred_element_type=jn...]
    ppermute x3, waiting for transfers between devices: 7.09 us -> 2.31 us  [on_device_paired(): arrived = [lax.ppermute(pair, 'col', over_y) for pair in pairs[:-1]]]
    ppermute x3, starting transfers between devices: 4.24 us -> 2.83 us  [on_device_paired(): arrived = [lax.ppermute(pair, 'col', over_y) for pair in pairs[:-1]]]
    ppermute x1, waiting for transfers between devices: 0.22 us -> 1.51 us  [on_device_paired(): bound_far = lax.ppermute(bound_pair, 'col', over_y)]
    unnamed x6 -> x16, local copies, waits for them, and re-layouts: 2.31 us -> 2.12 us
  transfers between devices with their start and end apart: 21 -> 21, of which waited for: 7 -> 7; matrix products, arithmetic and copies ran while one was open for 48% -> 55% of each run, Pallas kernels for 0% -> 0%
where the time goes in v6:
time: 115 us
  matrix products  30.7 us (27%)
  other arithmetic  24.7 us (21%)
  waiting for transfers between devices  23.8 us (21%)
  starting transfers between devices  14.5 us (13%)
  local copies, waits for them, and re-layouts  11.9 us (10%)
  between operations  8.96 us (8%)
    dot_general x10, matrix products, matmul_t(): lax.dot_general(a, b, (((1,), (1,)), ((), ())), preferred_element_type=jn...  18.4 us
    reduce_max x9, other arithmetic, top(): return jnp.max(jnp.abs(v)).astype(jnp.float32)  15.3 us
    dot_general x1, matrix products, on_device_paired(): lax.dot_general(act_full, piece, (((0,), (0,)), ((), ())), preferred_elem...  12.2 us
    ppermute x3, waiting for transfers between devices, on_device_paired(): shard = lax.ppermute(shard, 'row', next_z)  10.8 us
    ppermute x1, waiting for transfers between devices, on_device_paired(): arrived.append(lax.ppermute(last, 'col', over_y))  7.05 us
    ppermute x4, starting transfers between devices, on_device_paired(): other = lax.ppermute(shard, 'row', over_x)  4.61 us
    dynamic_update_slice x4, local copies, waits for them, and re-layouts, on_device_paired(): lax.dynamic_update_slice(piece, other[None, None], (place, 1 - x, 0, 0))  4.1 us
    add x1, other arithmetic, gelu_slope(): 0.5 * (1.0 + lax.erf(v / math.sqrt(2.0)))  4.09 us
  transfers between devices with their start and end apart: 21, of which 7 were waited for; matrix products, arithmetic and copies ran while one was open for 55% of the time, Pallas kernels for 0%

profile of v6, /device:TPU:0, one launch (start us, length us, event | category | flops | bytes accessed | tf_op | source)
XLA Modules:
  0.0 114.5 jit_solution(4670170607577098273)
XLA Ops:
  0.6 3.0 %collective-permute-start = (bf16[192,1024]{1,0:T(8,128)(2,1)}, bf16[192,1024]{1,0:T(8,128)(2,1)}, u32[]{:S(2)}, u32[]{:S(2)}) collective-permute-start(bf16[192,1024]{1,0:T(8,128)(2,1)} %param.4), channel_id=1, source_target_pairs={{0,4},{4,0},{8,12},{12,8},{16,20},{20,16},{24,28},{28,24},{1,5},{5... | collective-permute-start | bytes 1179656 | tf_op jit(solution)/shard_map/ppermute | solution.py:73
  3.6 1.6 %collective-permute-start.1 = (bf16[192,1024]{1,0:T(8,128)(2,1)}, bf16[192,1024]{1,0:T(8,128)(2,1)}, u32[]{:S(2)}, u32[]{:S(2)}) collective-permute-start(bf16[192,1024]{1,0:T(8,128)(2,1)} %param.4), channel_id=1, source_target_pairs={{0,8},{4,12},{8,16},{12,20},{16,24},{20,28},{24,0},{28,4},{1,9},{5... | collective-permute-start | bytes 1179656 | tf_op jit(solution)/shard_map/ppermute | solution.py:78
  5.2 1.5 %collective-permute-start.9 = (bf16[384,2048]{1,0:T(8,128)(2,1)}, bf16[384,2048]{1,0:T(8,128)(2,1)}, u32[]{:S(2)}, u32[]{:S(2)}) collective-permute-start(bf16[384,2048]{1,0:T(8,128)(2,1)} %param.6), channel_id=1, source_target_pairs={{0,2},{1,3},{2,0},{3,1},{4,6},{5,7},{6,4},{7,5},{8,10},{9,11},{10,... | collective-permute-start | bytes 4718600 | tf_op jit(solution)/shard_map/ppermute | solution.py:57
  6.7 4.1 %fusion.20 = (f32[384,2048]{1,0:T(8,128)}, bf16[384,2048]{1,0:T(8,128)(2,1)}) fusion(bf16[384,2048]{1,0:T(8,128)(2,1)} %param.6), kind=kLoop, calls=%fused_computation.27 | loop fusion | flops 9437184 | bytes 6291456 | tf_op jit(solution)/shard_map/add | solution.py:17
  11.9 0.7 abs_reduce_fusion.8
  12.5 3.8 %abs_reduce_fusion = bf16[]{:T(256)} fusion(bf16[2048,1024]{1,0:T(8,128)(2,1)} %param.5), kind=kLoop, calls=%fused_computation.14 | loop fusion | flops 4194303 | bytes 4194306 | tf_op jit(solution)/shard_map/reduce_max | solution.py:60
  16.4 1.5 %collective-permute-start.3 = (bf16[192,1024]{1,0:T(8,128)(2,1)}, bf16[192,1024]{1,0:T(8,128)(2,1)S(1)}, u32[]{:S(2)}, u32[]{:S(2)}) collective-permute-start(bf16[192,1024]{1,0:T(8,128)(2,1)} %collective-permute-done.1), channel_id=1, source_target_pairs={{0,8},{4,12},{8,16},{12,20},{16,24},{20,28},{24,0},{28,4},{1,9},{5... | collective-permute-start | bytes 1179656 | tf_op jit(solution)/shard_map/ppermute | solution.py:78
  18.5 1.0 bitcast_dynamic-update-slice_fusion.6
  19.5 1.7 %abs_reduce_fusion.7 = bf16[]{:T(256)} fusion(bf16[192,1024]{1,0:T(8,128)(2,1)} %collective-permute-done), kind=kLoop, calls=%fused_computation.79 | loop fusion | flops 393215 | bytes 393218 | tf_op jit(solution)/shard_map/reduce_max | solution.py:60
  22.6 1.7 %abs_reduce_fusion.6 = bf16[]{:T(256)} fusion(bf16[192,1024]{1,0:T(8,128)(2,1)} %collective-permute-done.1), kind=kLoop, calls=%fused_computation.78 | loop fusion | flops 393215 | bytes 393218 | tf_op jit(solution)/shard_map/reduce_max | solution.py:60
  24.2 1.0 bitcast_dynamic-update-slice_fusion.5
  25.3 4.0 %collective-permute-done.3 = bf16[192,1024]{1,0:T(8,128)(2,1)S(1)} collective-permute-done((bf16[192,1024]{1,0:T(8,128)(2,1)}, bf16[192,1024]{1,0:T(8,128)(2,1)S(1)}, u32[]{:S(2)}, u32[]{:S(2)}) %collective-permute-start.3) | collective-permute-done | bytes 393248 | tf_op jit(solution)/shard_map/ppermute | solution.py:78
  29.8 1.0 bitcast_dynamic-update-slice_fusion.4
  30.9 1.7 %abs_reduce_fusion.5 = bf16[]{:T(256)} fusion(bf16[192,1024]{1,0:T(8,128)(2,1)} %collective-permute-done.2), kind=kLoop, calls=%fused_computation.77 | loop fusion | flops 393215 | bytes 393218 | tf_op jit(solution)/shard_map/reduce_max | solution.py:60
  33.9 0.7 abs_reduce_fusion.4
  34.6 6.7 %collective-permute-done.5 = bf16[192,1024]{1,0:T(8,128)(2,1)} collective-permute-done((bf16[192,1024]{1,0:T(8,128)(2,1)S(1)}, bf16[192,1024]{1,0:T(8,128)(2,1)}, u32[]{:S(2)}, u32[]{:S(2)}) %collective-permute-start.5) | collective-permute-done | bytes 393248 | tf_op jit(solution)/shard_map/ppermute | solution.py:78
  41.8 1.0 bitcast_dynamic-update-slice_fusion.2
  42.8 1.7 %abs_reduce_fusion.3 = bf16[]{:T(256)} fusion(bf16[192,1024]{1,0:T(8,128)(2,1)} %collective-permute-done.4), kind=kLoop, calls=%fused_computation.75 | loop fusion | flops 393215 | bytes 393218 | tf_op jit(solution)/shard_map/reduce_max | solution.py:60
  45.8 1.7 %abs_reduce_fusion.2 = bf16[]{:T(256)} fusion(bf16[192,1024]{1,0:T(8,128)(2,1)} %collective-permute-done.5), kind=kLoop, calls=%fused_computation.74 | loop fusion | flops 393215 | bytes 393218 | tf_op jit(solution)/shard_map/reduce_max | solution.py:60
  47.5 1.0 bitcast_dynamic-update-slice_fusion.1
  48.5 2.1 %collective-permute-done.6 = bf16[192,1024]{1,0:T(8,128)(2,1)} collective-permute-done((bf16[192,1024]{1,0:T(8,128)(2,1)}, bf16[192,1024]{1,0:T(8,128)(2,1)}, u32[]{:S(2)}, u32[]{:S(2)}) %collective-permute-start.6) | collective-permute-done | bytes 393248 | tf_op jit(solution)/shard_map/ppermute | solution.py:73
  50.6 1.0 bitcast_dynamic-update-slice_fusion
  51.7 1.4 %fusion.45 = (bf16[1,2,192,1024]{3,2,1,0:T(8,128)(2,1)}, bf16[1,2,192,1024]{3,2,1,0:T(8,128)(2,1)}, bf16[1,2,192,1024]{3,2,1,0:T(8,128)(2,1)S(1)}, bf16[1,2,192,1024]{3,2,1,0:T(8,128)(2,1)}) fusion(bf16[4,2,192,1024]{3,2,1,0:T(8,128)(2,1)S(1)} %bitcast_dynamic-update-slice_fusion), kind=kLoop, calls=%fused_computation.83 | loop fusion | bytes 6291456 | tf_op jit(solution)/shard_map/slice | solution.py:89
  53.1 1.6 %copy-done.1 = bf16[2048,1024]{1,0:T(8,128)(2,1)S(1)} copy-done((bf16[2048,1024]{1,0:T(8,128)(2,1)S(1)}, bf16[2048,1024]{1,0:T(8,128)(2,1)}, u32[]{:S(2)}) %copy-start.1) | copy-done | bytes 4194328
  54.7 1.6 %fusion.35 = f32[384,512]{1,0:T(8,128)} fusion(bf16[384,1024]{1,0:T(8,128)(2,1)S(1)} %bitcast.44, bf16[2048,1024]{1,0:T(8,128)(2,1)S(1)} %copy-done.1), kind=kOutput, calls=%fused_computation.49 | convolution fusion | flops 402653184 | bytes 2621440 | tf_op jit(solution)/shard_map/dot_general | solution.py:41
  56.3 1.6 %fusion.29 = f32[384,512]{1,0:T(8,128)} fusion(bf16[384,1024]{1,0:T(8,128)(2,1)S(1)} %bitcast.45, bf16[2048,1024]{1,0:T(8,128)(2,1)S(1)} %copy-done.1), kind=kOutput, calls=%fused_computation.43 | convolution fusion | flops 402653184 | bytes 2621440 | tf_op jit(solution)/shard_map/dot_general | solution.py:41
  57.8 1.5 %fusion.32 = f32[384,512]{1,0:T(8,128)} fusion(bf16[384,1024]{1,0:T(8,128)(2,1)S(1)} %bitcast.46, bf16[2048,1024]{1,0:T(8,128)(2,1)S(1)} %copy-done.1), kind=kOutput, calls=%fused_computation.46 | convolution fusion | flops 402653184 | bytes 2621440 | tf_op jit(solution)/shard_map/dot_general | solution.py:41
  59.3 1.6 %fusion.38 = f32[384,512]{1,0:T(8,128)} fusion(bf16[384,1024]{1,0:T(8,128)(2,1)S(1)} %bitcast.47, bf16[2048,1024]{1,0:T(8,128)(2,1)S(1)} %copy-done.1), kind=kOutput, calls=%fused_computation.52 | convolution fusion | flops 402653184 | bytes 2621440 | tf_op jit(solution)/shard_map/dot_general | solution.py:41
  60.9 1.7 %abs_reduce_fusion.1 = bf16[]{:T(256)} fusion(bf16[192,1024]{1,0:T(8,128)(2,1)} %collective-permute-done.6), kind=kLoop, calls=%fused_computation.73 | loop fusion | flops 393215 | bytes 393218 | tf_op jit(solution)/shard_map/reduce_max | solution.py:60
  64.6 0.6 collective-permute-start.8
  65.7 2.7 %fusion.11 = bf16[384,2048]{1,0:T(8,128)(2,1)} fusion(bf16[384,2048]{1,0:T(8,128)(2,1)} %collective-permute-done.9), kind=kLoop, calls=%fused_computation.18 | loop fusion | flops 4718592 | bytes 3145728 | tf_op jit(solution)/shard_map/convert_element_type | solution.py:100
  68.6 0.6 slice.75
  70.0 2.1 %fusion.27 = f16[384,512]{1,0:T(8,128)(2,1)S(1)} fusion(f32[384,512]{1,0:T(8,128)} %collective-permute-done.10, bf16[384,1024]{1,0:T(8,128)(2,1)S(1)} %bitcast.41, bf16[2048,1024]{1,0:T(8,128)(2,1)} %param.5, f32[]{:T(128)} %bitcast.10), kind=kOutput, calls=%fused_computation.41 | convolution fusion | flops 403243008 | bytes 3015168 | tf_op jit(solution)/shard_map/dot_general | solution.py:41
  72.1 1.5 %collective-permute-done.17 = f32[8,128]{1,0:T(8,128)S(1)} collective-permute-done((f32[8,128]{1,0:T(8,128)S(1)}, f32[8,128]{1,0:T(8,128)S(1)}, u32[]{:S(2)}, u32[]{:S(2)}) %collective-permute-start.17) | collective-permute-done | bytes 4128 | tf_op jit(solution)/shard_map/ppermute | solution.py:84
  76.1 0.7 collective-permute-start.18
  76.7 2.6 %fusion.26 = f16[384,512]{1,0:T(8,128)(2,1)S(1)} fusion(f32[384,512]{1,0:T(8,128)} %collective-permute-done.15, bf16[384,1024]{1,0:T(8,128)(2,1)} %bitcast.40, bf16[2048,1024]{1,0:T(8,128)(2,1)} %param.5, f32[]{:T(128)} %bitcast.10), kind=kOutput, calls=%fused_computation.40 | convolution fusion | flops 403243008 | bytes 3015168 | tf_op jit(solution)/shard_map/dot_general | solution.py:41
  79.4 1.1 collective-permute-start.16
  80.5 2.1 %fusion.25 = f16[384,512]{1,0:T(8,128)(2,1)S(1)} fusion(f32[384,512]{1,0:T(8,128)} %collective-permute-done.19, bf16[384,1024]{1,0:T(8,128)(2,1)S(1)} %bitcast.42, bf16[2048,1024]{1,0:T(8,128)(2,1)} %param.5, f32[]{:T(128)} %bitcast.10), kind=kOutput, calls=%fused_computation.39 | convolution fusion | flops 403243008 | bytes 3015168 | tf_op jit(solution)/shard_map/dot_general | solution.py:41
  82.6 1.0 collective-permute-start.20
  83.7 1.7 %fusion.28 = f16[384,512]{1,0:T(8,128)(2,1)S(1)} fusion(f32[384,512]{1,0:T(8,128)} %collective-permute-done.7, bf16[384,1024]{1,0:T(8,128)(2,1)S(1)} %bitcast.43, bf16[2048,1024]{1,0:T(8,128)(2,1)S(1)} %copy-done.2, f32[]{:T(128)} %bitcast.10), kind=kOutput, calls=%fused_computation.42 | convolution fusion | flops 403243008 | bytes 3014660 | tf_op jit(solution)/shard_map/dot_general | solution.py:41
  85.4 1.8 %multiply_convert_fusion = f16[384,2048]{1,0:T(8,128)(2,1)S(1)} fusion(bf16[384,1024]{1,0:T(8,128)(2,1)S(1)} %bitcast.39, bf16[2048,1024]{1,0:T(8,128)(2,1)S(1)} %copy-done.2, f32[]{:T(128)S(6)} %div.97), kind=kOutput, calls=%fused_computation.29 | convolution fusion | flops 1612185600 | bytes 6553604 | tf_op jit(solution)/shard_map/dot_general | solution.py:41
  87.4 12.2 %multiply_add_fusion = f32[2048,1024]{1,0:T(8,128)} fusion(f32[2048,1024]{1,0:T(8,128)} %param.7, bf16[1536,1024]{1,0:T(8,128)(2,1)S(1)} %bitcast.37, bf16[384,2048]{1,0:T(8,128)(2,1)} %get-tuple-element.32, bf16[384,2048]{1,0:T(8,128)(2,1)} %collective-permute-done.12, bf16[384,2048]{1,0:T(8,128)(2,1)} %fusion.11, bf16[384,2048]{1,0:T(8,128)(2,1)} %collective-permute-done.11), kind=kOutput, calls=%fused_computation | convolution fusion | flops 6471811072 | bytes 26214400 | tf_op jit(solution)/shard_map/dot_general | solution.py:109
  99.6 1.1 collective-permute-start.14
  100.7 1.8 %multiply_add_fusion.1 = f32[384,2048]{1,0:T(8,128)S(1)} fusion(f16[384,2048]{1,0:T(8,128)(2,1)S(1)} %collective-permute-done.13, bf16[384,1024]{1,0:T(8,128)(2,1)S(1)} %bitcast.38, bf16[2048,1024]{1,0:T(8,128)(2,1)S(1)} %copy-done.2, f32[]{:T(128)} %bitcast.14), kind=kOutput, calls=%fused_computation.28 | convolution fusion | flops 1612972032 | bytes 9699332 | tf_op jit(solution)/shard_map/dot_general | solution.py:41
  102.6 2.3 %collective-permute-done.20 = f16[384,512]{1,0:T(8,128)(2,1)S(1)} collective-permute-done((f16[384,512]{1,0:T(8,128)(2,1)S(1)}, f16[384,512]{1,0:T(8,128)(2,1)S(1)}, u32[]{:S(2)}, u32[]{:S(2)}) %collective-permute-start.20) | collective-permute-done | bytes 393248 | tf_op jit(solution)/shard_map/ppermute | solution.py:98
  104.9 1.0 fusion.41
  105.9 7.0 %collective-permute-done.14 = f16[384,512]{1,0:T(8,128)(2,1)S(1)} collective-permute-done((f16[384,512]{1,0:T(8,128)(2,1)S(1)}, f16[384,512]{1,0:T(8,128)(2,1)S(1)}, u32[]{:S(2)}, u32[]{:S(2)}) %collective-permute-start.14) | collective-permute-done | bytes 393248 | tf_op jit(solution)/shard_map/ppermute | solution.py:115
  113.1 1.4 %pad_maximum_fusion = bf16[384,2048]{1,0:T(8,128)(2,1)} fusion(bf16[384,512]{1,0:T(8,128)(2,1)S(1)} %multiply_convert_fusion.1, bf16[384,512]{1,0:T(8,128)(2,1)S(1)} %get-tuple-element.18, bf16[384,512]{1,0:T(8,128)(2,1)S(1)} %get-tuple-element.17, bf16[384,512]{1,0:T(8,128)(2,1)S(1)} %get-tuple-element.16), kind=kLoop, calls=%fused_computation.30 | loop fusion | flops 6291456 | bytes 3145728 | tf_op jit(solution)/shard_map/concatenate | solution.py:126
  (50 shorter events, 4.9 us)
Async XLA Ops:
  0.6 17.8 %collective-permute-start = (bf16[192,1024]{1,0:T(8,128)(2,1)}, bf16[192,1024]{1,0:T(8,128)(2,1)}, u32[]{:S(2)}, u32[]{:S(2)}) collective-permute-start(bf16[192,1024]{1,0:T(8,128)(2,1)} %param.4), channel_id=1, source_target_pairs={{0,4},{4,0},{8,12},{12,8},{16,20},{20,16},{24,28},{28,24},{1,5},{5... | collective-permute-start | bytes 1179656 | tf_op jit(solution)/shard_map/ppermute | solution.py:73
  3.6 12.8 %collective-permute-start.1 = (bf16[192,1024]{1,0:T(8,128)(2,1)}, bf16[192,1024]{1,0:T(8,128)(2,1)}, u32[]{:S(2)}, u32[]{:S(2)}) collective-permute-start(bf16[192,1024]{1,0:T(8,128)(2,1)} %param.4), channel_id=1, source_target_pairs={{0,8},{4,12},{8,16},{12,20},{16,24},{20,28},{24,0},{28,4},{1,9},{5... | collective-permute-start | bytes 1179656 | tf_op jit(solution)/shard_map/ppermute | solution.py:78
  5.2 60.0 %collective-permute-start.9 = (bf16[384,2048]{1,0:T(8,128)(2,1)}, bf16[384,2048]{1,0:T(8,128)(2,1)}, u32[]{:S(2)}, u32[]{:S(2)}) collective-permute-start(bf16[384,2048]{1,0:T(8,128)(2,1)} %param.6), channel_id=1, source_target_pairs={{0,2},{1,3},{2,0},{3,1},{4,6},{5,7},{6,4},{7,5},{8,10},{9,11},{10,... | collective-permute-start | bytes 4718600 | tf_op jit(solution)/shard_map/ppermute | solution.py:57
  10.8 1.0 copy-start.3
  10.8 76.5 %collective-permute-start.12 = (bf16[384,2048]{1,0:T(8,128)(2,1)}, bf16[384,2048]{1,0:T(8,128)(2,1)}, u32[]{:S(2)}, u32[]{:S(2)}) collective-permute-start(bf16[384,2048]{1,0:T(8,128)(2,1)} %get-tuple-element.32), channel_id=1, source_target_pairs={{0,1},{1,0},{2,3},{3,2},{4,5},{5,4},{6,7},{7,6},{8,9},{9,8},{10,11... | collective-permute-start | bytes 4718600 | tf_op jit(solution)/shard_map/ppermute | solution.py:66
  16.4 12.9 %collective-permute-start.3 = (bf16[192,1024]{1,0:T(8,128)(2,1)}, bf16[192,1024]{1,0:T(8,128)(2,1)S(1)}, u32[]{:S(2)}, u32[]{:S(2)}) collective-permute-start(bf16[192,1024]{1,0:T(8,128)(2,1)} %collective-permute-done.1), channel_id=1, source_target_pairs={{0,8},{4,12},{8,16},{12,20},{16,24},{20,28},{24,0},{28,4},{1,9},{5... | collective-permute-start | bytes 1179656 | tf_op jit(solution)/shard_map/ppermute | solution.py:78
  17.9 11.9 %collective-permute-start.2 = (bf16[192,1024]{1,0:T(8,128)(2,1)}, bf16[192,1024]{1,0:T(8,128)(2,1)}, u32[]{:S(2)}, u32[]{:S(2)}) collective-permute-start(bf16[192,1024]{1,0:T(8,128)(2,1)} %collective-permute-done.1), channel_id=1, source_target_pairs={{0,4},{4,0},{8,12},{12,8},{16,20},{20,16},{24,28},{28,24},{1,5},{5... | collective-permute-start | bytes 1179656 | tf_op jit(solution)/shard_map/ppermute | solution.py:73
  29.3 11.9 %collective-permute-start.5 = (bf16[192,1024]{1,0:T(8,128)(2,1)S(1)}, bf16[192,1024]{1,0:T(8,128)(2,1)}, u32[]{:S(2)}, u32[]{:S(2)}) collective-permute-start(bf16[192,1024]{1,0:T(8,128)(2,1)S(1)} %collective-permute-done.3), channel_id=1, source_target_pairs={{0,8},{4,12},{8,16},{12,20},{16,24},{20,28},{24,0},{28,4},{1,9},{5... | collective-permute-start | bytes 1179656 | tf_op jit(solution)/shard_map/ppermute | solution.py:78
  29.3 12.4 %collective-permute-start.4 = (bf16[192,1024]{1,0:T(8,128)(2,1)S(1)}, bf16[192,1024]{1,0:T(8,128)(2,1)}, u32[]{:S(2)}, u32[]{:S(2)}) collective-permute-start(bf16[192,1024]{1,0:T(8,128)(2,1)S(1)} %collective-permute-done.3), channel_id=1, source_target_pairs={{0,4},{4,0},{8,12},{12,8},{16,20},{20,16},{24,28},{28,24},{1,5},{5... | collective-permute-start | bytes 1179656 | tf_op jit(solution)/shard_map/ppermute | solution.py:73
  41.2 9.4 %collective-permute-start.6 = (bf16[192,1024]{1,0:T(8,128)(2,1)}, bf16[192,1024]{1,0:T(8,128)(2,1)}, u32[]{:S(2)}, u32[]{:S(2)}) collective-permute-start(bf16[192,1024]{1,0:T(8,128)(2,1)} %collective-permute-done.5), channel_id=1, source_target_pairs={{0,4},{4,0},{8,12},{12,8},{16,20},{20,16},{24,28},{28,24},{1,5},{5... | collective-permute-start | bytes 1179656 | tf_op jit(solution)/shard_map/ppermute | solution.py:73
  51.7 3.0 %copy-start.1 = (bf16[2048,1024]{1,0:T(8,128)(2,1)S(1)}, bf16[2048,1024]{1,0:T(8,128)(2,1)}, u32[]{:S(2)}) copy-start(bf16[2048,1024]{1,0:T(8,128)(2,1)} %param.5) | copy-start | bytes 12582916
  56.3 13.7 %collective-permute-start.10 = (f32[384,512]{1,0:T(8,128)}, f32[384,512]{1,0:T(8,128)}, u32[]{:S(2)}, u32[]{:S(2)}) collective-permute-start(f32[384,512]{1,0:T(8,128)} %fusion.35), channel_id=1, source_target_pairs={{0,1},{1,0},{2,3},{3,2},{4,5},{5,4},{6,7},{7,6},{8,9},{9,8},{10,11... | collective-permute-start | bytes 2359304 | tf_op jit(solution)/shard_map/ppermute | solution.py:95
  64.6 5.4 %copy-start.6 = (bf16[1,2,192,1024]{3,2,1,0:T(8,128)(2,1)S(1)}, bf16[1,2,192,1024]{3,2,1,0:T(8,128)(2,1)}, u32[]{:S(2)}) copy-start(bf16[1,2,192,1024]{3,2,1,0:T(8,128)(2,1)} %get-tuple-element.30) | copy-start | bytes 2359300
  64.6 3.8 %collective-permute-start.8 = (f32[8,128]{1,0:T(8,128)S(1)}, f32[8,128]{1,0:T(8,128)S(1)}, u32[]{:S(2)}, u32[]{:S(2)}) collective-permute-start(f32[8,128]{1,0:T(8,128)S(1)} %broadcast_in_dim.39), channel_id=1, source_target_pairs={{0,1},{1,0},{2,3},{3,2},{4,5},{5,4},{6,7},{7,6},{8,9},{9,8},{10,11... | collective-permute-start | bytes 12296 | tf_op jit(solution)/shard_map/ppermute | solution.py:82
  65.2 17.5 %collective-permute-start.7 = (f32[384,512]{1,0:T(8,128)}, f32[384,512]{1,0:T(8,128)}, u32[]{:S(2)}, u32[]{:S(2)}) collective-permute-start(f32[384,512]{1,0:T(8,128)} %fusion.38), channel_id=1, source_target_pairs={{0,1},{1,0},{2,3},{3,2},{4,5},{5,4},{6,7},{7,6},{8,9},{9,8},{10,11... | collective-permute-start | bytes 2359304 | tf_op jit(solution)/shard_map/ppermute | solution.py:95
  65.3 10.8 %collective-permute-start.15 = (f32[384,512]{1,0:T(8,128)}, f32[384,512]{1,0:T(8,128)}, u32[]{:S(2)}, u32[]{:S(2)}) collective-permute-start(f32[384,512]{1,0:T(8,128)} %fusion.32), channel_id=1, source_target_pairs={{0,1},{1,0},{2,3},{3,2},{4,5},{5,4},{6,7},{7,6},{8,9},{9,8},{10,11... | collective-permute-start | bytes 2359304 | tf_op jit(solution)/shard_map/ppermute | solution.py:95
  68.4 11.0 %collective-permute-start.19 = (f32[384,512]{1,0:T(8,128)}, f32[384,512]{1,0:T(8,128)}, u32[]{:S(2)}, u32[]{:S(2)}) collective-permute-start(f32[384,512]{1,0:T(8,128)} %fusion.29), channel_id=1, source_target_pairs={{0,1},{1,0},{2,3},{3,2},{4,5},{5,4},{6,7},{7,6},{8,9},{9,8},{10,11... | collective-permute-start | bytes 2359304 | tf_op jit(solution)/shard_map/ppermute | solution.py:95
  69.9 3.7 %collective-permute-start.17 = (f32[8,128]{1,0:T(8,128)S(1)}, f32[8,128]{1,0:T(8,128)S(1)}, u32[]{:S(2)}, u32[]{:S(2)}) collective-permute-start(f32[8,128]{1,0:T(8,128)S(1)} %broadcast_add_fusion), channel_id=1, source_target_pairs={{0,2},{1,3},{2,0},{3,1},{4,6},{5,7},{6,4},{7,5},{8,10},{9,11},{10,... | collective-permute-start | bytes 12296 | tf_op jit(solution)/shard_map/ppermute | solution.py:84
  73.6 13.8 %collective-permute-start.11 = (bf16[384,2048]{1,0:T(8,128)(2,1)}, bf16[384,2048]{1,0:T(8,128)(2,1)}, u32[]{:S(2)}, u32[]{:S(2)}) collective-permute-start(bf16[384,2048]{1,0:T(8,128)(2,1)} %fusion.11), channel_id=1, source_target_pairs={{0,1},{1,0},{2,3},{3,2},{4,5},{5,4},{6,7},{7,6},{8,9},{9,8},{10,11... | collective-permute-start | bytes 4718600 | tf_op jit(solution)/shard_map/ppermute | solution.py:102
  73.7 6.9 %copy-start.7 = (bf16[1,2,192,1024]{3,2,1,0:T(8,128)(2,1)S(1)}, bf16[1,2,192,1024]{3,2,1,0:T(8,128)(2,1)}, u32[]{:S(2)}) copy-start(bf16[1,2,192,1024]{3,2,1,0:T(8,128)(2,1)} %get-tuple-element.30) | copy-start | bytes 2359300
  76.0 7.6 %copy-start.2 = (bf16[2048,1024]{1,0:T(8,128)(2,1)S(1)}, bf16[2048,1024]{1,0:T(8,128)(2,1)}, u32[]{:S(2)}) copy-start(bf16[2048,1024]{1,0:T(8,128)(2,1)} %param.5) | copy-start | bytes 12582916
  76.1 26.5 %collective-permute-start.18 = (f16[384,512]{1,0:T(8,128)(2,1)S(1)}, f16[384,512]{1,0:T(8,128)(2,1)S(1)}, u32[]{:S(2)}, u32[]{:S(2)}) collective-permute-start(f16[384,512]{1,0:T(8,128)(2,1)S(1)} %fusion.27), channel_id=1, source_target_pairs={{0,2},{1,3},{2,0},{3,1},{4,6},{5,7},{6,4},{7,5},{8,10},{9,11},{10,... | collective-permute-start | bytes 1179656 | tf_op jit(solution)/shard_map/ppermute | solution.py:98
  79.4 6.0 %copy-start.5 = (bf16[1,2,192,1024]{3,2,1,0:T(8,128)(2,1)S(1)}, bf16[1,2,192,1024]{3,2,1,0:T(8,128)(2,1)}, u32[]{:S(2)}) copy-start(bf16[1,2,192,1024]{3,2,1,0:T(8,128)(2,1)} %get-tuple-element.28) | copy-start | bytes 2359300
  79.4 23.2 %collective-permute-start.16 = (f16[384,512]{1,0:T(8,128)(2,1)S(1)}, f16[384,512]{1,0:T(8,128)(2,1)S(1)}, u32[]{:S(2)}, u32[]{:S(2)}) collective-permute-start(f16[384,512]{1,0:T(8,128)(2,1)S(1)} %fusion.26), channel_id=1, source_target_pairs={{0,2},{1,3},{2,0},{3,1},{4,6},{5,7},{6,4},{7,5},{8,10},{9,11},{10,... | collective-permute-start | bytes 1179656 | tf_op jit(solution)/shard_map/ppermute | solution.py:98
  82.6 22.2 %collective-permute-start.20 = (f16[384,512]{1,0:T(8,128)(2,1)S(1)}, f16[384,512]{1,0:T(8,128)(2,1)S(1)}, u32[]{:S(2)}, u32[]{:S(2)}) collective-permute-start(f16[384,512]{1,0:T(8,128)(2,1)S(1)} %fusion.25), channel_id=1, source_target_pairs={{0,2},{1,3},{2,0},{3,1},{4,6},{5,7},{6,4},{7,5},{8,10},{9,11},{10,... | collective-permute-start | bytes 1179656 | tf_op jit(solution)/shard_map/ppermute | solution.py:98
  87.3 13.4 %collective-permute-start.13 = (f16[384,2048]{1,0:T(8,128)(2,1)S(1)}, f16[384,2048]{1,0:T(8,128)(2,1)S(1)}, u32[]{:S(2)}, u32[]{:S(2)}) collective-permute-start(f16[384,2048]{1,0:T(8,128)(2,1)S(1)} %multiply_convert_fusion), channel_id=1, source_target_pairs={{0,1},{1,0},{2,3},{3,2},{4,5},{5,4},{6,7},{7,6},{8,9},{9,8},{10,11... | collective-permute-start | bytes 4718600 | tf_op jit(solution)/shard_map/ppermute | solution.py:105
  87.4 13.3 %copy-start.4 = (bf16[1,2,192,1024]{3,2,1,0:T(8,128)(2,1)S(1)}, bf16[1,2,192,1024]{3,2,1,0:T(8,128)(2,1)}, u32[]{:S(2)}) copy-start(bf16[1,2,192,1024]{3,2,1,0:T(8,128)(2,1)} %get-tuple-element.27) | copy-start | bytes 2359300
  99.6 13.3 %collective-permute-start.14 = (f16[384,512]{1,0:T(8,128)(2,1)S(1)}, f16[384,512]{1,0:T(8,128)(2,1)S(1)}, u32[]{:S(2)}, u32[]{:S(2)}) collective-permute-start(f16[384,512]{1,0:T(8,128)(2,1)S(1)} %fusion.28), channel_id=1, source_target_pairs={{0,2},{1,3},{2,0},{3,1},{4,6},{5,7},{6,4},{7,5},{8,10},{9,11},{10,... | collective-permute-start | bytes 1179656 | tf_op jit(solution)/shard_map/ppermute | solution.py:115
  100.7 4.2 %copy-start = (f32[384,2048]{1,0:T(8,128)S(1)}, f32[384,2048]{1,0:T(8,128)}, u32[]{:S(2)}) copy-start(f32[384,2048]{1,0:T(8,128)} %get-tuple-element.31) | copy-start | bytes 9437188
